TPU v7x, 256 devices: a whole 4x4x8 slice. The times are simulated.
256 devices in a mesh: gx: 4 (over y), gy: 8 (over x, z_hi), gz: 8 (over z_lo, core).
Axes of the slice: x: 4, y: 4, z: 8 (z_hi: 2, z_lo: 4; z = z_hi * 4 + z_lo), core: 2. Of those that a mesh axis runs over, the one named last changes fastest.
Arguments:
- inputs: bfloat16 [1024, 8192], P('gx', 'gy'), may hold values from -1.5 to 1.5
- out_grad: bfloat16 [1024, 8192], P('gx', 'gy'), may hold values from -1.5 to 1.5
- w_gate: bfloat16 [8192, 16384], P('gy', ('gx', 'gz')), may hold values from -0.25 to 0.25
- w_up: bfloat16 [8192, 16384], P('gy', ('gx', 'gz')), may hold values from -0.25 to 0.25
- w_down: bfloat16 [16384, 8192], P(('gx', 'gz'), 'gy'), may hold values from -0.046875 to 0.046875
Outputs:
- input_grad: bfloat16 [1024, 8192], P('gx', ('gy', 'gz'))
- gate_grad: bfloat16 [8192, 16384], P('gy', ('gx', 'gz'))
- up_grad: bfloat16 [8192, 16384], P('gy', ('gx', 'gz'))
- down_grad: bfloat16 [16384, 8192], P(('gx', 'gz'), 'gy')
All inputs are finite; a program needn't handle non-finite values.
Results may differ from a plain program's by a relative error of at most 0.015.
Values may be sent and summed in bfloat16 or wider, within the bound.
No kernel may reach another device: no remote copies, remote signals or barrier semaphores. Data moves between devices by JAX's collectives and lax.ppermute only.
A program may use at most 128 MiB of HBM per device.

v0:
```python
import jax
import jax.numpy as jnp
from jax import lax
from jax.sharding import PartitionSpec as P


def contract(left, right, left_dim, right_dim):
    return lax.dot_general(
        left, right, (((left_dim,), (right_dim,)), ((), ())), preferred_element_type=jnp.float32
    )


def silu_parts(gate, up_val, grad_hidden):
    sigma = jax.nn.sigmoid(gate)
    active = gate * sigma
    hidden = (active * up_val).astype(jnp.bfloat16)
    grad_gate = (grad_hidden * up_val * sigma * (1.0 + gate * (1.0 - sigma))).astype(jnp.bfloat16)
    grad_up = (grad_hidden * active).astype(jnp.bfloat16)
    return (hidden, grad_gate, grad_up)


def local(inputs, out_grad, w_gate, w_up, w_down):
    gate_cols, up_cols = (
        lax.all_gather(w_gate, "gx", axis=1, tiled=True),
        lax.all_gather(w_up, "gx", axis=1, tiled=True),
    )
    down_rows = lax.all_gather(w_down, "gx", axis=0, tiled=True)
    gate_part = contract(inputs, gate_cols, 1, 0)
    up_part = contract(inputs, up_cols, 1, 0)
    hidden_part = contract(out_grad, down_rows, 1, 1)
    gate, up_val, grad_hidden = lax.psum((gate_part, up_part, hidden_part), "gy")
    hidden, grad_gate, grad_up = silu_parts(gate, up_val, grad_hidden)
    gate_term = contract(inputs, grad_gate, 0, 0)
    up_term = contract(inputs, grad_up, 0, 0)
    gate_grad, up_grad = (
        lax.psum_scatter(gate_term, "gx", scatter_dimension=1, tiled=True),
        lax.psum_scatter(up_term, "gx", scatter_dimension=1, tiled=True),
    )
    down_grad = lax.psum_scatter(
        contract(hidden, out_grad, 0, 0).astype(jnp.bfloat16), "gx", scatter_dimension=0, tiled=True
    )
    input_term = contract(grad_gate, gate_cols, 1, 1) + contract(grad_up, up_cols, 1, 1)
    input_grad = lax.psum_scatter(input_term, "gz", scatter_dimension=1, tiled=True)
    return (
        input_grad.astype(jnp.bfloat16),
        gate_grad.astype(jnp.bfloat16),
        up_grad.astype(jnp.bfloat16),
        down_grad,
    )


def solution(mesh):
    placed = (
        P("gx", "gy"),
        P("gx", "gy"),
        P("gy", ("gx", "gz")),
        P("gy", ("gx", "gz")),
        P(("gx", "gz"), "gy"),
    )
    return jax.shard_map(
        local,
        mesh=mesh,
        in_specs=placed,
        out_specs=(
            P("gx", ("gy", "gz")),
            P("gy", ("gx", "gz")),
            P("gy", ("gx", "gz")),
            P(("gx", "gz"), "gy"),
        ),
        check_vma=False,
    )
```

profile of v0, /device:TPU:8, one launch (start us, length us, event | category | flops | bytes accessed | tf_op | source)
XLA Modules:
  0.0 958.1 jit_solution(14097060219427319256)
XLA Ops:
  7.2 0.0 copy-start
  7.2 0.0 all-gather.6.cloned.1.call-start
  7.2 0.7 all-gather.6.cloned.1.call-update
  7.9 0.0 all-gather.8.cloned.1.call-start
  8.0 0.7 all-gather.8.cloned.1.call-update
  8.7 0.0 all-gather.4.cloned.1.call-start
  8.7 0.7 all-gather.4.cloned.1.call-update
  9.4 0.0 all-reduce.3.cloned.1.call-start
  9.4 53.5 %all-gather.6.cloned.1.call-done = bf16[1024,2048]{1,0:T(8,128)(2,1)} async-done(((bf16[1024,512]{1,0:T(8,128)(2,1)}), bf16[1024,2048]{1,0:T(8,128)(2,1)}) %all-gather.6.cloned.1.call-update) | async-done | bytes 4194320 | tf_op jit(solution)/shard_map/all_gather | solution.py:25
  62.9 0.0 copy-done
  62.9 4.7 fusion.4
  67.7 0.0 copy-start.4
  67.7 48.3 %all-gather.8.cloned.1.call-done = bf16[1024,2048]{1,0:T(8,128)(2,1)} async-done(((bf16[1024,512]{1,0:T(8,128)(2,1)}), bf16[1024,2048]{1,0:T(8,128)(2,1)}) %all-gather.8.cloned.1.call-update) | async-done | bytes 4194320 | tf_op jit(solution)/shard_map/all_gather | solution.py:24
  116.0 4.8 fusion.5
  120.7 48.3 %all-gather.4.cloned.1.call-done = bf16[2048,1024]{1,0:T(8,128)(2,1)} async-done(((bf16[512,1024]{1,0:T(8,128)(2,1)}), bf16[2048,1024]{1,0:T(8,128)(2,1)}) %all-gather.4.cloned.1.call-update) | async-done | bytes 4194320 | tf_op jit(solution)/shard_map/all_gather | solution.py:27
  169.0 0.0 copy-done.4
  169.0 4.8 fusion.3
  173.8 0.0 all-reduce.3.cloned.1.call-update
  173.8 0.0 reduce-scatter.5.cloned.1.call-start
  173.9 513.8 %all-reduce.3.cloned.1.call-done = (f32[256,2048]{1,0:T(8,128)}, f32[256,2048]{1,0:T(8,128)}, f32[256,2048]{1,0:T(8,128)}) async-done(((f32[256,2048]{1,0:T(8,128)}, f32[256,2048]{1,0:T(8,128)}, f32[256,2048]{1,0:T(8,128)}), (f32[256,2048]{1,0:T(8,128)}, f32[256,2048]{1,0:T(8,128)}, f32[256,2048]{1,0:T(8,128)})) %all-reduce.3.cloned.1.call-update) | async-done | bytes 6291472 | tf_op jit(solution)/shard_map/psum | solution.py:31
  687.7 0.0 copy-start.3
  687.7 4.3 multiply_convert_fusion.1
  692.0 0.0 copy-done.3
  692.0 0.0 copy-start.2
  692.0 1.3 fusion.6
  693.3 0.9 copy-done.2
  694.2 2.3 convolution_add_fusion
  696.5 0.0 reduce-scatter.5.cloned.1.call-update
  696.5 0.0 reduce-scatter.9.cloned.1.call-start
  696.6 4.5 convolution_bitcast_fusion
  701.1 0.0 reduce-scatter.9.cloned.1.call-update
  701.1 0.0 reduce-scatter.7.cloned.1.call-start
  701.2 4.5 convolution_bitcast_fusion.1
  705.7 0.0 copy-start.1
  705.7 0.0 reduce-scatter.7.cloned.1.call-update
  705.7 0.0 reduce-scatter.11.cloned.1.call-start
  705.8 1.5 copy-done.1
  707.3 4.9 convolution_convert_fusion
  712.2 0.0 reduce-scatter.11.cloned.1.call-update
  712.2 18.3 %reduce-scatter.5.cloned.1.call-done = f32[256,128]{1,0:T(8,128)} async-done(((f32[256,1024]{1,0:T(8,128)}), f32[256,128]{1,0:T(8,128)}) %reduce-scatter.5.cloned.1.call-update) | async-done | bytes 131088 | tf_op jit(solution)/shard_map/reduce_scatter | solution.py:43
  730.5 1.5 convert_element_type.23
  732.1 81.5 %reduce-scatter.9.cloned.1.call-done = f32[1024,512]{0,1:T(8,128)} async-done(((f32[1024,2048]{0,1:T(8,128)}), f32[1024,512]{0,1:T(8,128)}) %reduce-scatter.9.cloned.1.call-update) | async-done | bytes 2097168 | tf_op jit(solution)/shard_map/reduce_scatter | solution.py:37
  813.5 1.7 convert_element_type.25
  815.3 1.3 copy.10
  816.6 82.4 %reduce-scatter.7.cloned.1.call-done = f32[1024,512]{0,1:T(8,128)} async-done(((f32[1024,2048]{0,1:T(8,128)}), f32[1024,512]{0,1:T(8,128)}) %reduce-scatter.7.cloned.1.call-update) | async-done | bytes 2097168 | tf_op jit(solution)/shard_map/reduce_scatter | solution.py:36
  899.0 1.7 convert_element_type.24
  900.7 1.3 copy.9
  902.1 49.2 %reduce-scatter.11.cloned.1.call-done = bf16[512,1024]{1,0:T(8,128)(2,1)} async-done(((bf16[2048,1024]{1,0:T(8,128)(2,1)}), bf16[512,1024]{1,0:T(8,128)(2,1)}) %reduce-scatter.11.cloned.1.call-update) | async-done | bytes 1048592 | tf_op jit(solution)/shard_map/reduce_scatter | solution.py:39
Async XLA Ops:
  7.2 55.8 %copy-start = (bf16[256,1024]{1,0:T(8,128)(2,1)S(1)}, bf16[256,1024]{1,0:T(8,128)(2,1)}, u32[]{:S(2)}) copy-start(bf16[256,1024]{1,0:T(8,128)(2,1)} %param.5) | copy-start | bytes 1572868
  7.2 55.7 %all-gather.6.cloned.1.call-start = ((), (), s32[]{:S(2)}) async-start(), calls=%async_computation.5 | async-start | bytes 5242880 | tf_op jit(solution)/shard_map/all_gather | solution.py:25
  7.9 108.0 %all-gather.8.cloned.1.call-start = ((), (), s32[]{:S(2)}) async-start(), calls=%async_computation.6 | async-start | bytes 5242880 | tf_op jit(solution)/shard_map/all_gather | solution.py:24
  8.7 160.3 %all-gather.4.cloned.1.call-start = ((), (), s32[]{:S(2)}) async-start(), calls=%async_computation.4 | async-start | bytes 5242880 | tf_op jit(solution)/shard_map/all_gather | solution.py:27
  9.4 678.3 %all-reduce.3.cloned.1.call-start = ((), (), s32[]{:S(2)}) async-start(), calls=%async_computation.11 | async-start | bytes 12582912 | tf_op jit(solution)/shard_map/psum | solution.py:31
  67.7 101.3 %copy-start.4 = (bf16[256,1024]{1,0:T(8,128)(2,1)S(1)}, bf16[256,1024]{1,0:T(8,128)(2,1)}, u32[]{:S(2)}) copy-start(bf16[256,1024]{1,0:T(8,128)(2,1)} %param.6) | copy-start | bytes 1572868
  173.8 556.7 %reduce-scatter.5.cloned.1.call-start = ((), (), s32[]{:S(2)}) async-start(), calls=%async_computation.7 | async-start | bytes 1179648 | tf_op jit(solution)/shard_map/reduce_scatter | solution.py:43
  687.7 4.3 copy-start.3
  692.0 2.2 copy-start.2
  696.5 117.0 %reduce-scatter.9.cloned.1.call-start = ((), (), s32[]{:S(2)}) async-start(), calls=%async_computation.9 | async-start | bytes 10485760 | tf_op jit(solution)/shard_map/reduce_scatter | solution.py:37
  701.1 197.9 %reduce-scatter.7.cloned.1.call-start = ((), (), s32[]{:S(2)}) async-start(), calls=%async_computation.8 | async-start | bytes 10485760 | tf_op jit(solution)/shard_map/reduce_scatter | solution.py:36
  705.7 1.6 copy-start.1
  705.7 245.6 %reduce-scatter.11.cloned.1.call-start = ((), (), s32[]{:S(2)}) async-start(), calls=%async_computation.10 | async-start | bytes 5242880 | tf_op jit(solution)/shard_map/reduce_scatter | solution.py:39
Sparse Core Ops, SparseCore 0:
  9.8 53.0 all-gather.5
  64.7 51.1 all-gather.7
  117.8 51.1 all-gather.3
  174.0 513.6 all-reduce.2
  696.6 33.8 reduce-scatter.4
  733.0 80.5 reduce-scatter.8
  816.1 82.8 reduce-scatter.6
  902.1 49.1 reduce-scatter.10
where the time goes:
time: 961 us; the launch traced here: 958 us
  waiting for transfers between devices  897 us (93%)
  matrix products  31.9 us (3%)
  between operations  14.2 us (1%)
    psum x1, waiting for transfers between devices, local(): lax.psum((gate_part, up_part, hidden_part), 'gy')  514 us
    reduce_scatter x1, waiting for transfers between devices, local(): lax.psum_scatter(gate_term, 'gx', scatter_dimension=1, tiled=True)  82.4 us
    reduce_scatter x1, waiting for transfers between devices, local(): lax.psum_scatter(up_term, 'gx', scatter_dimension=1, tiled=True)  81.5 us
    all_gather x1, waiting for transfers between devices, local(): lax.all_gather(w_up, 'gx', axis=1, tiled=True)  53.5 us
    reduce_scatter x1, waiting for transfers between devices, local(): lax.psum_scatter(contract(hidden, out_grad, 0, 0).astype(jnp.bfloat16), '...  49.2 us
    all_gather x1, waiting for transfers between devices, local(): lax.all_gather(w_gate, 'gx', axis=1, tiled=True)  48.3 us
    all_gather x1, waiting for transfers between devices, local(): down_rows = lax.all_gather(w_down, 'gx', axis=0, tiled=True)  48.3 us
    dot_general x8, matrix products, contract(): lax.dot_general(left, right, (((left_dim,), (right_dim,)), ((), ())), pre...  31.9 us
  transfers between devices with their start and end apart: 8, of which 8 were waited for; matrix products, arithmetic and copies ran while one was open for 3% of the time, Pallas kernels for 0%

commit v1 on v0

v1 whole, which is shorter than its diff:
```python
import jax
import jax.numpy as jnp
from jax import lax
from jax.experimental import pallas as pl
from jax.experimental.pallas import tpu as pltpu
from jax.sharding import Mesh, PartitionSpec as P

BF = jnp.bfloat16
F32 = jnp.float32
ROWS = 64
SIDE = ((0, 1), (2, 3))
BACK = ((1, 2), (3, 0))
FAR = ((0, 1),)


def both(pairs):
    return [q for a, b in pairs for q in ((a, b), (b, a))]


def swap(a, axis, pairs):
    return lax.ppermute(a, axis, both(pairs))


def turn(a, shift):
    return lax.ppermute(a, "y", [(i, (i + shift) % 4) for i in range(4)])


def dot(a, b, ca, cb):
    return lax.dot_general(a, b, (((ca,), (cb,)), ((), ())), preferred_element_type=F32)


def call(body, outs, args, flops=0, scratch=(), scalars=0):
    vmem = pl.BlockSpec(memory_space=pltpu.VMEM)
    smem = pl.BlockSpec(memory_space=pltpu.SMEM)
    size = sum(a.size * a.dtype.itemsize for a in args) + sum(
        jnp.dtype(o[1]).itemsize * o[0][0] * o[0][1] for o in outs
    )
    return pl.pallas_call(
        body,
        out_shape=[jax.ShapeDtypeStruct(s, d) for s, d in outs],
        in_specs=[smem] * scalars + [vmem] * (len(args) - scalars),
        out_specs=[vmem] * len(outs),
        scratch_shapes=list(scratch),
        compiler_params=pltpu.CompilerParams(vmem_limit_bytes=40 * 1024 * 1024),
        cost_estimate=pl.CostEstimate(flops=flops, bytes_accessed=size, transcendentals=0),
    )(*args)


def order_rows(place, x, dy, first, second):
    for j in range(4):
        rows = pl.ds(pl.multiple_of(place[j] * ROWS, ROWS), ROWS)
        to = first if j < 2 else second
        at = (j % 2) * ROWS
        to[at : at + ROWS, :] = x[rows, :]
        to[2 * ROWS + at : 3 * ROWS + at, :] = dy[rows, :]


def split_rows(value, send, keep, cols, kind):
    r = ROWS
    if kind == 0:
        keep[:, cols] = value[: 2 * r]
        send[:, cols] = value[2 * r :].astype(BF)
    else:
        keep[:r, cols] = value[:r]
        keep[r:, cols] = value[2 * r : 3 * r]
        send[:r, cols] = value[r : 2 * r].astype(BF)
        send[r:, cols] = value[3 * r :].astype(BF)


def partials(kind):
    def body(first, second, wg, wu, wd, send, keep):
        n = wg.shape[1]
        h = 2 * ROWS
        x = jnp.concatenate([first[:h], second[:h]], axis=0)
        split_rows(dot(x, wg[...], 1, 0), send, keep, slice(0, n), kind)
        split_rows(dot(x, wu[...], 1, 0), send, keep, slice(n, 2 * n), kind)
        dy = jnp.concatenate([first[h:], second[h:]], axis=0)
        split_rows(dot(dy, wd[...], 1, 1), send, keep, slice(2 * n, 3 * n), kind)

    return body


def halve(got, kept, send, keep):
    r = ROWS
    keep[...] = kept[:r] + got[:r].astype(F32)
    send[...] = (kept[r:] + got[r:].astype(F32)).astype(BF)


def add_round(got, kept, keep, send):
    total = kept[...] + got[...].astype(F32)
    keep[...] = total
    send[...] = total.astype(BF)


def silu_grads(got, kept, out):
    n = out.shape[1] // 3
    total = [kept[:, i * n : (i + 1) * n] + got[:, i * n : (i + 1) * n].astype(F32) for i in range(3)]
    gate, up, grad = total
    sigma = 1.0 / (1.0 + jnp.exp(-gate))
    active = gate * sigma
    out[:, :n] = (grad * up * sigma * (1.0 + gate * (1.0 - sigma))).astype(BF)
    out[:, n : 2 * n] = (grad * active).astype(BF)
    out[:, 2 * n :] = (active * up).astype(BF)


def input_partial(place, b0, b1, b2, b3, wg, wu, mine, other, full, held):
    n = wg.shape[1]
    for j, b in enumerate((b0, b1, b2, b3)):
        full[j * ROWS : (j + 1) * ROWS, :] = b[...]
    total = dot(full[:, :n], wg[...], 1, 1) + dot(full[:, n : 2 * n], wu[...], 1, 1)
    for j in range(4):
        rows = pl.ds(pl.multiple_of(place[j] * ROWS, ROWS), ROWS)
        held[rows, :] = total[j * ROWS : (j + 1) * ROWS]
    core = place[4]
    for k in range(4):
        cols = slice(k * 128, (k + 1) * 128)
        mine[:, cols] = held[:, pl.ds(pl.multiple_of((2 * k + core) * 128, 128), 128)]
        other[:, cols] = held[:, pl.ds(pl.multiple_of((2 * k + 1 - core) * 128, 128), 128)].astype(BF)


def add_cast(mine, got, out):
    out[...] = (mine[...] + got[...].astype(F32)).astype(BF)


def sum_blocks(place, mine, got, r1, r2, r3, keep, s1, s2, s3, held):
    held[...] = (
        mine[...] + got[...].astype(F32) + r1[...].astype(F32) + r2[...].astype(F32) + r3[...].astype(F32)
    )
    for k, to in enumerate((keep, s1, s2, s3)):
        to[...] = held[:, pl.ds(pl.multiple_of(place[5 + k] * 128, 128), 128)].astype(to.dtype)


def sum_last(keep, r1, r2, r3, out):
    out[...] = (keep[...] + r1[...].astype(F32) + r2[...].astype(F32) + r3[...].astype(F32)).astype(BF)


def weight_grads(*refs):
    tokens, grads, outs = refs[:8], refs[8:12], refs[12:15]
    n = outs[0].shape[1]
    h = 2 * ROWS
    full = jnp.concatenate([g[...] for g in grads], axis=0)
    for i in range(4):
        cols = slice(i * 256, (i + 1) * 256)
        x = jnp.concatenate([t[:h, cols] for t in tokens], axis=0)
        both_grads = dot(x, full[:, : 2 * n], 0, 0)
        outs[0][cols, :] = both_grads[:, :n].astype(BF)
        outs[1][cols, :] = both_grads[:, n:].astype(BF)
    dy = jnp.concatenate([t[h:, :] for t in tokens], axis=0)
    for i in range(2):
        cols = slice(i * 256, (i + 1) * 256)
        outs[2][cols, :] = dot(full[:, 2 * n + i * 256 : 2 * n + (i + 1) * 256], dy, 0, 0).astype(BF)


def local(inputs, out_grad, w_gate, w_up, w_down):
    rows, width = inputs.shape
    n = w_gate.shape[1]
    x, core, zl = lax.axis_index("x"), lax.axis_index("core"), lax.axis_index("zl")
    side = jnp.where((x == 1) | (x == 2), 1, 0)
    back = jnp.where(x >= 2, 1, 0)
    me = 2 * (side ^ core) + back
    place = jnp.stack([me, me ^ 1, me ^ 2, me ^ 3, core, zl, zl ^ 1, zl ^ 2, zl ^ 3]).astype(jnp.int32)

    first, second = call(order_rows, [((rows, width), BF)] * 2, (place, inputs, out_grad), scalars=1)
    chunks = [(first, second)]
    for shift in (-1, 1, 2):
        near = turn(first, shift)
        chunks.append((near, swap(near, "core", FAR)))

    kinds = (0, 1, 0, 1)
    axes = (SIDE, BACK)
    wide = 3 * n
    gathered = []
    for (a, b), kind in zip(chunks, kinds):
        one, two = axes[kind], axes[1 - kind]
        send, keep = call(
            partials(kind),
            [((2 * ROWS, wide), BF), ((2 * ROWS, wide), F32)],
            (a, b, w_gate, w_up, w_down),
            flops=2 * rows * width * wide,
        )
        got = swap(send, "x", one)
        send, keep = call(halve, [((ROWS, wide), BF), ((ROWS, wide), F32)], (got, keep))
        got = swap(send, "x", two)
        keep, send = call(add_round, [((ROWS, wide), F32), ((ROWS, wide), BF)], (got, keep))
        got = swap(send, "zh", FAR)
        (own,) = call(silu_grads, [((ROWS, wide), BF)], (got, keep))
        by_one, by_two = swap(own, "x", one), swap(own, "x", two)
        last = swap(by_one, "x", two)
        blocks = (own, by_two, by_one, last) if kind == 0 else (own, by_one, by_two, last)
        gathered.append(blocks)

    fulls, sums = [], []
    for blocks in gathered:
        mine, other, full = call(
            input_partial,
            [((rows, width // 2), F32), ((rows, width // 2), BF), ((rows, wide), BF)],
            (place, *blocks, w_gate, w_up),
            flops=2 * rows * width * 2 * n,
            scratch=[pltpu.VMEM((rows, width), F32)],
            scalars=1,
        )
        fulls.append(full)
        sums.append((mine, swap(other, "core", FAR)))

    arrived = []
    for (mine, got), shift in zip(sums[1:], (1, -1, 2)):
        (part,) = call(add_cast, [((rows, width // 2), BF)], (mine, got))
        arrived.append(turn(part, shift))
    gate_grad, up_grad, down_grad = call(
        weight_grads,
        [((width, n), BF), ((width, n), BF), ((n, width), BF)],
        (*[t for c in chunks for t in c], *fulls),
        flops=2 * 4 * rows * width * wide,
    )
    keep, *sends = call(
        sum_blocks,
        [((rows, 128), F32)] + [((rows, 128), BF)] * 3,
        (place, *sums[0], *arrived),
        scratch=[pltpu.VMEM((rows, width // 2), F32)],
        scalars=1,
    )
    last = [
        lax.ppermute(s, "zl", [(i, i ^ k) for i in range(4)]) for k, s in zip((1, 2, 3), sends)
    ]
    (input_grad,) = call(sum_last, [((rows, 128), BF)], (keep, *last))
    return input_grad, gate_grad, up_grad, down_grad


def solution(mesh):
    axes = ("y", "x", "zh", "zl", "core")
    fine = Mesh(mesh.devices.reshape(4, 4, 2, 4, 2), axes)
    tokens = P("y", ("x", "zh"))
    cols = P(("x", "zh"), ("y", "zl", "core"))
    lines = P(("y", "zl", "core"), ("x", "zh"))
    return jax.shard_map(
        local,
        mesh=fine,
        in_specs=(tokens, tokens, cols, cols, lines),
        out_specs=(P("y", ("x", "zh", "zl", "core")), cols, cols, lines),
        check_vma=False,
    )
```

time: 961 us -> 163 us (0.17)
  waiting for transfers between devices: 897 us -> 67.8 us
  starting transfers between devices: 0.32 us -> 71.9 us
  matrix products: 31.9 us -> 0 us
  Pallas kernels: 0 us -> 17.3 us
  between operations: 14.2 us -> 0.92 us
    psum x1 -> x0, waiting for transfers between devices: 514 us -> none  [local(): lax.psum((gate_part, up_part, hidden_part), 'gy')]
    reduce_scatter x4 -> x0, waiting for transfers between devices: 231 us -> none  [the longest x1 82.4 us: local(): lax.psum_scatter(gate_term, 'gx', scatter_dimension=1, tiled=True)]
    all_gather x3 -> x0, waiting for transfers between devices: 150 us -> none  [the longest x1 53.5 us: local(): lax.all_gather(w_up, 'gx', axis=1, tiled=True)]
    ppermute x0 -> x40, starting transfers between devices: none -> 71.9 us  [the longest x31 54.6 us: swap(): return lax.ppermute(a, axis, both(pairs))]
    ppermute x0 -> x40, waiting for transfers between devices: none -> 67.8 us  [the longest x31 35.6 us: swap(): return lax.ppermute(a, axis, both(pairs))]
    dot_general x8 -> x0, matrix products: 31.9 us -> none  [contract(): lax.dot_general(left, right, (((left_dim,), (right_dim,)), ((), ())), pre...]
    pallas_call x0 -> x27, Pallas kernels: none -> 17.3 us  [call(): pl.pallas_call(body, out_shape=[jax.ShapeDtypeStruct(s, d) for s, d in ou...]
  transfers between devices with their start and end apart: 8 -> 40, of which waited for: 8 -> 18; matrix products, arithmetic and copies ran while one was open for 3% -> 0% of each run, Pallas kernels for 0% -> 9%
where the time goes in v1:
time: 163 us
  starting transfers between devices  71.9 us (44%)
  waiting for transfers between devices  67.8 us (42%)
  Pallas kernels  17.3 us (11%)
  local copies, waits for them, and re-layouts  4.69 us (3%)
    ppermute x31, starting transfers between devices, swap(): return lax.ppermute(a, axis, both(pairs))  54.6 us
    ppermute x31, waiting for transfers between devices, swap(): return lax.ppermute(a, axis, both(pairs))  35.6 us
    ppermute x6, waiting for transfers between devices, turn(): return lax.ppermute(a, 'y', [(i, (i + shift) % 4) for i in range(4)])  32.2 us
    pallas_call x27, Pallas kernels, call(): pl.pallas_call(body, out_shape=[jax.ShapeDtypeStruct(s, d) for s, d in ou...  17.3 us
    ppermute x6, starting transfers between devices, turn(): return lax.ppermute(a, 'y', [(i, (i + shift) % 4) for i in range(4)])  12.8 us
    unnamed x12, local copies, waits for them, and re-layouts  4.61 us
    ppermute x3, starting transfers between devices, local(): lax.ppermute(s, 'zl', [(i, i ^ k) for i in range(4)])  4.47 us
  transfers between devices with their start and end apart: 40, of which 18 were waited for; matrix products, arithmetic and copies ran while one was open for 0% of the time, Pallas kernels for 9%

profile of v1, /device:TPU:8, one launch (start us, length us, event | category | flops | bytes accessed | tf_op | source)
XLA Modules:
  0.0 162.5 jit_solution(541790116383063392)
XLA Ops:
  0.8 1.1 copy-done.4
  1.9 1.0 copy-done.5
  3.5 2.3 %collective-permute-start.7 = (bf16[256,1024]{1,0:T(8,128)(2,1)S(1)}, bf16[256,1024]{1,0:T(8,128)(2,1)S(1)}, u32[]{:S(2)}, u32[]{:S(2)}) collective-permute-start(bf16[256,1024]{1,0:T(8,128)(2,1)S(1)} %get-tuple-element.49.first.refs_0_), channel_id=1, source_target_pairs={{0,192},{64,0},{128,64},{192,128},{1,193},{65,1},{129,65},{193,129... | collective-permute-start | bytes 1572872 | tf_op jit(solution)/shard_map/ppermute | solution.py:25
  5.8 3.3 %collective-permute-start.27 = (bf16[256,1024]{1,0:T(8,128)(2,1)S(1)}, bf16[256,1024]{1,0:T(8,128)(2,1)S(1)}, u32[]{:S(2)}, u32[]{:S(2)}) collective-permute-start(bf16[256,1024]{1,0:T(8,128)(2,1)S(1)} %get-tuple-element.49.first.refs_0_), channel_id=1, source_target_pairs={{0,128},{64,192},{128,0},{192,64},{1,129},{65,193},{129,1},{193,65... | collective-permute-start | bytes 1572872 | tf_op jit(solution)/shard_map/ppermute | solution.py:25
  9.1 9.0 %collective-permute-done.7.first.refs_2_ = bf16[256,1024]{1,0:T(8,128)(2,1)S(1)} collective-permute-done((bf16[256,1024]{1,0:T(8,128)(2,1)S(1)}, bf16[256,1024]{1,0:T(8,128)(2,1)S(1)}, u32[]{:S(2)}, u32[]{:S(2)}) %collective-permute-start.7) | collective-permute-done | bytes 524320 | tf_op jit(solution)/shard_map/ppermute | solution.py:25
  18.2 2.5 %collective-permute-done.17.first.refs_4_ = bf16[256,1024]{1,0:T(8,128)(2,1)S(1)} collective-permute-done((bf16[256,1024]{1,0:T(8,128)(2,1)S(1)}, bf16[256,1024]{1,0:T(8,128)(2,1)S(1)}, u32[]{:S(2)}, u32[]{:S(2)}) %collective-permute-start.17) | collective-permute-done | bytes 524320 | tf_op jit(solution)/shard_map/ppermute | solution.py:25
  20.7 8.9 %collective-permute-done.27.first.refs_6_ = bf16[256,1024]{1,0:T(8,128)(2,1)S(1)} collective-permute-done((bf16[256,1024]{1,0:T(8,128)(2,1)S(1)}, bf16[256,1024]{1,0:T(8,128)(2,1)S(1)}, u32[]{:S(2)}, u32[]{:S(2)}) %collective-permute-start.27) | collective-permute-done | bytes 524320 | tf_op jit(solution)/shard_map/ppermute | solution.py:25
  29.5 1.2 copy-done.1
  30.8 1.2 copy-done.3
  32.0 1.0 shard_map.90
  33.0 2.8 %collective-permute-start.9 = (bf16[128,1536]{1,0:T(8,128)(2,1)S(1)}, bf16[128,1536]{1,0:T(8,128)(2,1)S(1)}, u32[]{:S(2)}, u32[]{:S(2)}) collective-permute-start(bf16[128,1536]{1,0:T(8,128)(2,1)S(1)} %get-tuple-element.59), channel_id=1, source_target_pairs={{16,32},{32,16},{48,0},{0,48},{17,33},{33,17},{49,1},{1,49},{18,34... | collective-permute-start | bytes 1179656 | tf_op jit(solution)/shard_map/ppermute | solution.py:21
  35.8 1.0 shard_map.96
  37.1 1.0 shard_map.102
  38.1 1.2 collective-permute-start.29
  39.3 1.0 shard_map.85
  41.1 5.1 %collective-permute-done.9.got = bf16[128,1536]{1,0:T(8,128)(2,1)S(1)} collective-permute-done((bf16[128,1536]{1,0:T(8,128)(2,1)S(1)}, bf16[128,1536]{1,0:T(8,128)(2,1)S(1)}, u32[]{:S(2)}, u32[]{:S(2)}) %collective-permute-start.9) | collective-permute-done | bytes 393248 | tf_op jit(solution)/shard_map/ppermute | solution.py:21
  46.6 2.2 %collective-permute-done.19.got = bf16[128,1536]{1,0:T(8,128)(2,1)S(1)} collective-permute-done((bf16[128,1536]{1,0:T(8,128)(2,1)S(1)}, bf16[128,1536]{1,0:T(8,128)(2,1)S(1)}, u32[]{:S(2)}, u32[]{:S(2)}) %collective-permute-start.19) | collective-permute-done | bytes 393248 | tf_op jit(solution)/shard_map/ppermute | solution.py:21
  49.5 5.1 %collective-permute-done.29.got = bf16[128,1536]{1,0:T(8,128)(2,1)S(1)} collective-permute-done((bf16[128,1536]{1,0:T(8,128)(2,1)S(1)}, bf16[128,1536]{1,0:T(8,128)(2,1)S(1)}, u32[]{:S(2)}, u32[]{:S(2)}) %collective-permute-start.29) | collective-permute-done | bytes 393248 | tf_op jit(solution)/shard_map/ppermute | solution.py:21
  55.0 6.4 %collective-permute-done.10.got = bf16[64,1536]{1,0:T(8,128)(2,1)S(1)} collective-permute-done((bf16[64,1536]{1,0:T(8,128)(2,1)S(1)}, bf16[64,1536]{1,0:T(8,128)(2,1)S(1)}, u32[]{:S(2)}, u32[]{:S(2)}) %collective-permute-start.10) | collective-permute-done | bytes 196640 | tf_op jit(solution)/shard_map/ppermute | solution.py:21
  61.5 7.3 %collective-permute-start.11 = (bf16[64,1536]{1,0:T(8,128)(2,1)S(1)}, bf16[64,1536]{1,0:T(8,128)(2,1)S(1)}, u32[]{:S(2)}, u32[]{:S(2)}) collective-permute-start(bf16[64,1536]{1,0:T(8,128)(2,1)S(1)} %get-tuple-element.63), channel_id=1, source_target_pairs={{0,8},{8,0},{1,9},{9,1},{2,10},{10,2},{3,11},{11,3},{4,12},{12,4},... | collective-permute-start | bytes 589832 | tf_op jit(solution)/shard_map/ppermute | solution.py:21
  69.9 6.0 %collective-permute-start.31 = (bf16[64,1536]{1,0:T(8,128)(2,1)S(1)}, bf16[64,1536]{1,0:T(8,128)(2,1)S(1)}, u32[]{:S(2)}, u32[]{:S(2)}) collective-permute-start(bf16[64,1536]{1,0:T(8,128)(2,1)S(1)} %get-tuple-element.79), channel_id=1, source_target_pairs={{0,8},{8,0},{1,9},{9,1},{2,10},{10,2},{3,11},{11,3},{4,12},{12,4},... | collective-permute-start | bytes 589832 | tf_op jit(solution)/shard_map/ppermute | solution.py:21
  76.2 6.0 %collective-permute-start.12 = (bf16[64,1536]{1,0:T(8,128)(2,1)S(1)}, bf16[64,1536]{1,0:T(8,128)(2,1)S(1)}, u32[]{:S(2)}, u32[]{:S(2)}) collective-permute-start(bf16[64,1536]{1,0:T(8,128)(2,1)S(1)} %shard_map.93.b0), channel_id=1, source_target_pairs={{16,32},{32,16},{48,0},{0,48},{17,33},{33,17},{49,1},{1,49},{18,34... | collective-permute-start | bytes 589832 | tf_op jit(solution)/shard_map/ppermute | solution.py:21
  82.2 6.8 %collective-permute-start.2 = (bf16[64,1536]{1,0:T(8,128)(2,1)S(1)}, bf16[64,1536]{1,0:T(8,128)(2,1)S(1)}, u32[]{:S(2)}, u32[]{:S(2)}) collective-permute-start(bf16[64,1536]{1,0:T(8,128)(2,1)S(1)} %get-tuple-element.55), channel_id=1, source_target_pairs={{0,8},{8,0},{1,9},{9,1},{2,10},{10,2},{3,11},{11,3},{4,12},{12,4},... | collective-permute-start | bytes 589832 | tf_op jit(solution)/shard_map/ppermute | solution.py:21
  89.2 2.0 %collective-permute-start.13 = (bf16[64,1536]{1,0:T(8,128)(2,1)S(1)}, bf16[64,1536]{1,0:T(8,128)(2,1)S(1)}, u32[]{:S(2)}, u32[]{:S(2)}) collective-permute-start(bf16[64,1536]{1,0:T(8,128)(2,1)S(1)} %shard_map.93.b0), channel_id=1, source_target_pairs={{0,16},{16,0},{32,48},{48,32},{1,17},{17,1},{33,49},{49,33},{2,18}... | collective-permute-start | bytes 589832 | tf_op jit(solution)/shard_map/ppermute | solution.py:21
  91.3 10.3 %collective-permute-start.32 = (bf16[64,1536]{1,0:T(8,128)(2,1)S(1)}, bf16[64,1536]{1,0:T(8,128)(2,1)S(1)}, u32[]{:S(2)}, u32[]{:S(2)}) collective-permute-start(bf16[64,1536]{1,0:T(8,128)(2,1)S(1)} %shard_map.105.b0), channel_id=1, source_target_pairs={{16,32},{32,16},{48,0},{0,48},{17,33},{33,17},{49,1},{1,49},{18,34... | collective-permute-start | bytes 589832 | tf_op jit(solution)/shard_map/ppermute | solution.py:21
  101.6 3.1 %collective-permute-start.22 = (bf16[64,1536]{1,0:T(8,128)(2,1)S(1)}, bf16[64,1536]{1,0:T(8,128)(2,1)S(1)}, u32[]{:S(2)}, u32[]{:S(2)}) collective-permute-start(bf16[64,1536]{1,0:T(8,128)(2,1)S(1)} %shard_map.99.b0), channel_id=1, source_target_pairs={{16,32},{32,16},{48,0},{0,48},{17,33},{33,17},{49,1},{1,49},{18,34... | collective-permute-start | bytes 589832 | tf_op jit(solution)/shard_map/ppermute | solution.py:21
  105.8 1.2 collective-permute-start.34
  107.1 1.3 collective-permute-done.14.b3
  108.4 1.4 shard_map.94
  109.8 1.0 collective-permute-done.22.b1
  110.8 2.9 %collective-permute-done.24.b3 = bf16[64,1536]{1,0:T(8,128)(2,1)S(1)} collective-permute-done((bf16[64,1536]{1,0:T(8,128)(2,1)S(1)}, bf16[64,1536]{1,0:T(8,128)(2,1)S(1)}, u32[]{:S(2)}, u32[]{:S(2)}) %collective-permute-start.24) | collective-permute-done | bytes 196640 | tf_op jit(solution)/shard_map/ppermute | solution.py:21
  113.7 1.4 shard_map.100
  115.3 1.8 %collective-permute-done.34.b3 = bf16[64,1536]{1,0:T(8,128)(2,1)S(1)} collective-permute-done((bf16[64,1536]{1,0:T(8,128)(2,1)S(1)}, bf16[64,1536]{1,0:T(8,128)(2,1)S(1)}, u32[]{:S(2)}, u32[]{:S(2)}) %collective-permute-start.34) | collective-permute-done | bytes 196640 | tf_op jit(solution)/shard_map/ppermute | solution.py:21
  117.0 1.4 shard_map.106
  118.6 2.7 %collective-permute-start.3 = (bf16[64,1536]{1,0:T(8,128)(2,1)S(1)}, bf16[64,1536]{1,0:T(8,128)(2,1)S(1)}, u32[]{:S(2)}, u32[]{:S(2)}) collective-permute-start(bf16[64,1536]{1,0:T(8,128)(2,1)S(1)} %shard_map.88.b0), channel_id=1, source_target_pairs={{16,32},{32,16},{48,0},{0,48},{17,33},{33,17},{49,1},{1,49},{18,34... | collective-permute-start | bytes 589832 | tf_op jit(solution)/shard_map/ppermute | solution.py:21
  121.9 5.7 %collective-permute-done.3.b1 = bf16[64,1536]{1,0:T(8,128)(2,1)S(1)} collective-permute-done((bf16[64,1536]{1,0:T(8,128)(2,1)S(1)}, bf16[64,1536]{1,0:T(8,128)(2,1)S(1)}, u32[]{:S(2)}, u32[]{:S(2)}) %collective-permute-start.3) | collective-permute-done | bytes 196640 | tf_op jit(solution)/shard_map/ppermute | solution.py:21
  127.6 3.7 %collective-permute-done.5.b3 = bf16[64,1536]{1,0:T(8,128)(2,1)S(1)} collective-permute-done((bf16[64,1536]{1,0:T(8,128)(2,1)S(1)}, bf16[64,1536]{1,0:T(8,128)(2,1)S(1)}, u32[]{:S(2)}, u32[]{:S(2)}) %collective-permute-start.5) | collective-permute-done | bytes 196640 | tf_op jit(solution)/shard_map/ppermute | solution.py:21
  131.3 1.4 shard_map.89
  132.9 2.0 %collective-permute-start.16 = (bf16[256,512]{1,0:T(8,128)(2,1)S(1)}, bf16[256,512]{1,0:T(8,128)(2,1)S(1)}, u32[]{:S(2)}, u32[]{:S(2)}) collective-permute-start(bf16[256,512]{1,0:T(8,128)(2,1)S(1)} %shard_map.95), channel_id=1, source_target_pairs={{0,64},{64,128},{128,192},{192,0},{1,65},{65,129},{129,193},{193,1... | collective-permute-start | bytes 786440 | tf_op jit(solution)/shard_map/ppermute | solution.py:25
  135.0 1.8 %collective-permute-start.26 = (bf16[256,512]{1,0:T(8,128)(2,1)S(1)}, bf16[256,512]{1,0:T(8,128)(2,1)S(1)}, u32[]{:S(2)}, u32[]{:S(2)}) collective-permute-start(bf16[256,512]{1,0:T(8,128)(2,1)S(1)} %shard_map.101), channel_id=1, source_target_pairs={{0,192},{64,0},{128,64},{192,128},{1,193},{65,1},{129,65},{193,129... | collective-permute-start | bytes 786440 | tf_op jit(solution)/shard_map/ppermute | solution.py:25
  136.8 3.4 %collective-permute-start.36 = (bf16[256,512]{1,0:T(8,128)(2,1)S(1)}, bf16[256,512]{1,0:T(8,128)(2,1)S(1)}, u32[]{:S(2)}, u32[]{:S(2)}) collective-permute-start(bf16[256,512]{1,0:T(8,128)(2,1)S(1)} %shard_map.107), channel_id=1, source_target_pairs={{0,128},{64,192},{128,0},{192,64},{1,129},{65,193},{129,1},{193,65... | collective-permute-start | bytes 786440 | tf_op jit(solution)/shard_map/ppermute | solution.py:25
  140.2 3.5 %collective-permute-done.16.r1 = bf16[256,512]{1,0:T(8,128)(2,1)S(1)} collective-permute-done((bf16[256,512]{1,0:T(8,128)(2,1)S(1)}, bf16[256,512]{1,0:T(8,128)(2,1)S(1)}, u32[]{:S(2)}, u32[]{:S(2)}) %collective-permute-start.16) | collective-permute-done | bytes 262176 | tf_op jit(solution)/shard_map/ppermute | solution.py:25
  143.7 1.6 collective-permute-done.26.r2
  145.3 6.8 %collective-permute-done.36.r3 = bf16[256,512]{1,0:T(8,128)(2,1)S(1)} collective-permute-done((bf16[256,512]{1,0:T(8,128)(2,1)S(1)}, bf16[256,512]{1,0:T(8,128)(2,1)S(1)}, u32[]{:S(2)}, u32[]{:S(2)}) %collective-permute-start.36) | collective-permute-done | bytes 262176 | tf_op jit(solution)/shard_map/ppermute | solution.py:25
  152.1 0.8 shard_map.108
  153.0 2.0 %collective-permute-start.38 = (bf16[256,128]{1,0:T(8,128)(2,1)S(1)}, bf16[256,128]{1,0:T(8,128)(2,1)S(1)}, u32[]{:S(2)}, u32[]{:S(2)}) collective-permute-start(bf16[256,128]{1,0:T(8,128)(2,1)S(1)} %get-tuple-element.85), channel_id=1, source_target_pairs={{0,4},{2,6},{4,0},{6,2},{1,5},{3,7},{5,1},{7,3},{8,12},{10,14},{12... | collective-permute-start | bytes 196616 | tf_op jit(solution)/shard_map/ppermute | solution.py:223
  155.0 2.4 %collective-permute-start.39 = (bf16[256,128]{1,0:T(8,128)(2,1)S(1)}, bf16[256,128]{1,0:T(8,128)(2,1)S(1)}, u32[]{:S(2)}, u32[]{:S(2)}) collective-permute-start(bf16[256,128]{1,0:T(8,128)(2,1)S(1)} %get-tuple-element.86), channel_id=1, source_target_pairs={{0,6},{2,4},{4,2},{6,0},{1,7},{3,5},{5,3},{7,1},{8,14},{10,12},{12... | collective-permute-start | bytes 196616 | tf_op jit(solution)/shard_map/ppermute | solution.py:223
  157.4 4.5 %shard_map.110 = (bf16[1024,512]{1,0:T(8,128)(2,1)}, bf16[1024,512]{1,0:T(8,128)(2,1)}, bf16[512,1024]{1,0:T(8,128)(2,1)}) custom-call(bf16[256,1024]{1,0:T(8,128)(2,1)S(1)} %get-tuple-element.49.first.refs_0_, bf16[256,1024]{1,0:T(8,128)(2,1)S(1)} %get-tuple-element.50.second.refs_1_, bf16[256,1024]{1,0:T(8,128)(2,1)S(1)} %collective-permute-done.7.first.refs_2_, ...), custom_call_target="tpu_custom_call" | custom-call | flops 3221225472 | bytes 10485760 | tf_op jit(solution)/shard_map/pallas_call | solution.py:38
  (72 shorter events, 8.1 us)
Async XLA Ops:
  0.6 28.9 %copy-start = (bf16[1024,512]{1,0:T(8,128)(2,1)S(1)}, bf16[1024,512]{1,0:T(8,128)(2,1)}, u32[]{:S(2)}) copy-start(bf16[1024,512]{1,0:T(8,128)(2,1)} %wg.15) | copy-start | bytes 3145732
  0.7 1.1 copy-start.4
  1.9 1.0 copy-start.5
  3.5 14.6 %collective-permute-start.7 = (bf16[256,1024]{1,0:T(8,128)(2,1)S(1)}, bf16[256,1024]{1,0:T(8,128)(2,1)S(1)}, u32[]{:S(2)}, u32[]{:S(2)}) collective-permute-start(bf16[256,1024]{1,0:T(8,128)(2,1)S(1)} %get-tuple-element.49.first.refs_0_), channel_id=1, source_target_pairs={{0,192},{64,0},{128,64},{192,128},{1,193},{65,1},{129,65},{193,129... | collective-permute-start | bytes 1572872 | tf_op jit(solution)/shard_map/ppermute | solution.py:25
  5.8 14.9 %collective-permute-start.17 = (bf16[256,1024]{1,0:T(8,128)(2,1)S(1)}, bf16[256,1024]{1,0:T(8,128)(2,1)S(1)}, u32[]{:S(2)}, u32[]{:S(2)}) collective-permute-start(bf16[256,1024]{1,0:T(8,128)(2,1)S(1)} %get-tuple-element.49.first.refs_0_), channel_id=1, source_target_pairs={{0,64},{64,128},{128,192},{192,0},{1,65},{65,129},{129,193},{193,1... | collective-permute-start | bytes 1572872 | tf_op jit(solution)/shard_map/ppermute | solution.py:25
  5.8 23.7 %collective-permute-start.27 = (bf16[256,1024]{1,0:T(8,128)(2,1)S(1)}, bf16[256,1024]{1,0:T(8,128)(2,1)S(1)}, u32[]{:S(2)}, u32[]{:S(2)}) collective-permute-start(bf16[256,1024]{1,0:T(8,128)(2,1)S(1)} %get-tuple-element.49.first.refs_0_), channel_id=1, source_target_pairs={{0,128},{64,192},{128,0},{192,64},{1,129},{65,193},{129,1},{193,65... | collective-permute-start | bytes 1572872 | tf_op jit(solution)/shard_map/ppermute | solution.py:25
  18.2 11.3 %collective-permute-start.8 = (bf16[256,1024]{1,0:T(8,128)(2,1)S(1)}, bf16[256,1024]{1,0:T(8,128)(2,1)S(1)}, u32[]{:S(2)}, u32[]{:S(2)}) collective-permute-start(bf16[256,1024]{1,0:T(8,128)(2,1)S(1)} %collective-permute-done.7.first.refs_2_), channel_id=1, source_target_pairs={{0,1},{1,0},{2,3},{3,2},{4,5},{5,4},{6,7},{7,6},{8,9},{9,8},{10,11... | collective-permute-start | bytes 1572872 | tf_op jit(solution)/shard_map/ppermute | solution.py:21
  20.6 15.2 %collective-permute-start.18 = (bf16[256,1024]{1,0:T(8,128)(2,1)S(1)}, bf16[256,1024]{1,0:T(8,128)(2,1)S(1)}, u32[]{:S(2)}, u32[]{:S(2)}) collective-permute-start(bf16[256,1024]{1,0:T(8,128)(2,1)S(1)} %collective-permute-done.17.first.refs_4_), channel_id=1, source_target_pairs={{0,1},{1,0},{2,3},{3,2},{4,5},{5,4},{6,7},{7,6},{8,9},{9,8},{10,11... | collective-permute-start | bytes 1572872 | tf_op jit(solution)/shard_map/ppermute | solution.py:21
  29.5 7.6 %collective-permute-start.28 = (bf16[256,1024]{1,0:T(8,128)(2,1)S(1)}, bf16[256,1024]{1,0:T(8,128)(2,1)S(1)}, u32[]{:S(2)}, u32[]{:S(2)}) collective-permute-start(bf16[256,1024]{1,0:T(8,128)(2,1)S(1)} %collective-permute-done.27.first.refs_6_), channel_id=1, source_target_pairs={{0,1},{1,0},{2,3},{3,2},{4,5},{5,4},{6,7},{7,6},{8,9},{9,8},{10,11... | collective-permute-start | bytes 1572872 | tf_op jit(solution)/shard_map/ppermute | solution.py:21
  29.5 1.2 copy-start.1
  30.8 1.2 copy-start.3
  33.0 13.2 %collective-permute-start.9 = (bf16[128,1536]{1,0:T(8,128)(2,1)S(1)}, bf16[128,1536]{1,0:T(8,128)(2,1)S(1)}, u32[]{:S(2)}, u32[]{:S(2)}) collective-permute-start(bf16[128,1536]{1,0:T(8,128)(2,1)S(1)} %get-tuple-element.59), channel_id=1, source_target_pairs={{16,32},{32,16},{48,0},{0,48},{17,33},{33,17},{49,1},{1,49},{18,34... | collective-permute-start | bytes 1179656 | tf_op jit(solution)/shard_map/ppermute | solution.py:21
  36.8 2.5 %copy-start.2 = (bf16[1024,512]{1,0:T(8,128)(2,1)S(1)}, bf16[1024,512]{1,0:T(8,128)(2,1)}, u32[]{:S(2)}) copy-start(bf16[1024,512]{1,0:T(8,128)(2,1)} %wu.15) | copy-start | bytes 3145732
  36.8 12.0 %collective-permute-start.19 = (bf16[128,1536]{1,0:T(8,128)(2,1)S(1)}, bf16[128,1536]{1,0:T(8,128)(2,1)S(1)}, u32[]{:S(2)}, u32[]{:S(2)}) collective-permute-start(bf16[128,1536]{1,0:T(8,128)(2,1)S(1)} %get-tuple-element.67), channel_id=1, source_target_pairs={{0,16},{16,0},{32,48},{48,32},{1,17},{17,1},{33,49},{49,33},{2,18}... | collective-permute-start | bytes 1179656 | tf_op jit(solution)/shard_map/ppermute | solution.py:21
  38.1 16.5 %collective-permute-start.29 = (bf16[128,1536]{1,0:T(8,128)(2,1)S(1)}, bf16[128,1536]{1,0:T(8,128)(2,1)S(1)}, u32[]{:S(2)}, u32[]{:S(2)}) collective-permute-start(bf16[128,1536]{1,0:T(8,128)(2,1)S(1)} %get-tuple-element.75), channel_id=1, source_target_pairs={{16,32},{32,16},{48,0},{0,48},{17,33},{33,17},{49,1},{1,49},{18,34... | collective-permute-start | bytes 1179656 | tf_op jit(solution)/shard_map/ppermute | solution.py:21
  40.3 28.5 %collective-permute-start = (bf16[128,1536]{1,0:T(8,128)(2,1)S(1)}, bf16[128,1536]{1,0:T(8,128)(2,1)S(1)}, u32[]{:S(2)}, u32[]{:S(2)}) collective-permute-start(bf16[128,1536]{1,0:T(8,128)(2,1)S(1)} %get-tuple-element.51), channel_id=1, source_target_pairs={{0,16},{16,0},{32,48},{48,32},{1,17},{17,1},{33,49},{49,33},{2,18}... | collective-permute-start | bytes 1179656 | tf_op jit(solution)/shard_map/ppermute | solution.py:21
  46.2 15.2 %collective-permute-start.10 = (bf16[64,1536]{1,0:T(8,128)(2,1)S(1)}, bf16[64,1536]{1,0:T(8,128)(2,1)S(1)}, u32[]{:S(2)}, u32[]{:S(2)}) collective-permute-start(bf16[64,1536]{1,0:T(8,128)(2,1)S(1)} %get-tuple-element.61), channel_id=1, source_target_pairs={{0,16},{16,0},{32,48},{48,32},{1,17},{17,1},{33,49},{49,33},{2,18}... | collective-permute-start | bytes 589832 | tf_op jit(solution)/shard_map/ppermute | solution.py:21
  48.9 20.5 %collective-permute-start.20 = (bf16[64,1536]{1,0:T(8,128)(2,1)S(1)}, bf16[64,1536]{1,0:T(8,128)(2,1)S(1)}, u32[]{:S(2)}, u32[]{:S(2)}) collective-permute-start(bf16[64,1536]{1,0:T(8,128)(2,1)S(1)} %get-tuple-element.69), channel_id=1, source_target_pairs={{16,32},{32,16},{48,0},{0,48},{17,33},{33,17},{49,1},{1,49},{18,34... | collective-permute-start | bytes 589832 | tf_op jit(solution)/shard_map/ppermute | solution.py:21
  54.7 15.1 %collective-permute-start.30 = (bf16[64,1536]{1,0:T(8,128)(2,1)S(1)}, bf16[64,1536]{1,0:T(8,128)(2,1)S(1)}, u32[]{:S(2)}, u32[]{:S(2)}) collective-permute-start(bf16[64,1536]{1,0:T(8,128)(2,1)S(1)} %get-tuple-element.77), channel_id=1, source_target_pairs={{0,16},{16,0},{32,48},{48,32},{1,17},{17,1},{33,49},{49,33},{2,18}... | collective-permute-start | bytes 589832 | tf_op jit(solution)/shard_map/ppermute | solution.py:21
  61.5 14.5 %collective-permute-start.11 = (bf16[64,1536]{1,0:T(8,128)(2,1)S(1)}, bf16[64,1536]{1,0:T(8,128)(2,1)S(1)}, u32[]{:S(2)}, u32[]{:S(2)}) collective-permute-start(bf16[64,1536]{1,0:T(8,128)(2,1)S(1)} %get-tuple-element.63), channel_id=1, source_target_pairs={{0,8},{8,0},{1,9},{9,1},{2,10},{10,2},{3,11},{11,3},{4,12},{12,4},... | collective-permute-start | bytes 589832 | tf_op jit(solution)/shard_map/ppermute | solution.py:21
  68.9 13.3 %collective-permute-start.1 = (bf16[64,1536]{1,0:T(8,128)(2,1)S(1)}, bf16[64,1536]{1,0:T(8,128)(2,1)S(1)}, u32[]{:S(2)}, u32[]{:S(2)}) collective-permute-start(bf16[64,1536]{1,0:T(8,128)(2,1)S(1)} %get-tuple-element.53), channel_id=1, source_target_pairs={{16,32},{32,16},{48,0},{0,48},{17,33},{33,17},{49,1},{1,49},{18,34... | collective-permute-start | bytes 589832 | tf_op jit(solution)/shard_map/ppermute | solution.py:21
  69.5 19.5 %collective-permute-start.21 = (bf16[64,1536]{1,0:T(8,128)(2,1)S(1)}, bf16[64,1536]{1,0:T(8,128)(2,1)S(1)}, u32[]{:S(2)}, u32[]{:S(2)}) collective-permute-start(bf16[64,1536]{1,0:T(8,128)(2,1)S(1)} %get-tuple-element.71), channel_id=1, source_target_pairs={{0,8},{8,0},{1,9},{9,1},{2,10},{10,2},{3,11},{11,3},{4,12},{12,4},... | collective-permute-start | bytes 589832 | tf_op jit(solution)/shard_map/ppermute | solution.py:21
  69.9 21.3 %collective-permute-start.31 = (bf16[64,1536]{1,0:T(8,128)(2,1)S(1)}, bf16[64,1536]{1,0:T(8,128)(2,1)S(1)}, u32[]{:S(2)}, u32[]{:S(2)}) collective-permute-start(bf16[64,1536]{1,0:T(8,128)(2,1)S(1)} %get-tuple-element.79), channel_id=1, source_target_pairs={{0,8},{8,0},{1,9},{9,1},{2,10},{10,2},{3,11},{11,3},{4,12},{12,4},... | collective-permute-start | bytes 589832 | tf_op jit(solution)/shard_map/ppermute | solution.py:21
  76.2 25.5 %collective-permute-start.12 = (bf16[64,1536]{1,0:T(8,128)(2,1)S(1)}, bf16[64,1536]{1,0:T(8,128)(2,1)S(1)}, u32[]{:S(2)}, u32[]{:S(2)}) collective-permute-start(bf16[64,1536]{1,0:T(8,128)(2,1)S(1)} %shard_map.93.b0), channel_id=1, source_target_pairs={{16,32},{32,16},{48,0},{0,48},{17,33},{33,17},{49,1},{1,49},{18,34... | collective-permute-start | bytes 589832 | tf_op jit(solution)/shard_map/ppermute | solution.py:21
  82.2 19.4 %collective-permute-start.2 = (bf16[64,1536]{1,0:T(8,128)(2,1)S(1)}, bf16[64,1536]{1,0:T(8,128)(2,1)S(1)}, u32[]{:S(2)}, u32[]{:S(2)}) collective-permute-start(bf16[64,1536]{1,0:T(8,128)(2,1)S(1)} %get-tuple-element.55), channel_id=1, source_target_pairs={{0,8},{8,0},{1,9},{9,1},{2,10},{10,2},{3,11},{11,3},{4,12},{12,4},... | collective-permute-start | bytes 589832 | tf_op jit(solution)/shard_map/ppermute | solution.py:21
  89.1 15.6 %collective-permute-start.23 = (bf16[64,1536]{1,0:T(8,128)(2,1)S(1)}, bf16[64,1536]{1,0:T(8,128)(2,1)S(1)}, u32[]{:S(2)}, u32[]{:S(2)}) collective-permute-start(bf16[64,1536]{1,0:T(8,128)(2,1)S(1)} %shard_map.99.b0), channel_id=1, source_target_pairs={{0,16},{16,0},{32,48},{48,32},{1,17},{17,1},{33,49},{49,33},{2,18}... | collective-permute-start | bytes 589832 | tf_op jit(solution)/shard_map/ppermute | solution.py:21
  89.2 15.8 %collective-permute-start.13 = (bf16[64,1536]{1,0:T(8,128)(2,1)S(1)}, bf16[64,1536]{1,0:T(8,128)(2,1)S(1)}, u32[]{:S(2)}, u32[]{:S(2)}) collective-permute-start(bf16[64,1536]{1,0:T(8,128)(2,1)S(1)} %shard_map.93.b0), channel_id=1, source_target_pairs={{0,16},{16,0},{32,48},{48,32},{1,17},{17,1},{33,49},{49,33},{2,18}... | collective-permute-start | bytes 589832 | tf_op jit(solution)/shard_map/ppermute | solution.py:21
  91.3 14.5 %collective-permute-start.32 = (bf16[64,1536]{1,0:T(8,128)(2,1)S(1)}, bf16[64,1536]{1,0:T(8,128)(2,1)S(1)}, u32[]{:S(2)}, u32[]{:S(2)}) collective-permute-start(bf16[64,1536]{1,0:T(8,128)(2,1)S(1)} %shard_map.105.b0), channel_id=1, source_target_pairs={{16,32},{32,16},{48,0},{0,48},{17,33},{33,17},{49,1},{1,49},{18,34... | collective-permute-start | bytes 589832 | tf_op jit(solution)/shard_map/ppermute | solution.py:21
  101.6 6.7 %collective-permute-start.14 = (bf16[64,1536]{1,0:T(8,128)(2,1)S(1)}, bf16[64,1536]{1,0:T(8,128)(2,1)S(1)}, u32[]{:S(2)}, u32[]{:S(2)}) collective-permute-start(bf16[64,1536]{1,0:T(8,128)(2,1)S(1)} %collective-permute-done.12.b1), channel_id=1, source_target_pairs={{0,16},{16,0},{32,48},{48,32},{1,17},{17,1},{33,49},{49,33},{2,18}... | collective-permute-start | bytes 589832 | tf_op jit(solution)/shard_map/ppermute | solution.py:21
  101.6 9.1 %collective-permute-start.22 = (bf16[64,1536]{1,0:T(8,128)(2,1)S(1)}, bf16[64,1536]{1,0:T(8,128)(2,1)S(1)}, u32[]{:S(2)}, u32[]{:S(2)}) collective-permute-start(bf16[64,1536]{1,0:T(8,128)(2,1)S(1)} %shard_map.99.b0), channel_id=1, source_target_pairs={{16,32},{32,16},{48,0},{0,48},{17,33},{33,17},{49,1},{1,49},{18,34... | collective-permute-start | bytes 589832 | tf_op jit(solution)/shard_map/ppermute | solution.py:21
  104.7 9.0 %collective-permute-start.24 = (bf16[64,1536]{1,0:T(8,128)(2,1)S(1)}, bf16[64,1536]{1,0:T(8,128)(2,1)S(1)}, u32[]{:S(2)}, u32[]{:S(2)}) collective-permute-start(bf16[64,1536]{1,0:T(8,128)(2,1)S(1)} %collective-permute-done.23.b2), channel_id=1, source_target_pairs={{16,32},{32,16},{48,0},{0,48},{17,33},{33,17},{49,1},{1,49},{18,34... | collective-permute-start | bytes 589832 | tf_op jit(solution)/shard_map/ppermute | solution.py:21
  105.0 10.3 %collective-permute-start.33 = (bf16[64,1536]{1,0:T(8,128)(2,1)S(1)}, bf16[64,1536]{1,0:T(8,128)(2,1)S(1)}, u32[]{:S(2)}, u32[]{:S(2)}) collective-permute-start(bf16[64,1536]{1,0:T(8,128)(2,1)S(1)} %shard_map.105.b0), channel_id=1, source_target_pairs={{0,16},{16,0},{32,48},{48,32},{1,17},{17,1},{33,49},{49,33},{2,18}... | collective-permute-start | bytes 589832 | tf_op jit(solution)/shard_map/ppermute | solution.py:21
  105.8 11.2 %collective-permute-start.34 = (bf16[64,1536]{1,0:T(8,128)(2,1)S(1)}, bf16[64,1536]{1,0:T(8,128)(2,1)S(1)}, u32[]{:S(2)}, u32[]{:S(2)}) collective-permute-start(bf16[64,1536]{1,0:T(8,128)(2,1)S(1)} %collective-permute-done.32.b1), channel_id=1, source_target_pairs={{0,16},{16,0},{32,48},{48,32},{1,17},{17,1},{33,49},{49,33},{2,18}... | collective-permute-start | bytes 589832 | tf_op jit(solution)/shard_map/ppermute | solution.py:21
  108.4 12.9 %collective-permute-start.4 = (bf16[64,1536]{1,0:T(8,128)(2,1)S(1)}, bf16[64,1536]{1,0:T(8,128)(2,1)S(1)}, u32[]{:S(2)}, u32[]{:S(2)}) collective-permute-start(bf16[64,1536]{1,0:T(8,128)(2,1)S(1)} %shard_map.88.b0), channel_id=1, source_target_pairs={{0,16},{16,0},{32,48},{48,32},{1,17},{17,1},{33,49},{49,33},{2,18}... | collective-permute-start | bytes 589832 | tf_op jit(solution)/shard_map/ppermute | solution.py:21
  110.8 22.1 %collective-permute-start.15 = (bf16[256,512]{1,0:T(8,128)(2,1)S(1)}, bf16[256,512]{1,0:T(8,128)(2,1)S(1)}, u32[]{:S(2)}, u32[]{:S(2)}) collective-permute-start(bf16[256,512]{1,0:T(8,128)(2,1)S(1)} %get-tuple-element.66), channel_id=1, source_target_pairs={{0,1},{1,0},{2,3},{3,2},{4,5},{5,4},{6,7},{7,6},{8,9},{9,8},{10,11... | collective-permute-start | bytes 786440 | tf_op jit(solution)/shard_map/ppermute | solution.py:21
  115.1 19.8 %collective-permute-start.25 = (bf16[256,512]{1,0:T(8,128)(2,1)S(1)}, bf16[256,512]{1,0:T(8,128)(2,1)S(1)}, u32[]{:S(2)}, u32[]{:S(2)}) collective-permute-start(bf16[256,512]{1,0:T(8,128)(2,1)S(1)} %get-tuple-element.74), channel_id=1, source_target_pairs={{0,1},{1,0},{2,3},{3,2},{4,5},{5,4},{6,7},{7,6},{8,9},{9,8},{10,11... | collective-permute-start | bytes 786440 | tf_op jit(solution)/shard_map/ppermute | solution.py:21
  118.5 18.3 %collective-permute-start.35 = (bf16[256,512]{1,0:T(8,128)(2,1)S(1)}, bf16[256,512]{1,0:T(8,128)(2,1)S(1)}, u32[]{:S(2)}, u32[]{:S(2)}) collective-permute-start(bf16[256,512]{1,0:T(8,128)(2,1)S(1)} %get-tuple-element.82), channel_id=1, source_target_pairs={{0,1},{1,0},{2,3},{3,2},{4,5},{5,4},{6,7},{7,6},{8,9},{9,8},{10,11... | collective-permute-start | bytes 786440 | tf_op jit(solution)/shard_map/ppermute | solution.py:21
  118.6 9.0 %collective-permute-start.3 = (bf16[64,1536]{1,0:T(8,128)(2,1)S(1)}, bf16[64,1536]{1,0:T(8,128)(2,1)S(1)}, u32[]{:S(2)}, u32[]{:S(2)}) collective-permute-start(bf16[64,1536]{1,0:T(8,128)(2,1)S(1)} %shard_map.88.b0), channel_id=1, source_target_pairs={{16,32},{32,16},{48,0},{0,48},{17,33},{33,17},{49,1},{1,49},{18,34... | collective-permute-start | bytes 589832 | tf_op jit(solution)/shard_map/ppermute | solution.py:21
  121.3 10.0 %collective-permute-start.5 = (bf16[64,1536]{1,0:T(8,128)(2,1)S(1)}, bf16[64,1536]{1,0:T(8,128)(2,1)S(1)}, u32[]{:S(2)}, u32[]{:S(2)}) collective-permute-start(bf16[64,1536]{1,0:T(8,128)(2,1)S(1)} %collective-permute-done.4.b2), channel_id=1, source_target_pairs={{16,32},{32,16},{48,0},{0,48},{17,33},{33,17},{49,1},{1,49},{18,34... | collective-permute-start | bytes 589832 | tf_op jit(solution)/shard_map/ppermute | solution.py:21
  132.8 7.5 %collective-permute-start.6 = (bf16[256,512]{1,0:T(8,128)(2,1)S(1)}, bf16[256,512]{1,0:T(8,128)(2,1)S(1)}, u32[]{:S(2)}, u32[]{:S(2)}) collective-permute-start(bf16[256,512]{1,0:T(8,128)(2,1)S(1)} %get-tuple-element.58), channel_id=1, source_target_pairs={{0,1},{1,0},{2,3},{3,2},{4,5},{5,4},{6,7},{7,6},{8,9},{9,8},{10,11... | collective-permute-start | bytes 786440 | tf_op jit(solution)/shard_map/ppermute | solution.py:21
  132.9 10.8 %collective-permute-start.16 = (bf16[256,512]{1,0:T(8,128)(2,1)S(1)}, bf16[256,512]{1,0:T(8,128)(2,1)S(1)}, u32[]{:S(2)}, u32[]{:S(2)}) collective-permute-start(bf16[256,512]{1,0:T(8,128)(2,1)S(1)} %shard_map.95), channel_id=1, source_target_pairs={{0,64},{64,128},{128,192},{192,0},{1,65},{65,129},{129,193},{193,1... | collective-permute-start | bytes 786440 | tf_op jit(solution)/shard_map/ppermute | solution.py:25
  135.0 10.3 %collective-permute-start.26 = (bf16[256,512]{1,0:T(8,128)(2,1)S(1)}, bf16[256,512]{1,0:T(8,128)(2,1)S(1)}, u32[]{:S(2)}, u32[]{:S(2)}) collective-permute-start(bf16[256,512]{1,0:T(8,128)(2,1)S(1)} %shard_map.101), channel_id=1, source_target_pairs={{0,192},{64,0},{128,64},{192,128},{1,193},{65,1},{129,65},{193,129... | collective-permute-start | bytes 786440 | tf_op jit(solution)/shard_map/ppermute | solution.py:25
  136.8 15.3 %collective-permute-start.36 = (bf16[256,512]{1,0:T(8,128)(2,1)S(1)}, bf16[256,512]{1,0:T(8,128)(2,1)S(1)}, u32[]{:S(2)}, u32[]{:S(2)}) collective-permute-start(bf16[256,512]{1,0:T(8,128)(2,1)S(1)} %shard_map.107), channel_id=1, source_target_pairs={{0,128},{64,192},{128,0},{192,64},{1,129},{65,193},{129,1},{193,65... | collective-permute-start | bytes 786440 | tf_op jit(solution)/shard_map/ppermute | solution.py:25
  152.9 8.9 %collective-permute-start.37 = (bf16[256,128]{1,0:T(8,128)(2,1)S(1)}, bf16[256,128]{1,0:T(8,128)(2,1)S(1)}, u32[]{:S(2)}, u32[]{:S(2)}) collective-permute-start(bf16[256,128]{1,0:T(8,128)(2,1)S(1)} %get-tuple-element.84), channel_id=1, source_target_pairs={{0,2},{2,0},{4,6},{6,4},{1,3},{3,1},{5,7},{7,5},{8,10},{10,8},{12,... | collective-permute-start | bytes 196616 | tf_op jit(solution)/shard_map/ppermute | solution.py:223
  153.0 8.8 %collective-permute-start.38 = (bf16[256,128]{1,0:T(8,128)(2,1)S(1)}, bf16[256,128]{1,0:T(8,128)(2,1)S(1)}, u32[]{:S(2)}, u32[]{:S(2)}) collective-permute-start(bf16[256,128]{1,0:T(8,128)(2,1)S(1)} %get-tuple-element.85), channel_id=1, source_target_pairs={{0,4},{2,6},{4,0},{6,2},{1,5},{3,7},{5,1},{7,3},{8,12},{10,14},{12... | collective-permute-start | bytes 196616 | tf_op jit(solution)/shard_map/ppermute | solution.py:223
  155.0 6.8 %collective-permute-start.39 = (bf16[256,128]{1,0:T(8,128)(2,1)S(1)}, bf16[256,128]{1,0:T(8,128)(2,1)S(1)}, u32[]{:S(2)}, u32[]{:S(2)}) collective-permute-start(bf16[256,128]{1,0:T(8,128)(2,1)S(1)} %get-tuple-element.86), channel_id=1, source_target_pairs={{0,6},{2,4},{4,2},{6,0},{1,7},{3,5},{5,3},{7,1},{8,14},{10,12},{12... | collective-permute-start | bytes 196616 | tf_op jit(solution)/shard_map/ppermute | solution.py:223

commit v2 on v1

v2 whole, which is shorter than its diff:
```python
import jax
import jax.numpy as jnp
from jax import lax
from jax.experimental import pallas as pl
from jax.experimental.pallas import tpu as pltpu
from jax.sharding import Mesh, PartitionSpec as P

BF = jnp.bfloat16
F32 = jnp.float32
ROWS = 64
SIDE = ((0, 1), (2, 3))
BACK = ((1, 2), (3, 0))
ACROSS = ((0, 2), (1, 3))
FAR = ((0, 1),)


def both(pairs):
    return [q for a, b in pairs for q in ((a, b), (b, a))]


def swap(a, axis, pairs):
    return lax.ppermute(a, axis, both(pairs))


def turn(a, shift):
    return lax.ppermute(a, "y", [(i, (i + shift) % 4) for i in range(4)])


def dot(a, b, ca, cb):
    return lax.dot_general(a, b, (((ca,), (cb,)), ((), ())), preferred_element_type=F32)


def call(body, outs, args, scratch=(), scalars=0, after=(), same=None):
    vmem = pl.BlockSpec(memory_space=pltpu.VMEM)
    smem = pl.BlockSpec(memory_space=pltpu.SMEM)
    some = pl.BlockSpec(memory_space=pl.ANY)
    count = len(args)

    def run(*refs):
        body(*refs[:count], *refs[count + len(after) :])

    return pl.pallas_call(
        run,
        out_shape=[jax.ShapeDtypeStruct(s, d) for s, d in outs],
        in_specs=([smem] * scalars + [vmem] * (count - scalars) if same is None else [some] * count)
        + [some] * len(after),
        out_specs=[vmem if same is None else some] * len(outs),
        input_output_aliases={} if same is None else {same: 0},
        scratch_shapes=list(scratch),
        compiler_params=pltpu.CompilerParams(vmem_limit_bytes=40 * 1024 * 1024),
        cost_estimate=pl.CostEstimate(flops=0, bytes_accessed=0, transcendentals=0),
    )(*args, *after)


class Line:
    def __init__(self):
        self.last = ()

    def __call__(self, body, outs, args, wait=(), **options):
        result = call(body, outs, args, after=(*self.last, *wait), **options)
        self.last = (result[0],)
        return result

    def hold(self, value, *others):
        def nothing(*refs):
            pass

        result = call(nothing, [(value.shape, value.dtype)], (value, *others), after=self.last, same=0)
        self.last = (result[0],)
        return result[0]


def order_rows(place, x, dy, first, second):
    for j in range(4):
        rows = pl.ds(pl.multiple_of(place[j] * ROWS, ROWS), ROWS)
        to = first if j < 2 else second
        at = (j % 2) * ROWS
        to[at : at + ROWS, :] = x[rows, :]
        to[2 * ROWS + at : 3 * ROWS + at, :] = dy[rows, :]


def products(x, dy, weights, emit):
    r = ROWS
    wg, wu, wd = weights
    n = wg.shape[1]
    for k, (lhs, w, dim) in enumerate(((x, wg, 0), (x, wu, 0), (dy, wd, 1))):
        value = dot(lhs, w[...], 1, dim)
        for i in range(value.shape[0] // (4 * r)):
            emit(i, slice(k * n, (k + 1) * n), value[i * 4 * r : (i + 1) * 4 * r])


def spread_rows(sends, keep, base):
    r = ROWS

    def emit(i, cols, part):
        keep[i * r : (i + 1) * r, cols] = part[:r]
        for to, j in zip(sends, (2, 1, 3)):
            to[base + i * r : base + (i + 1) * r, cols] = part[j * r : (j + 1) * r].astype(BF)

    return emit


def partials(count):
    def body(*refs):
        pieces, refs = refs[: 2 * count], refs[2 * count :]
        wg, wu, wd, *sends, keep = refs
        h = 2 * ROWS
        x = jnp.concatenate([p[:h] for p in pieces], axis=0)
        dy = jnp.concatenate([p[h:] for p in pieces], axis=0)
        products(x, dy, (wg, wu, wd), spread_rows(sends, keep, 0))

    return body


def sum_and_partials(g1, g2, g3, kept, near, xs, ds, own, wg, wu, wd, send, keep, s1, s2, s3, last):
    block_sum(g1, g2, g3, kept, send, keep)
    h = 2 * ROWS
    for to in (s1, s2, s3):
        to[:ROWS, :] = own[...]
    x = jnp.concatenate([near[:h], xs[...]], axis=0)
    dy = jnp.concatenate([near[h:], ds[...]], axis=0)
    products(x, dy, (wg, wu, wd), spread_rows((s1, s2, s3), last, ROWS))


def cut(whole, top, low, again):
    h = 2 * ROWS
    top[...] = whole[:h]
    low[...] = whole[h:]
    again[...] = whole[...]


def block_sum(*refs):
    *got, kept, send, keep = refs
    tall = keep.shape[0]
    total = kept[...]
    for g in got:
        total = total + g[g.shape[0] - tall :, :].astype(F32)
    keep[...] = total
    send[...] = total.astype(BF)


def silu_grads(got, kept, out):
    n = out.shape[1] // 3
    total = [kept[:, i * n : (i + 1) * n] + got[:, i * n : (i + 1) * n].astype(F32) for i in range(3)]
    gate, up, grad = total
    sigma = 1.0 / (1.0 + jnp.exp(-gate))
    active = gate * sigma
    out[:, :n] = (grad * up * sigma * (1.0 + gate * (1.0 - sigma))).astype(BF)
    out[:, n : 2 * n] = (grad * active).astype(BF)
    out[:, 2 * n :] = (active * up).astype(BF)


def input_partial(place, own, from_side, from_back, from_across, wg, wu, other, mine, full, held):
    count = own.shape[0] // ROWS
    n = wg.shape[1]
    tall = 4 * ROWS
    for i in range(count):
        rows = slice(i * ROWS, (i + 1) * ROWS)
        for j, b in enumerate((own, from_back, from_side, from_across)):
            full[i * tall + j * ROWS : i * tall + (j + 1) * ROWS, :] = b[rows, :]
    total = dot(full[:, :n], wg[...], 1, 1) + dot(full[:, n : 2 * n], wu[...], 1, 1)
    for i in range(count):
        for j in range(4):
            rows = pl.ds(pl.multiple_of(i * tall + place[j] * ROWS, ROWS), ROWS)
            held[rows, :] = total[i * tall + j * ROWS : i * tall + (j + 1) * ROWS]
    core = place[4]
    for k in range(4):
        cols = slice(k * 128, (k + 1) * 128)
        mine[:, cols] = held[:, pl.ds(pl.multiple_of((2 * k + core) * 128, 128), 128)]
        other[:, cols] = held[:, pl.ds(pl.multiple_of((2 * k + 1 - core) * 128, 128), 128)].astype(BF)


def add_cast(mine, got, *outs):
    rows = outs[0].shape[0]
    for i, out in enumerate(outs):
        part = slice(i * rows, (i + 1) * rows)
        out[...] = (mine[part, :] + got[part, :].astype(F32)).astype(BF)


def sum_some(mine, got, r1, r2, out):
    out[...] = mine[...] + got[...].astype(F32) + r1[...].astype(F32) + r2[...].astype(F32)


def sum_near(place, mine, *refs):
    *near, s1, s2, s3, keep, held = refs
    total = mine[...]
    for r in near:
        total = total + r[...].astype(F32)
    held[...] = total
    for k, to in enumerate((keep, s1, s2, s3)):
        to[...] = held[:, pl.ds(pl.multiple_of(place[5 + k] * 128, 128), 128)].astype(to.dtype)


def sum_last(keep, *refs):
    *parts, out = refs
    total = keep[...]
    for p in parts:
        total = total + p[...].astype(F32)
    out[...] = total.astype(BF)


def weight_grads(*refs):
    tokens, (xs, ds), grads, outs = refs[:7], refs[7:9], refs[9:12], refs[12:15]
    n = outs[0].shape[1]
    h = 2 * ROWS
    full = jnp.concatenate([g[...] for g in grads], axis=0)
    for i in range(4):
        cols = slice(i * 256, (i + 1) * 256)
        x = jnp.concatenate([t[:h, cols] for t in tokens] + [xs[:, cols]], axis=0)
        both_grads = dot(x, full[:, : 2 * n], 0, 0)
        outs[0][cols, :] = both_grads[:, :n].astype(BF)
        outs[1][cols, :] = both_grads[:, n:].astype(BF)
    dy = jnp.concatenate([t[h:, :] for t in tokens] + [ds[...]], axis=0)
    for i in range(2):
        cols = slice(i * 256, (i + 1) * 256)
        outs[2][cols, :] = dot(full[:, 2 * n + i * 256 : 2 * n + (i + 1) * 256], dy, 0, 0).astype(BF)


def local(inputs, out_grad, w_gate, w_up, w_down):
    rows, width = inputs.shape
    n = w_gate.shape[1]
    x, core, zl = lax.axis_index("x"), lax.axis_index("core"), lax.axis_index("zl")
    side = jnp.where((x == 1) | (x == 2), 1, 0)
    back = jnp.where(x >= 2, 1, 0)
    me = 2 * (side ^ core) + back
    place = jnp.stack([me, me ^ 1, me ^ 2, me ^ 3, core, zl, zl ^ 1, zl ^ 2, zl ^ 3]).astype(jnp.int32)

    line = Line()
    wide = 3 * n

    def spread(blocks):
        return [swap(b, "x", pairs) for b, pairs in zip(blocks, (SIDE, BACK, ACROSS))]

    def partial(chunks):
        tall = len(chunks) * ROWS
        *sends, keep = line(
            partials(len(chunks)),
            [((tall, wide), BF)] * 3 + [((tall, wide), F32)],
            (*[c for pair in chunks for c in pair], w_gate, w_up, w_down),
        )
        return spread(sends), keep

    def far_sum(got, kept):
        send, keep = line(block_sum, [(kept.shape, BF), (kept.shape, F32)], (*got, kept))
        return swap(send, "zh", FAR), keep

    def nonlinear(got, kept, wait=()):
        (own,) = line(silu_grads, [(kept.shape, BF)], (got, kept), wait=wait)
        return own

    def back_input(own, got):
        tall = 4 * own.shape[0]
        other, mine, full = line(
            input_partial,
            [((tall, width // 2), BF), ((tall, width // 2), F32), ((tall, wide), BF)],
            (place, own, *got, w_gate, w_up),
            scratch=[pltpu.VMEM((tall, width), F32)],
            scalars=1,
        )
        return mine, swap(other, "core", FAR), full

    first, second = line(order_rows, [((rows, width), BF)] * 2, (place, inputs, out_grad), scalars=1)
    up_y, down_y = turn(first, -1), turn(first, 1)
    got0, keep0 = partial([(first, second)])
    far0, keep0 = far_sum(got0, keep0)
    up_y, down_y = line.hold(up_y), line.hold(down_y)
    chunk1 = (up_y, swap(up_y, "core", FAR))
    chunk2 = (down_y, swap(down_y, "core", FAR))
    first = line.hold(first)
    far_y = turn(first, 2)
    got12, keep12 = partial([chunk1, chunk2])
    own0 = nonlinear(far0, keep0)
    half = ((rows // 2, width), BF)
    top, low, far_y = line(cut, [half, half, ((rows, width), BF)], (far_y,))
    top, low = swap(top, "core", FAR), swap(low, "core", FAR)
    send, keep12, *sends, keep3 = line(
        sum_and_partials,
        [((2 * ROWS, wide), BF), ((2 * ROWS, wide), F32)] + [((2 * ROWS, wide), BF)] * 3 + [((ROWS, wide), F32)],
        (*got12, keep12, far_y, top, low, own0, w_gate, w_up, w_down),
    )
    far12, mixed = swap(send, "zh", FAR), spread(sends)
    far3, keep3 = far_sum(mixed, keep3)
    own12 = nonlinear(far12, keep12)
    all12 = spread([own12] * 3)
    mine0, other0, full0 = back_input(own0, mixed)
    own3 = nonlinear(far3, keep3)
    all3 = spread([own3] * 3)
    mine12, other12, full12 = back_input(own12, all12)
    parts = line(add_cast, [((rows, width // 2), BF)] * 2, (mine12, other12))
    r1, r2 = turn(parts[0], 1), turn(parts[1], -1)
    (some,) = line(sum_some, [((rows, width // 2), F32)], (mine0, other0, r1, r2))
    mine3, other3, full3 = back_input(own3, all3)
    parts = line(add_cast, [((rows, width // 2), BF)], (mine3, other3))
    near = [turn(parts[0], 2)]
    gate_grad, up_grad, down_grad = line(
        weight_grads,
        [((width, n), BF), ((width, n), BF), ((n, width), BF)],
        (first, second, *chunk1, *chunk2, far_y, top, low, full0, full12, full3),
    )
    *sends, keep = line(
        sum_near,
        [((rows, 128), BF)] * 3 + [((rows, 128), F32)],
        (place, some, *near),
        scratch=[pltpu.VMEM((rows, width // 2), F32)],
        scalars=1,
    )
    last = [lax.ppermute(s, "zl", [(i, i ^ k) for i in range(4)]) for k, s in zip((1, 2, 3), sends)]
    (input_grad,) = line(sum_last, [((rows, 128), BF)], (keep, *last))
    return input_grad, gate_grad, up_grad, down_grad


def solution(mesh):
    axes = ("y", "x", "zh", "zl", "core")
    fine = Mesh(mesh.devices.reshape(4, 4, 2, 4, 2), axes)
    tokens = P("y", ("x", "zh"))
    cols = P(("x", "zh"), ("y", "zl", "core"))
    lines = P(("y", "zl", "core"), ("x", "zh"))
    return jax.shard_map(
        local,
        mesh=fine,
        in_specs=(tokens, tokens, cols, cols, lines),
        out_specs=(P("y", ("x", "zh", "zl", "core")), cols, cols, lines),
        check_vma=False,
    )
```

time: 163 us -> 145 us (0.89)
  starting transfers between devices: 71.9 us -> 47.3 us
  waiting for transfers between devices: 67.8 us -> 74.3 us
    ppermute x31 -> x25, waiting for transfers between devices: 35.6 us -> 63.3 us  [swap(): return lax.ppermute(a, axis, both(pairs))]
    ppermute x6, waiting for transfers between devices: 32.2 us -> 5.91 us  [turn(): return lax.ppermute(a, 'y', [(i, (i + shift) % 4) for i in range(4)])]
    ppermute x31 -> x25, starting transfers between devices: 54.6 us -> 29.7 us  [swap(): return lax.ppermute(a, axis, both(pairs))]
    ppermute x3, waiting for transfers between devices: 0.01 us -> 5.08 us  [local(): lax.ppermute(s, 'zl', [(i, i ^ k) for i in range(4)])]
    ppermute x3, starting transfers between devices: 4.47 us -> 7.62 us  [local(): lax.ppermute(s, 'zl', [(i, i ^ k) for i in range(4)])]
    ppermute x6, starting transfers between devices: 12.8 us -> 10 us  [turn(): return lax.ppermute(a, 'y', [(i, (i + shift) % 4) for i in range(4)])]
    unnamed x12 -> x14, local copies, waits for them, and re-layouts: 4.61 us -> 5.84 us
    pallas_call x27 -> x22, Pallas kernels: 17.3 us -> 16.4 us  [call(): pl.pallas_call(run, out_shape=[jax.ShapeDtypeStruct(s, d) for s, d in out...]
  transfers between devices with their start and end apart: 40 -> 34, of which waited for: 18 -> 20; matrix products, arithmetic and copies ran while one was open for 0% -> 0% of each run, Pallas kernels for 9% -> 6%
where the time goes in v2:
time: 145 us
  waiting for transfers between devices  74.3 us (51%)
  starting transfers between devices  47.3 us (33%)
  Pallas kernels  16.4 us (11%)
  local copies, waits for them, and re-layouts  5.92 us (4%)
    ppermute x25, waiting for transfers between devices, swap(): return lax.ppermute(a, axis, both(pairs))  63.3 us
    ppermute x25, starting transfers between devices, swap(): return lax.ppermute(a, axis, both(pairs))  29.7 us
    pallas_call x22, Pallas kernels, call(): pl.pallas_call(run, out_shape=[jax.ShapeDtypeStruct(s, d) for s, d in out...  16.4 us
    ppermute x6, starting transfers between devices, turn(): return lax.ppermute(a, 'y', [(i, (i + shift) % 4) for i in range(4)])  10 us
    ppermute x3, starting transfers between devices, local(): lax.ppermute(s, 'zl', [(i, i ^ k) for i in range(4)])  7.62 us
    ppermute x6, waiting for transfers between devices, turn(): return lax.ppermute(a, 'y', [(i, (i + shift) % 4) for i in range(4)])  5.91 us
    unnamed x14, local copies, waits for them, and re-layouts  5.84 us
    ppermute x3, waiting for transfers between devices, local(): lax.ppermute(s, 'zl', [(i, i ^ k) for i in range(4)])  5.08 us
  transfers between devices with their start and end apart: 34, of which 20 were waited for; matrix products, arithmetic and copies ran while one was open for 0% of the time, Pallas kernels for 6%

profile of v2, /device:TPU:8, one launch (start us, length us, event | category | flops | bytes accessed | tf_op | source)
XLA Modules:
  0.0 144.9 jit_solution(12705109875613808154)
XLA Ops:
  0.8 1.1 copy-done.5
  1.9 1.0 copy-done.6
  3.5 2.3 %collective-permute-start.4 = (bf16[256,1024]{1,0:T(8,128)(2,1)S(1)}, bf16[256,1024]{1,0:T(8,128)(2,1)S(1)}, u32[]{:S(2)}, u32[]{:S(2)}) collective-permute-start(bf16[256,1024]{1,0:T(8,128)(2,1)S(1)} %get-tuple-element.45.refs_0_.refs_5_), channel_id=1, source_target_pairs={{0,192},{64,0},{128,64},{192,128},{1,193},{65,1},{129,65},{193,129... | collective-permute-start | bytes 1572872 | tf_op jit(solution)/shard_map/ppermute | solution.py:26
  5.8 1.2 copy-done.1
  7.0 1.2 copy-done.3
  8.2 1.0 shard_map.85
  9.2 2.7 %collective-permute-start.1 = (bf16[64,1536]{1,0:T(8,128)(2,1)S(1)}, bf16[64,1536]{1,0:T(8,128)(2,1)S(1)}, u32[]{:S(2)}, u32[]{:S(2)}) collective-permute-start(bf16[64,1536]{1,0:T(8,128)(2,1)S(1)} %get-tuple-element.48), channel_id=1, source_target_pairs={{16,32},{32,16},{48,0},{0,48},{17,33},{33,17},{49,1},{1,49},{18,34... | collective-permute-start | bytes 589832 | tf_op jit(solution)/shard_map/ppermute | solution.py:22
  11.9 0.8 collective-permute-start.2
  12.7 0.7 collective-permute-start
  13.4 6.6 %collective-permute-done.1.refs_1_ = bf16[64,1536]{1,0:T(8,128)(2,1)S(1)} collective-permute-done((bf16[64,1536]{1,0:T(8,128)(2,1)S(1)}, bf16[64,1536]{1,0:T(8,128)(2,1)S(1)}, u32[]{:S(2)}, u32[]{:S(2)}) %collective-permute-start.1) | collective-permute-done | bytes 196640 | tf_op jit(solution)/shard_map/ppermute | solution.py:22
  20.1 1.2 collective-permute-done.2.refs_2_
  22.0 3.5 %collective-permute-start.11 = (bf16[256,1024]{1,0:T(8,128)(2,1)S(1)}, bf16[256,1024]{1,0:T(8,128)(2,1)S(1)}, u32[]{:S(2)}, u32[]{:S(2)}) collective-permute-start(bf16[256,1024]{1,0:T(8,128)(2,1)S(1)} %shard_map.89.refs_7_.refs_0_), channel_id=1, source_target_pairs={{0,128},{64,192},{128,0},{192,64},{1,129},{65,193},{129,1},{193,65... | collective-permute-start | bytes 1572872 | tf_op jit(solution)/shard_map/ppermute | solution.py:26
  25.5 7.2 %collective-permute-start.3 = (bf16[64,1536]{1,0:T(8,128)(2,1)S(1)}, bf16[64,1536]{1,0:T(8,128)(2,1)S(1)}, u32[]{:S(2)}, u32[]{:S(2)}) collective-permute-start(bf16[64,1536]{1,0:T(8,128)(2,1)S(1)} %get-tuple-element.51.refs_1_), channel_id=1, source_target_pairs={{0,8},{8,0},{1,9},{9,1},{2,10},{10,2},{3,11},{11,3},{4,12},{12,4},... | collective-permute-start | bytes 589832 | tf_op jit(solution)/shard_map/ppermute | solution.py:22
  32.7 1.8 %shard_map.90 = (bf16[128,1536]{1,0:T(8,128)(2,1)S(1)}, bf16[128,1536]{1,0:T(8,128)(2,1)S(1)}, bf16[128,1536]{1,0:T(8,128)(2,1)S(1)}, f32[128,1536]{1,0:T(8,128)S(1)}) custom-call(bf16[256,1024]{1,0:T(8,128)(2,1)S(1)} %shard_map.87.refs_1_.refs_0_.refs_2_, bf16[256,1024]{1,0:T(8,128)(2,1)S(1)} %collective-permute-done.5.refs_1_.refs_3_, ...), custom_call_target="tpu_custom_call" | custom-call | tf_op jit(solution)/shard_map/pallas_call | solution.py:42
  34.5 2.8 %collective-permute-start.9 = (bf16[128,1536]{1,0:T(8,128)(2,1)S(1)}, bf16[128,1536]{1,0:T(8,128)(2,1)S(1)}, u32[]{:S(2)}, u32[]{:S(2)}) collective-permute-start(bf16[128,1536]{1,0:T(8,128)(2,1)S(1)} %get-tuple-element.54), channel_id=1, source_target_pairs={{16,32},{32,16},{48,0},{0,48},{17,33},{33,17},{49,1},{1,49},{18,34... | collective-permute-start | bytes 1179656 | tf_op jit(solution)/shard_map/ppermute | solution.py:22
  37.4 0.8 collective-permute-start.10
  39.5 1.0 collective-permute-done.13.refs_6_.refs_8_
  40.9 13.9 %collective-permute-done.9.refs_1_ = bf16[128,1536]{1,0:T(8,128)(2,1)S(1)} collective-permute-done((bf16[128,1536]{1,0:T(8,128)(2,1)S(1)}, bf16[128,1536]{1,0:T(8,128)(2,1)S(1)}, u32[]{:S(2)}, u32[]{:S(2)}) %collective-permute-start.9) | collective-permute-done | bytes 393248 | tf_op jit(solution)/shard_map/ppermute | solution.py:22
  55.4 1.3 shard_map.93
  56.7 1.6 %collective-permute-start.14 = (bf16[128,1536]{1,0:T(8,128)(2,1)S(1)}, bf16[128,1536]{1,0:T(8,128)(2,1)S(1)}, u32[]{:S(2)}, u32[]{:S(2)}) collective-permute-start(bf16[128,1536]{1,0:T(8,128)(2,1)S(1)} %get-tuple-element.60), channel_id=1, source_target_pairs={{0,16},{16,0},{32,48},{48,32},{1,17},{17,1},{33,49},{49,33},{2,18}... | collective-permute-start | bytes 1179656 | tf_op jit(solution)/shard_map/ppermute | solution.py:22
  58.3 2.1 %collective-permute-start.15 = (bf16[128,1536]{1,0:T(8,128)(2,1)S(1)}, bf16[128,1536]{1,0:T(8,128)(2,1)S(1)}, u32[]{:S(2)}, u32[]{:S(2)}) collective-permute-start(bf16[128,1536]{1,0:T(8,128)(2,1)S(1)} %get-tuple-element.61), channel_id=1, source_target_pairs={{16,32},{32,16},{48,0},{0,48},{17,33},{33,17},{49,1},{1,49},{18,34... | collective-permute-start | bytes 1179656 | tf_op jit(solution)/shard_map/ppermute | solution.py:22
  61.3 7.5 %collective-permute-done.14.refs_0_.refs_2_ = bf16[128,1536]{1,0:T(8,128)(2,1)S(1)} collective-permute-done((bf16[128,1536]{1,0:T(8,128)(2,1)S(1)}, bf16[128,1536]{1,0:T(8,128)(2,1)S(1)}, u32[]{:S(2)}, u32[]{:S(2)}) %collective-permute-start.14) | collective-permute-done | bytes 393248 | tf_op jit(solution)/shard_map/ppermute | solution.py:22
  68.9 6.8 %collective-permute-done.15.refs_1_.refs_3_ = bf16[128,1536]{1,0:T(8,128)(2,1)S(1)} collective-permute-done((bf16[128,1536]{1,0:T(8,128)(2,1)S(1)}, bf16[128,1536]{1,0:T(8,128)(2,1)S(1)}, u32[]{:S(2)}, u32[]{:S(2)}) %collective-permute-start.15) | collective-permute-done | bytes 393248 | tf_op jit(solution)/shard_map/ppermute | solution.py:22
  75.7 1.6 %collective-permute-done.16.refs_2_.refs_4_ = bf16[128,1536]{1,0:T(8,128)(2,1)S(1)} collective-permute-done((bf16[128,1536]{1,0:T(8,128)(2,1)S(1)}, bf16[128,1536]{1,0:T(8,128)(2,1)S(1)}, u32[]{:S(2)}, u32[]{:S(2)}) %collective-permute-start.16) | collective-permute-done | bytes 393248 | tf_op jit(solution)/shard_map/ppermute | solution.py:22
  77.4 4.6 %collective-permute-done.17.refs_0_ = bf16[128,1536]{1,0:T(8,128)(2,1)S(1)} collective-permute-done((bf16[128,1536]{1,0:T(8,128)(2,1)S(1)}, bf16[128,1536]{1,0:T(8,128)(2,1)S(1)}, u32[]{:S(2)}, u32[]{:S(2)}) %collective-permute-start.17) | collective-permute-done | bytes 393248 | tf_op jit(solution)/shard_map/ppermute | solution.py:22
  82.2 2.4 %collective-permute-start.21 = (bf16[128,1536]{1,0:T(8,128)(2,1)S(1)}, bf16[128,1536]{1,0:T(8,128)(2,1)S(1)}, u32[]{:S(2)}, u32[]{:S(2)}) collective-permute-start(bf16[128,1536]{1,0:T(8,128)(2,1)S(1)} %shard_map.95.refs_7_.refs_1_), channel_id=1, source_target_pairs={{0,32},{32,0},{16,48},{48,16},{1,33},{33,1},{17,49},{49,17},{2,34}... | collective-permute-start | bytes 1179656 | tf_op jit(solution)/shard_map/ppermute | solution.py:22
  84.7 1.0 collective-permute-start.19
  85.8 1.4 shard_map.96
  87.2 10.2 %collective-permute-done.22.refs_0_ = bf16[64,1536]{1,0:T(8,128)(2,1)S(1)} collective-permute-done((bf16[64,1536]{1,0:T(8,128)(2,1)S(1)}, bf16[64,1536]{1,0:T(8,128)(2,1)S(1)}, u32[]{:S(2)}, u32[]{:S(2)}) %collective-permute-start.22) | collective-permute-done | bytes 196640 | tf_op jit(solution)/shard_map/ppermute | solution.py:22
  97.6 2.2 %shard_map.98 = (bf16[512,512]{1,0:T(8,128)(2,1)S(1)}, f32[512,512]{1,0:T(8,128)S(1)}, bf16[512,1536]{1,0:T(8,128)(2,1)S(1)}) custom-call(s32[9]{0:T(128)S(1)} %stack.39.refs_0_, bf16[128,1536]{1,0:T(8,128)(2,1)S(1)} %shard_map.95.refs_7_.refs_1_, bf16[128,1536]{1,0:T(8,128)(2,1)S(1)} %collective-permute-done.19.refs_2_, ...), custom_call_target="tpu_custom_call" | custom-call | tf_op jit(solution)/shard_map/pallas_call | solution.py:42
  100.3 1.4 collective-permute-done.23.refs_1_
  101.9 2.0 %collective-permute-start.24 = (bf16[256,512]{1,0:T(8,128)(2,1)S(1)}, bf16[256,512]{1,0:T(8,128)(2,1)S(1)}, u32[]{:S(2)}, u32[]{:S(2)}) collective-permute-start(bf16[256,512]{1,0:T(8,128)(2,1)S(1)} %get-tuple-element.72.refs_4_), channel_id=1, source_target_pairs={{0,64},{64,128},{128,192},{192,0},{1,65},{65,129},{129,193},{193,1... | collective-permute-start | bytes 786440 | tf_op jit(solution)/shard_map/ppermute | solution.py:26
  104.0 3.5 %collective-permute-start.28 = (bf16[64,1536]{1,0:T(8,128)(2,1)S(1)}, bf16[64,1536]{1,0:T(8,128)(2,1)S(1)}, u32[]{:S(2)}, u32[]{:S(2)}) collective-permute-start(bf16[64,1536]{1,0:T(8,128)(2,1)S(1)} %shard_map.97.refs_7_.refs_1_), channel_id=1, source_target_pairs={{0,32},{32,0},{16,48},{48,16},{1,33},{33,1},{17,49},{49,17},{2,34}... | collective-permute-start | bytes 589832 | tf_op jit(solution)/shard_map/ppermute | solution.py:22
  108.0 2.2 %collective-permute-done.25.refs_3_ = bf16[256,512]{1,0:T(8,128)(2,1)S(1)} collective-permute-done((bf16[256,512]{1,0:T(8,128)(2,1)S(1)}, bf16[256,512]{1,0:T(8,128)(2,1)S(1)}, u32[]{:S(2)}, u32[]{:S(2)}) %collective-permute-start.25) | collective-permute-done | bytes 262176 | tf_op jit(solution)/shard_map/ppermute | solution.py:26
  110.5 2.3 %collective-permute-done.28.refs_4_ = bf16[64,1536]{1,0:T(8,128)(2,1)S(1)} collective-permute-done((bf16[64,1536]{1,0:T(8,128)(2,1)S(1)}, bf16[64,1536]{1,0:T(8,128)(2,1)S(1)}, u32[]{:S(2)}, u32[]{:S(2)}) %collective-permute-start.28) | collective-permute-done | bytes 196640 | tf_op jit(solution)/shard_map/ppermute | solution.py:22
  112.8 3.5 %collective-permute-done.27.refs_3_ = bf16[64,1536]{1,0:T(8,128)(2,1)S(1)} collective-permute-done((bf16[64,1536]{1,0:T(8,128)(2,1)S(1)}, bf16[64,1536]{1,0:T(8,128)(2,1)S(1)}, u32[]{:S(2)}, u32[]{:S(2)}) %collective-permute-start.27) | collective-permute-done | bytes 196640 | tf_op jit(solution)/shard_map/ppermute | solution.py:22
  116.3 1.4 shard_map.101
  117.9 1.5 %collective-permute-done.29.refs_1_ = bf16[256,512]{1,0:T(8,128)(2,1)S(1)} collective-permute-done((bf16[256,512]{1,0:T(8,128)(2,1)S(1)}, bf16[256,512]{1,0:T(8,128)(2,1)S(1)}, u32[]{:S(2)}, u32[]{:S(2)}) %collective-permute-start.29) | collective-permute-done | bytes 262176 | tf_op jit(solution)/shard_map/ppermute | solution.py:22
  119.4 2.2 %collective-permute-start.30 = (bf16[256,512]{1,0:T(8,128)(2,1)S(1)}, bf16[256,512]{1,0:T(8,128)(2,1)S(1)}, u32[]{:S(2)}, u32[]{:S(2)}) collective-permute-start(bf16[256,512]{1,0:T(8,128)(2,1)S(1)} %shard_map.102.refs_12_), channel_id=1, source_target_pairs={{0,128},{64,192},{128,0},{192,64},{1,129},{65,193},{129,1},{193,65... | collective-permute-start | bytes 786440 | tf_op jit(solution)/shard_map/ppermute | solution.py:26
  121.6 4.4 %shard_map.103 = (bf16[1024,512]{1,0:T(8,128)(2,1)}, bf16[1024,512]{1,0:T(8,128)(2,1)}, bf16[512,1024]{1,0:T(8,128)(2,1)}) custom-call(bf16[256,1024]{1,0:T(8,128)(2,1)S(1)} %shard_map.89.refs_7_.refs_0_, bf16[256,1024]{1,0:T(8,128)(2,1)S(1)} %get-tuple-element.46.refs_1_, bf16[256,1024]{1,0:T(8,128)(2,1)S(1)} %shard_map.87.refs_1_.refs_0_.refs_2_, ...), custom_call_target="tpu_custom_call" | custom-call | tf_op jit(solution)/shard_map/pallas_call | solution.py:42
  126.0 3.6 %collective-permute-done.30.refs_2_ = bf16[256,512]{1,0:T(8,128)(2,1)S(1)} collective-permute-done((bf16[256,512]{1,0:T(8,128)(2,1)S(1)}, bf16[256,512]{1,0:T(8,128)(2,1)S(1)}, u32[]{:S(2)}, u32[]{:S(2)}) %collective-permute-start.30) | collective-permute-done | bytes 262176 | tf_op jit(solution)/shard_map/ppermute | solution.py:26
  129.6 1.2 copy-done.4
  130.8 0.7 shard_map.104
  131.5 6.6 %collective-permute-start.32 = (bf16[256,128]{1,0:T(8,128)(2,1)S(1)}, bf16[256,128]{1,0:T(8,128)(2,1)S(1)}, u32[]{:S(2)}, u32[]{:S(2)}) collective-permute-start(bf16[256,128]{1,0:T(8,128)(2,1)S(1)} %get-tuple-element.82), channel_id=1, source_target_pairs={{0,4},{2,6},{4,0},{6,2},{1,5},{3,7},{5,1},{7,3},{8,12},{10,14},{12... | collective-permute-start | bytes 196616 | tf_op jit(solution)/shard_map/ppermute | solution.py:307
  138.1 1.0 collective-permute-start.33
  139.1 3.4 %collective-permute-done.32.refs_2_ = bf16[256,128]{1,0:T(8,128)(2,1)S(1)} collective-permute-done((bf16[256,128]{1,0:T(8,128)(2,1)S(1)}, bf16[256,128]{1,0:T(8,128)(2,1)S(1)}, u32[]{:S(2)}, u32[]{:S(2)}) %collective-permute-start.32) | collective-permute-done | bytes 65568 | tf_op jit(solution)/shard_map/ppermute | solution.py:307
  142.5 1.7 %collective-permute-done.33.refs_3_ = bf16[256,128]{1,0:T(8,128)(2,1)S(1)} collective-permute-done((bf16[256,128]{1,0:T(8,128)(2,1)S(1)}, bf16[256,128]{1,0:T(8,128)(2,1)S(1)}, u32[]{:S(2)}, u32[]{:S(2)}) %collective-permute-start.33) | collective-permute-done | bytes 65568 | tf_op jit(solution)/shard_map/ppermute | solution.py:307
  144.2 0.7 shard_map.105
  (57 shorter events, 6.9 us)
Async XLA Ops:
  0.6 5.2 %copy-start = (bf16[1024,512]{1,0:T(8,128)(2,1)S(1)}, bf16[1024,512]{1,0:T(8,128)(2,1)}, u32[]{:S(2)}) copy-start(bf16[1024,512]{1,0:T(8,128)(2,1)} %refs_5_.7) | copy-start | bytes 3145732
  0.7 1.1 copy-start.5
  1.9 1.0 copy-start.6
  3.5 17.9 %collective-permute-start.4 = (bf16[256,1024]{1,0:T(8,128)(2,1)S(1)}, bf16[256,1024]{1,0:T(8,128)(2,1)S(1)}, u32[]{:S(2)}, u32[]{:S(2)}) collective-permute-start(bf16[256,1024]{1,0:T(8,128)(2,1)S(1)} %get-tuple-element.45.refs_0_.refs_5_), channel_id=1, source_target_pairs={{0,192},{64,0},{128,64},{192,128},{1,193},{65,1},{129,65},{193,129... | collective-permute-start | bytes 1572872 | tf_op jit(solution)/shard_map/ppermute | solution.py:26
  5.8 15.6 %collective-permute-start.6 = (bf16[256,1024]{1,0:T(8,128)(2,1)S(1)}, bf16[256,1024]{1,0:T(8,128)(2,1)S(1)}, u32[]{:S(2)}, u32[]{:S(2)}) collective-permute-start(bf16[256,1024]{1,0:T(8,128)(2,1)S(1)} %get-tuple-element.45.refs_0_.refs_5_), channel_id=1, source_target_pairs={{0,64},{64,128},{128,192},{192,0},{1,65},{65,129},{129,193},{193,1... | collective-permute-start | bytes 1572872 | tf_op jit(solution)/shard_map/ppermute | solution.py:26
  5.8 1.2 copy-start.1
  7.0 1.2 copy-start.3
  9.2 10.8 %collective-permute-start.1 = (bf16[64,1536]{1,0:T(8,128)(2,1)S(1)}, bf16[64,1536]{1,0:T(8,128)(2,1)S(1)}, u32[]{:S(2)}, u32[]{:S(2)}) collective-permute-start(bf16[64,1536]{1,0:T(8,128)(2,1)S(1)} %get-tuple-element.48), channel_id=1, source_target_pairs={{16,32},{32,16},{48,0},{0,48},{17,33},{33,17},{49,1},{1,49},{18,34... | collective-permute-start | bytes 589832 | tf_op jit(solution)/shard_map/ppermute | solution.py:22
  11.9 9.3 %collective-permute-start.2 = (bf16[64,1536]{1,0:T(8,128)(2,1)S(1)}, bf16[64,1536]{1,0:T(8,128)(2,1)S(1)}, u32[]{:S(2)}, u32[]{:S(2)}) collective-permute-start(bf16[64,1536]{1,0:T(8,128)(2,1)S(1)} %get-tuple-element.49), channel_id=1, source_target_pairs={{0,32},{32,0},{16,48},{48,16},{1,33},{33,1},{17,49},{49,17},{2,34}... | collective-permute-start | bytes 589832 | tf_op jit(solution)/shard_map/ppermute | solution.py:22
  12.7 8.6 %collective-permute-start = (bf16[64,1536]{1,0:T(8,128)(2,1)S(1)}, bf16[64,1536]{1,0:T(8,128)(2,1)S(1)}, u32[]{:S(2)}, u32[]{:S(2)}) collective-permute-start(bf16[64,1536]{1,0:T(8,128)(2,1)S(1)} %get-tuple-element.47.refs_4_), channel_id=1, source_target_pairs={{0,16},{16,0},{32,48},{48,32},{1,17},{17,1},{33,49},{49,33},{2,18}... | collective-permute-start | bytes 589832 | tf_op jit(solution)/shard_map/ppermute | solution.py:22
  21.4 11.3 %copy-start.2 = (bf16[1024,512]{1,0:T(8,128)(2,1)S(1)}, bf16[1024,512]{1,0:T(8,128)(2,1)}, u32[]{:S(2)}) copy-start(bf16[1024,512]{1,0:T(8,128)(2,1)} %refs_6_.7) | copy-start | bytes 3145732
  21.4 11.3 %collective-permute-start.7 = (bf16[256,1024]{1,0:T(8,128)(2,1)S(1)}, bf16[256,1024]{1,0:T(8,128)(2,1)S(1)}, u32[]{:S(2)}, u32[]{:S(2)}) collective-permute-start(bf16[256,1024]{1,0:T(8,128)(2,1)S(1)} %shard_map.88.refs_1_.refs_2_.refs_4_), channel_id=1, source_target_pairs={{0,1},{1,0},{2,3},{3,2},{4,5},{5,4},{6,7},{7,6},{8,9},{9,8},{10,11... | collective-permute-start | bytes 1572872 | tf_op jit(solution)/shard_map/ppermute | solution.py:22
  21.5 11.2 %collective-permute-start.5 = (bf16[256,1024]{1,0:T(8,128)(2,1)S(1)}, bf16[256,1024]{1,0:T(8,128)(2,1)S(1)}, u32[]{:S(2)}, u32[]{:S(2)}) collective-permute-start(bf16[256,1024]{1,0:T(8,128)(2,1)S(1)} %shard_map.87.refs_1_.refs_0_.refs_2_), channel_id=1, source_target_pairs={{0,1},{1,0},{2,3},{3,2},{4,5},{5,4},{6,7},{7,6},{8,9},{9,8},{10,11... | collective-permute-start | bytes 1572872 | tf_op jit(solution)/shard_map/ppermute | solution.py:22
  22.0 16.8 %collective-permute-start.11 = (bf16[256,1024]{1,0:T(8,128)(2,1)S(1)}, bf16[256,1024]{1,0:T(8,128)(2,1)S(1)}, u32[]{:S(2)}, u32[]{:S(2)}) collective-permute-start(bf16[256,1024]{1,0:T(8,128)(2,1)S(1)} %shard_map.89.refs_7_.refs_0_), channel_id=1, source_target_pairs={{0,128},{64,192},{128,0},{192,64},{1,129},{65,193},{129,1},{193,65... | collective-permute-start | bytes 1572872 | tf_op jit(solution)/shard_map/ppermute | solution.py:26
  25.5 13.2 %collective-permute-start.3 = (bf16[64,1536]{1,0:T(8,128)(2,1)S(1)}, bf16[64,1536]{1,0:T(8,128)(2,1)S(1)}, u32[]{:S(2)}, u32[]{:S(2)}) collective-permute-start(bf16[64,1536]{1,0:T(8,128)(2,1)S(1)} %get-tuple-element.51.refs_1_), channel_id=1, source_target_pairs={{0,8},{8,0},{1,9},{9,1},{2,10},{10,2},{3,11},{11,3},{4,12},{12,4},... | collective-permute-start | bytes 589832 | tf_op jit(solution)/shard_map/ppermute | solution.py:22
  34.5 20.3 %collective-permute-start.9 = (bf16[128,1536]{1,0:T(8,128)(2,1)S(1)}, bf16[128,1536]{1,0:T(8,128)(2,1)S(1)}, u32[]{:S(2)}, u32[]{:S(2)}) collective-permute-start(bf16[128,1536]{1,0:T(8,128)(2,1)S(1)} %get-tuple-element.54), channel_id=1, source_target_pairs={{16,32},{32,16},{48,0},{0,48},{17,33},{33,17},{49,1},{1,49},{18,34... | collective-permute-start | bytes 1179656 | tf_op jit(solution)/shard_map/ppermute | solution.py:22
  37.4 17.4 %collective-permute-start.10 = (bf16[128,1536]{1,0:T(8,128)(2,1)S(1)}, bf16[128,1536]{1,0:T(8,128)(2,1)S(1)}, u32[]{:S(2)}, u32[]{:S(2)}) collective-permute-start(bf16[128,1536]{1,0:T(8,128)(2,1)S(1)} %get-tuple-element.55), channel_id=1, source_target_pairs={{0,32},{32,0},{16,48},{48,16},{1,33},{33,1},{17,49},{49,17},{2,34}... | collective-permute-start | bytes 1179656 | tf_op jit(solution)/shard_map/ppermute | solution.py:22
  38.2 17.3 %collective-permute-start.8 = (bf16[128,1536]{1,0:T(8,128)(2,1)S(1)}, bf16[128,1536]{1,0:T(8,128)(2,1)S(1)}, u32[]{:S(2)}, u32[]{:S(2)}) collective-permute-start(bf16[128,1536]{1,0:T(8,128)(2,1)S(1)} %get-tuple-element.53.refs_2_), channel_id=1, source_target_pairs={{0,16},{16,0},{32,48},{48,32},{1,17},{17,1},{33,49},{49,33},{2,18}... | collective-permute-start | bytes 1179656 | tf_op jit(solution)/shard_map/ppermute | solution.py:22
  38.9 1.6 %collective-permute-start.13 = (bf16[128,1024]{1,0:T(8,128)(2,1)S(1)}, bf16[128,1024]{1,0:T(8,128)(2,1)S(1)}, u32[]{:S(2)}, u32[]{:S(2)}) collective-permute-start(bf16[128,1024]{1,0:T(8,128)(2,1)S(1)} %get-tuple-element.59), channel_id=1, source_target_pairs={{0,1},{1,0},{2,3},{3,2},{4,5},{5,4},{6,7},{7,6},{8,9},{9,8},{10,11... | collective-permute-start | bytes 786440 | tf_op jit(solution)/shard_map/ppermute | solution.py:22
  39.0 1.9 %collective-permute-start.12 = (bf16[128,1024]{1,0:T(8,128)(2,1)S(1)}, bf16[128,1024]{1,0:T(8,128)(2,1)S(1)}, u32[]{:S(2)}, u32[]{:S(2)}) collective-permute-start(bf16[128,1024]{1,0:T(8,128)(2,1)S(1)} %get-tuple-element.58.refs_11_), channel_id=1, source_target_pairs={{0,1},{1,0},{2,3},{3,2},{4,5},{5,4},{6,7},{7,6},{8,9},{9,8},{10,11... | collective-permute-start | bytes 786440 | tf_op jit(solution)/shard_map/ppermute | solution.py:22
  56.7 12.1 %collective-permute-start.14 = (bf16[128,1536]{1,0:T(8,128)(2,1)S(1)}, bf16[128,1536]{1,0:T(8,128)(2,1)S(1)}, u32[]{:S(2)}, u32[]{:S(2)}) collective-permute-start(bf16[128,1536]{1,0:T(8,128)(2,1)S(1)} %get-tuple-element.60), channel_id=1, source_target_pairs={{0,16},{16,0},{32,48},{48,32},{1,17},{17,1},{33,49},{49,33},{2,18}... | collective-permute-start | bytes 1179656 | tf_op jit(solution)/shard_map/ppermute | solution.py:22
  58.3 17.4 %collective-permute-start.15 = (bf16[128,1536]{1,0:T(8,128)(2,1)S(1)}, bf16[128,1536]{1,0:T(8,128)(2,1)S(1)}, u32[]{:S(2)}, u32[]{:S(2)}) collective-permute-start(bf16[128,1536]{1,0:T(8,128)(2,1)S(1)} %get-tuple-element.61), channel_id=1, source_target_pairs={{16,32},{32,16},{48,0},{0,48},{17,33},{33,17},{49,1},{1,49},{18,34... | collective-permute-start | bytes 1179656 | tf_op jit(solution)/shard_map/ppermute | solution.py:22
  60.4 16.9 %collective-permute-start.16 = (bf16[128,1536]{1,0:T(8,128)(2,1)S(1)}, bf16[128,1536]{1,0:T(8,128)(2,1)S(1)}, u32[]{:S(2)}, u32[]{:S(2)}) collective-permute-start(bf16[128,1536]{1,0:T(8,128)(2,1)S(1)} %get-tuple-element.62), channel_id=1, source_target_pairs={{0,32},{32,0},{16,48},{48,16},{1,33},{33,1},{17,49},{49,17},{2,34}... | collective-permute-start | bytes 1179656 | tf_op jit(solution)/shard_map/ppermute | solution.py:22
  61.0 20.9 %collective-permute-start.17 = (bf16[128,1536]{1,0:T(8,128)(2,1)S(1)}, bf16[128,1536]{1,0:T(8,128)(2,1)S(1)}, u32[]{:S(2)}, u32[]{:S(2)}) collective-permute-start(bf16[128,1536]{1,0:T(8,128)(2,1)S(1)} %get-tuple-element.63.refs_4_), channel_id=1, source_target_pairs={{0,8},{8,0},{1,9},{9,1},{2,10},{10,2},{3,11},{11,3},{4,12},{12,4},... | collective-permute-start | bytes 1179656 | tf_op jit(solution)/shard_map/ppermute | solution.py:22
  82.2 15.4 %collective-permute-start.21 = (bf16[128,1536]{1,0:T(8,128)(2,1)S(1)}, bf16[128,1536]{1,0:T(8,128)(2,1)S(1)}, u32[]{:S(2)}, u32[]{:S(2)}) collective-permute-start(bf16[128,1536]{1,0:T(8,128)(2,1)S(1)} %shard_map.95.refs_7_.refs_1_), channel_id=1, source_target_pairs={{0,32},{32,0},{16,48},{48,16},{1,33},{33,1},{17,49},{49,17},{2,34}... | collective-permute-start | bytes 1179656 | tf_op jit(solution)/shard_map/ppermute | solution.py:22
  84.6 13.0 %collective-permute-start.20 = (bf16[128,1536]{1,0:T(8,128)(2,1)S(1)}, bf16[128,1536]{1,0:T(8,128)(2,1)S(1)}, u32[]{:S(2)}, u32[]{:S(2)}) collective-permute-start(bf16[128,1536]{1,0:T(8,128)(2,1)S(1)} %shard_map.95.refs_7_.refs_1_), channel_id=1, source_target_pairs={{16,32},{32,16},{48,0},{0,48},{17,33},{33,17},{49,1},{1,49},{18,34... | collective-permute-start | bytes 1179656 | tf_op jit(solution)/shard_map/ppermute | solution.py:22
  84.7 12.9 %collective-permute-start.19 = (bf16[128,1536]{1,0:T(8,128)(2,1)S(1)}, bf16[128,1536]{1,0:T(8,128)(2,1)S(1)}, u32[]{:S(2)}, u32[]{:S(2)}) collective-permute-start(bf16[128,1536]{1,0:T(8,128)(2,1)S(1)} %shard_map.95.refs_7_.refs_1_), channel_id=1, source_target_pairs={{0,16},{16,0},{32,48},{48,32},{1,17},{17,1},{33,49},{49,33},{2,18}... | collective-permute-start | bytes 1179656 | tf_op jit(solution)/shard_map/ppermute | solution.py:22
  85.8 11.7 %collective-permute-start.22 = (bf16[64,1536]{1,0:T(8,128)(2,1)S(1)}, bf16[64,1536]{1,0:T(8,128)(2,1)S(1)}, u32[]{:S(2)}, u32[]{:S(2)}) collective-permute-start(bf16[64,1536]{1,0:T(8,128)(2,1)S(1)} %get-tuple-element.66.refs_2_), channel_id=1, source_target_pairs={{0,8},{8,0},{1,9},{9,1},{2,10},{10,2},{3,11},{11,3},{4,12},{12,4},... | collective-permute-start | bytes 589832 | tf_op jit(solution)/shard_map/ppermute | solution.py:22
  99.7 2.0 %collective-permute-start.23 = (bf16[512,512]{1,0:T(8,128)(2,1)S(1)}, bf16[512,512]{1,0:T(8,128)(2,1)S(1)}, u32[]{:S(2)}, u32[]{:S(2)}) collective-permute-start(bf16[512,512]{1,0:T(8,128)(2,1)S(1)} %get-tuple-element.71.refs_2_), channel_id=1, source_target_pairs={{0,1},{1,0},{2,3},{3,2},{4,5},{5,4},{6,7},{7,6},{8,9},{9,8},{10,11... | collective-permute-start | bytes 1572872 | tf_op jit(solution)/shard_map/ppermute | solution.py:22
  99.8 8.2 %collective-permute-start.18 = (bf16[256,512]{1,0:T(8,128)(2,1)S(1)}, bf16[256,512]{1,0:T(8,128)(2,1)S(1)}, u32[]{:S(2)}, u32[]{:S(2)}) collective-permute-start(bf16[256,512]{1,0:T(8,128)(2,1)S(1)} %get-tuple-element.68.refs_2_), channel_id=1, source_target_pairs={{0,1},{1,0},{2,3},{3,2},{4,5},{5,4},{6,7},{7,6},{8,9},{9,8},{10,11... | collective-permute-start | bytes 786440 | tf_op jit(solution)/shard_map/ppermute | solution.py:22
  101.9 8.4 %collective-permute-start.25 = (bf16[256,512]{1,0:T(8,128)(2,1)S(1)}, bf16[256,512]{1,0:T(8,128)(2,1)S(1)}, u32[]{:S(2)}, u32[]{:S(2)}) collective-permute-start(bf16[256,512]{1,0:T(8,128)(2,1)S(1)} %get-tuple-element.73), channel_id=1, source_target_pairs={{0,192},{64,0},{128,64},{192,128},{1,193},{65,1},{129,65},{193,129... | collective-permute-start | bytes 786440 | tf_op jit(solution)/shard_map/ppermute | solution.py:26
  101.9 8.4 %collective-permute-start.24 = (bf16[256,512]{1,0:T(8,128)(2,1)S(1)}, bf16[256,512]{1,0:T(8,128)(2,1)S(1)}, u32[]{:S(2)}, u32[]{:S(2)}) collective-permute-start(bf16[256,512]{1,0:T(8,128)(2,1)S(1)} %get-tuple-element.72.refs_4_), channel_id=1, source_target_pairs={{0,64},{64,128},{128,192},{192,0},{1,65},{65,129},{129,193},{193,1... | collective-permute-start | bytes 786440 | tf_op jit(solution)/shard_map/ppermute | solution.py:26
  104.0 8.8 %collective-permute-start.28 = (bf16[64,1536]{1,0:T(8,128)(2,1)S(1)}, bf16[64,1536]{1,0:T(8,128)(2,1)S(1)}, u32[]{:S(2)}, u32[]{:S(2)}) collective-permute-start(bf16[64,1536]{1,0:T(8,128)(2,1)S(1)} %shard_map.97.refs_7_.refs_1_), channel_id=1, source_target_pairs={{0,32},{32,0},{16,48},{48,16},{1,33},{33,1},{17,49},{49,17},{2,34}... | collective-permute-start | bytes 589832 | tf_op jit(solution)/shard_map/ppermute | solution.py:22
  107.5 8.9 %collective-permute-start.27 = (bf16[64,1536]{1,0:T(8,128)(2,1)S(1)}, bf16[64,1536]{1,0:T(8,128)(2,1)S(1)}, u32[]{:S(2)}, u32[]{:S(2)}) collective-permute-start(bf16[64,1536]{1,0:T(8,128)(2,1)S(1)} %shard_map.97.refs_7_.refs_1_), channel_id=1, source_target_pairs={{16,32},{32,16},{48,0},{0,48},{17,33},{33,17},{49,1},{1,49},{18,34... | collective-permute-start | bytes 589832 | tf_op jit(solution)/shard_map/ppermute | solution.py:22
  108.0 8.3 %collective-permute-start.26 = (bf16[64,1536]{1,0:T(8,128)(2,1)S(1)}, bf16[64,1536]{1,0:T(8,128)(2,1)S(1)}, u32[]{:S(2)}, u32[]{:S(2)}) collective-permute-start(bf16[64,1536]{1,0:T(8,128)(2,1)S(1)} %shard_map.97.refs_7_.refs_1_), channel_id=1, source_target_pairs={{0,16},{16,0},{32,48},{48,32},{1,17},{17,1},{33,49},{49,33},{2,18}... | collective-permute-start | bytes 589832 | tf_op jit(solution)/shard_map/ppermute | solution.py:22
  117.8 1.6 %collective-permute-start.29 = (bf16[256,512]{1,0:T(8,128)(2,1)S(1)}, bf16[256,512]{1,0:T(8,128)(2,1)S(1)}, u32[]{:S(2)}, u32[]{:S(2)}) collective-permute-start(bf16[256,512]{1,0:T(8,128)(2,1)S(1)} %get-tuple-element.75.refs_2_), channel_id=1, source_target_pairs={{0,1},{1,0},{2,3},{3,2},{4,5},{5,4},{6,7},{7,6},{8,9},{9,8},{10,11... | collective-permute-start | bytes 786440 | tf_op jit(solution)/shard_map/ppermute | solution.py:22
  119.4 10.2 %collective-permute-start.30 = (bf16[256,512]{1,0:T(8,128)(2,1)S(1)}, bf16[256,512]{1,0:T(8,128)(2,1)S(1)}, u32[]{:S(2)}, u32[]{:S(2)}) collective-permute-start(bf16[256,512]{1,0:T(8,128)(2,1)S(1)} %shard_map.102.refs_12_), channel_id=1, source_target_pairs={{0,128},{64,192},{128,0},{192,64},{1,129},{65,193},{129,1},{193,65... | collective-permute-start | bytes 786440 | tf_op jit(solution)/shard_map/ppermute | solution.py:26
  129.6 1.2 copy-start.4
  131.5 11.0 %collective-permute-start.32 = (bf16[256,128]{1,0:T(8,128)(2,1)S(1)}, bf16[256,128]{1,0:T(8,128)(2,1)S(1)}, u32[]{:S(2)}, u32[]{:S(2)}) collective-permute-start(bf16[256,128]{1,0:T(8,128)(2,1)S(1)} %get-tuple-element.82), channel_id=1, source_target_pairs={{0,4},{2,6},{4,0},{6,2},{1,5},{3,7},{5,1},{7,3},{8,12},{10,14},{12... | collective-permute-start | bytes 196616 | tf_op jit(solution)/shard_map/ppermute | solution.py:307
  138.1 6.1 %collective-permute-start.33 = (bf16[256,128]{1,0:T(8,128)(2,1)S(1)}, bf16[256,128]{1,0:T(8,128)(2,1)S(1)}, u32[]{:S(2)}, u32[]{:S(2)}) collective-permute-start(bf16[256,128]{1,0:T(8,128)(2,1)S(1)} %get-tuple-element.83), channel_id=1, source_target_pairs={{0,6},{2,4},{4,2},{6,0},{1,7},{3,5},{5,3},{7,1},{8,14},{10,12},{12... | collective-permute-start | bytes 196616 | tf_op jit(solution)/shard_map/ppermute | solution.py:307
  139.1 5.1 %collective-permute-start.31 = (bf16[256,128]{1,0:T(8,128)(2,1)S(1)}, bf16[256,128]{1,0:T(8,128)(2,1)S(1)}, u32[]{:S(2)}, u32[]{:S(2)}) collective-permute-start(bf16[256,128]{1,0:T(8,128)(2,1)S(1)} %get-tuple-element.81.refs_4_), channel_id=1, source_target_pairs={{0,2},{2,0},{4,6},{6,4},{1,3},{3,1},{5,7},{7,5},{8,10},{10,8},{12,... | collective-permute-start | bytes 196616 | tf_op jit(solution)/shard_map/ppermute | solution.py:307

commit v3 on v2

--- a/solution.py
+++ b/solution.py
@@ -139,18 +139,24 @@
     send[...] = total.astype(BF)
 
 
-def silu_grads(got, kept, out):
-    n = out.shape[1] // 3
-    total = [kept[:, i * n : (i + 1) * n] + got[:, i * n : (i + 1) * n].astype(F32) for i in range(3)]
-    gate, up, grad = total
+def silu_grads(got, kept, *outs):
+    n = got.shape[1] // 3
+    gate, up, grad = (
+        kept[:, i * n : (i + 1) * n] + got[:, i * n : (i + 1) * n].astype(F32) for i in range(3)
+    )
     sigma = 1.0 / (1.0 + jnp.exp(-gate))
     active = gate * sigma
-    out[:, :n] = (grad * up * sigma * (1.0 + gate * (1.0 - sigma))).astype(BF)
-    out[:, n : 2 * n] = (grad * active).astype(BF)
-    out[:, 2 * n :] = (active * up).astype(BF)
-
-
-def input_partial(place, own, from_side, from_back, from_across, wg, wu, other, mine, full, held):
+    outs[0][:, :n] = (grad * up * sigma * (1.0 + gate * (1.0 - sigma))).astype(BF)
+    outs[0][:, n : 2 * n] = (grad * active).astype(BF)
+    hidden = (active * up).astype(BF)
+    if len(outs) == 1:
+        outs[0][:, 2 * n :] = hidden
+    else:
+        outs[1][...] = hidden
+
+
+def input_partial(place, own, from_side, from_back, from_across, wg, wu, *refs):
+    *others, mine, full, held = refs
     count = own.shape[0] // ROWS
     n = wg.shape[1]
     tall = 4 * ROWS
@@ -167,7 +173,10 @@
     for k in range(4):
         cols = slice(k * 128, (k + 1) * 128)
         mine[:, cols] = held[:, pl.ds(pl.multiple_of((2 * k + core) * 128, 128), 128)]
-        other[:, cols] = held[:, pl.ds(pl.multiple_of((2 * k + 1 - core) * 128, 128), 128)].astype(BF)
+        theirs = pl.ds(pl.multiple_of((2 * k + 1 - core) * 128, 128), 128)
+        part = held.shape[0] // len(others)
+        for i, other in enumerate(others):
+            other[:, cols] = held[i * part : (i + 1) * part, theirs].astype(BF)
 
 
 def add_cast(mine, got, *outs):
@@ -177,18 +186,25 @@
         out[...] = (mine[part, :] + got[part, :].astype(F32)).astype(BF)
 
 
-def sum_some(mine, got, r1, r2, out):
+def sum_some(mine, got, r1, r2, mine3, top, low, part, out):
+    h = top.shape[0]
+    part[:h, :] = (mine3[:h] + top[...].astype(F32)).astype(BF)
+    part[h:, :] = (mine3[h:] + low[...].astype(F32)).astype(BF)
     out[...] = mine[...] + got[...].astype(F32) + r1[...].astype(F32) + r2[...].astype(F32)
 
 
-def sum_near(place, mine, *refs):
-    *near, s1, s2, s3, keep, held = refs
-    total = mine[...]
-    for r in near:
-        total = total + r[...].astype(F32)
-    held[...] = total
-    for k, to in enumerate((keep, s1, s2, s3)):
-        to[...] = held[:, pl.ds(pl.multiple_of(place[5 + k] * 128, 128), 128)].astype(to.dtype)
+def sum_near(place, mine, r3, send, keep, held):
+    held[...] = mine[...] + r3[...].astype(F32)
+    for k in range(2):
+        cols = slice(k * 128, (k + 1) * 128)
+        keep[:, cols] = held[:, pl.ds(pl.multiple_of(place[5 + k] * 128, 128), 128)]
+        send[:, cols] = held[:, pl.ds(pl.multiple_of(place[7 + k] * 128, 128), 128)].astype(BF)
+
+
+def sum_half(kept, got, send, keep):
+    total = kept[...] + got[...].astype(F32)
+    keep[...] = total[:, :128]
+    send[...] = total[:, 128:].astype(BF)
 
 
 def sum_last(keep, *refs):
@@ -200,20 +216,37 @@
 
 
 def weight_grads(*refs):
-    tokens, (xs, ds), grads, outs = refs[:7], refs[7:9], refs[9:12], refs[12:15]
+    tokens, xs, grads, mark, outs = refs[:7], refs[7], refs[8:11], refs[11], refs[12:14]
+    mark[...] = jnp.zeros_like(mark)
     n = outs[0].shape[1]
     h = 2 * ROWS
-    full = jnp.concatenate([g[...] for g in grads], axis=0)
+    full = jnp.concatenate([g[:, : 2 * n] for g in grads], axis=0)
     for i in range(4):
         cols = slice(i * 256, (i + 1) * 256)
         x = jnp.concatenate([t[:h, cols] for t in tokens] + [xs[:, cols]], axis=0)
-        both_grads = dot(x, full[:, : 2 * n], 0, 0)
+        both_grads = dot(x, full, 0, 0)
         outs[0][cols, :] = both_grads[:, :n].astype(BF)
         outs[1][cols, :] = both_grads[:, n:].astype(BF)
+
+
+def join(a, b, out):
+    out[: a.shape[0], :] = a[...]
+    out[a.shape[0] :, :] = b[...]
+
+
+def down_grads(*refs):
+    tokens, (ds, first, own, side, back, across, mark, out) = refs[:7], refs[7:]
+    mark[...] = jnp.zeros_like(mark)
+    n = out.shape[0]
+    h, r = 2 * ROWS, ROWS
+    pieces = [first[:, 2 * n :]]
+    for i in range(3):
+        pieces += [b[i * r : (i + 1) * r, :] for b in (own, back, side, across)]
+    hidden = jnp.concatenate(pieces, axis=0)
     dy = jnp.concatenate([t[h:, :] for t in tokens] + [ds[...]], axis=0)
     for i in range(2):
         cols = slice(i * 256, (i + 1) * 256)
-        outs[2][cols, :] = dot(full[:, 2 * n + i * 256 : 2 * n + (i + 1) * 256], dy, 0, 0).astype(BF)
+        out[cols, :] = dot(hidden[:, cols], dy, 0, 0).astype(BF)
 
 
 def local(inputs, out_grad, w_gate, w_up, w_down):
@@ -244,22 +277,26 @@
         send, keep = line(block_sum, [(kept.shape, BF), (kept.shape, F32)], (*got, kept))
         return swap(send, "zh", FAR), keep
 
-    def nonlinear(got, kept, wait=()):
-        (own,) = line(silu_grads, [(kept.shape, BF)], (got, kept), wait=wait)
-        return own
-
-    def back_input(own, got):
+    def nonlinear(got, kept, split=True):
+        tall = kept.shape[0]
+        shapes = [(tall, 2 * n), (tall, n)] if split else [(tall, wide)]
+        return line(silu_grads, [(s, BF) for s in shapes], (got, kept))
+
+    def back_input(own, got, parts=1):
         tall = 4 * own.shape[0]
-        other, mine, full = line(
+        *others, mine, full = line(
             input_partial,
-            [((tall, width // 2), BF), ((tall, width // 2), F32), ((tall, wide), BF)],
+            [((tall // parts, width // 2), BF)] * parts
+            + [((tall, width // 2), F32), ((tall, own.shape[1]), BF)],
             (place, own, *got, w_gate, w_up),
             scratch=[pltpu.VMEM((tall, width), F32)],
             scalars=1,
         )
-        return mine, swap(other, "core", FAR), full
-
-    first, second = line(order_rows, [((rows, width), BF)] * 2, (place, inputs, out_grad), scalars=1)
+        return mine, *[swap(o, "core", FAR) for o in others], full
+
+    first, second = line(
+        order_rows, [((rows, width), BF)] * 2, (place, inputs, out_grad), scalars=1
+    )
     up_y, down_y = turn(first, -1), turn(first, 1)
     got0, keep0 = partial([(first, second)])
     far0, keep0 = far_sum(got0, keep0)
@@ -269,7 +306,7 @@
     first = line.hold(first)
     far_y = turn(first, 2)
     got12, keep12 = partial([chunk1, chunk2])
-    own0 = nonlinear(far0, keep0)
+    (own0,) = nonlinear(far0, keep0, split=False)
     half = ((rows // 2, width), BF)
     top, low, far_y = line(cut, [half, half, ((rows, width), BF)], (far_y,))
     top, low = swap(top, "core", FAR), swap(low, "core", FAR)
@@ -279,33 +316,41 @@
         (*got12, keep12, far_y, top, low, own0, w_gate, w_up, w_down),
     )
     far12, mixed = swap(send, "zh", FAR), spread(sends)
+    own12, hidden12 = nonlinear(far12, keep12)
+    all12 = spread([own12] * 3)
     far3, keep3 = far_sum(mixed, keep3)
-    own12 = nonlinear(far12, keep12)
-    all12 = spread([own12] * 3)
     mine0, other0, full0 = back_input(own0, mixed)
-    own3 = nonlinear(far3, keep3)
+    own3, hidden3 = nonlinear(far3, keep3)
     all3 = spread([own3] * 3)
     mine12, other12, full12 = back_input(own12, all12)
     parts = line(add_cast, [((rows, width // 2), BF)] * 2, (mine12, other12))
     r1, r2 = turn(parts[0], 1), turn(parts[1], -1)
-    (some,) = line(sum_some, [((rows, width // 2), F32)], (mine0, other0, r1, r2))
-    mine3, other3, full3 = back_input(own3, all3)
-    parts = line(add_cast, [((rows, width // 2), BF)], (mine3, other3))
-    near = [turn(parts[0], 2)]
-    gate_grad, up_grad, down_grad = line(
-        weight_grads,
-        [((width, n), BF), ((width, n), BF), ((n, width), BF)],
-        (first, second, *chunk1, *chunk2, far_y, top, low, full0, full12, full3),
-    )
-    *sends, keep = line(
+    mine3, top3, low3, full3 = back_input(own3, all3, parts=2)
+    part3, some = line(
+        sum_some,
+        [((rows, width // 2), BF), ((rows, width // 2), F32)],
+        (mine0, other0, r1, r2, mine3, top3, low3),
+    )
+    r3 = turn(part3, 2)
+    (hidden,) = line(join, [((3 * ROWS, n), BF)], (hidden12, hidden3))
+    hiddens = spread([hidden] * 3)
+    tokens = (first, second, *chunk1, *chunk2, far_y)
+    mark = ((8, 128), F32)
+    _, gate_grad, up_grad = line(
+        weight_grads, [mark] + [((width, n), BF)] * 2, (*tokens, top, full0, full12, full3)
+    )
+    send, keep = line(
         sum_near,
-        [((rows, 128), BF)] * 3 + [((rows, 128), F32)],
-        (place, some, *near),
+        [((rows, 256), BF), ((rows, 256), F32)],
+        (place, some, r3),
         scratch=[pltpu.VMEM((rows, width // 2), F32)],
         scalars=1,
     )
-    last = [lax.ppermute(s, "zl", [(i, i ^ k) for i in range(4)]) for k, s in zip((1, 2, 3), sends)]
-    (input_grad,) = line(sum_last, [((rows, 128), BF)], (keep, *last))
+    got = lax.ppermute(send, "zl", [(i, i ^ 2) for i in range(4)])
+    _, down_grad = line(down_grads, [mark, ((n, width), BF)], (*tokens, low, full0, hidden, *hiddens))
+    send, keep = line(sum_half, [((rows, 128), BF), ((rows, 128), F32)], (keep, got))
+    got = lax.ppermute(send, "zl", [(i, i ^ 1) for i in range(4)])
+    (input_grad,) = line(sum_last, [((rows, 128), BF)], (keep, got))
     return input_grad, gate_grad, up_grad, down_grad
 
 

time: 145 us -> 137 us (0.945)
  starting transfers between devices: 47.3 us -> 43.1 us
  waiting for transfers between devices: 74.3 us -> 70.8 us
    ppermute x3 -> x2, starting transfers between devices: 7.62 us -> 0.56 us  [the longest x1 0.46 us: local(): got = lax.ppermute(send, 'zl', [(i, i ^ 2) for i in range(4)])]
    ppermute x25 -> x29, starting transfers between devices: 29.7 us -> 35.5 us  [swap(): return lax.ppermute(a, axis, both(pairs))]
    ppermute x6, waiting for transfers between devices: 5.91 us -> 1.46 us  [turn(): return lax.ppermute(a, 'y', [(i, (i + shift) % 4) for i in range(4)])]
    ppermute x6, starting transfers between devices: 10 us -> 7.08 us  [turn(): return lax.ppermute(a, 'y', [(i, (i + shift) % 4) for i in range(4)])]
    ppermute x3 -> x2, waiting for transfers between devices: 5.08 us -> 8.04 us  [the longest x1 4.25 us: local(): got = lax.ppermute(send, 'zl', [(i, i ^ 1) for i in range(4)])]
    ppermute x25 -> x29, waiting for transfers between devices: 63.3 us -> 61.3 us  [swap(): return lax.ppermute(a, axis, both(pairs))]
    pallas_call x22 -> x24, Pallas kernels: 16.4 us -> 17.6 us  [call(): pl.pallas_call(run, out_shape=[jax.ShapeDtypeStruct(s, d) for s, d in out...]
    unnamed x14 -> x12, local copies, waits for them, and re-layouts: 5.84 us -> 4.61 us
  transfers between devices with their start and end apart: 34 -> 37, of which waited for: 20 -> 17; matrix products, arithmetic and copies ran while one was open for 0% -> 0% of each run, Pallas kernels for 6% -> 9%
where the time goes in v3:
time: 137 us
  waiting for transfers between devices  70.8 us (52%)
  starting transfers between devices  43.1 us (31%)
  Pallas kernels  17.6 us (13%)
  local copies, waits for them, and re-layouts  4.7 us (3%)
    ppermute x29, waiting for transfers between devices, swap(): return lax.ppermute(a, axis, both(pairs))  61.3 us
    ppermute x29, starting transfers between devices, swap(): return lax.ppermute(a, axis, both(pairs))  35.5 us
    pallas_call x24, Pallas kernels, call(): pl.pallas_call(run, out_shape=[jax.ShapeDtypeStruct(s, d) for s, d in out...  17.6 us
    ppermute x6, starting transfers between devices, turn(): return lax.ppermute(a, 'y', [(i, (i + shift) % 4) for i in range(4)])  7.08 us
    unnamed x12, local copies, waits for them, and re-layouts  4.61 us
    ppermute x1, waiting for transfers between devices, local(): got = lax.ppermute(send, 'zl', [(i, i ^ 1) for i in range(4)])  4.25 us
    ppermute x1, waiting for transfers between devices, local(): got = lax.ppermute(send, 'zl', [(i, i ^ 2) for i in range(4)])  3.79 us
  transfers between devices with their start and end apart: 37, of which 17 were waited for; matrix products, arithmetic and copies ran while one was open for 0% of the time, Pallas kernels for 9%

profile of v3, /device:TPU:8, one launch (start us, length us, event | category | flops | bytes accessed | tf_op | source)
XLA Modules:
  0.0 137.2 jit_solution(378157565411407272)
XLA Ops:
  0.8 1.1 copy-done.4
  1.9 1.0 copy-done.5
  3.5 2.3 %collective-permute-start.4 = (bf16[256,1024]{1,0:T(8,128)(2,1)S(1)}, bf16[256,1024]{1,0:T(8,128)(2,1)S(1)}, u32[]{:S(2)}, u32[]{:S(2)}) collective-permute-start(bf16[256,1024]{1,0:T(8,128)(2,1)S(1)} %get-tuple-element.54.refs_0_.refs_5_), channel_id=1, source_target_pairs={{0,192},{64,0},{128,64},{192,128},{1,193},{65,1},{129,65},{193,129... | collective-permute-start | bytes 1572872 | tf_op jit(solution)/shard_map/ppermute | solution.py:26
  5.8 1.2 copy-done.1
  7.0 1.2 copy-done.3
  8.2 1.0 shard_map.85
  9.2 1.4 %collective-permute-start = (bf16[64,1536]{1,0:T(8,128)(2,1)S(1)}, bf16[64,1536]{1,0:T(8,128)(2,1)S(1)}, u32[]{:S(2)}, u32[]{:S(2)}) collective-permute-start(bf16[64,1536]{1,0:T(8,128)(2,1)S(1)} %get-tuple-element.56.refs_4_), channel_id=1, source_target_pairs={{0,16},{16,0},{32,48},{48,32},{1,17},{17,1},{33,49},{49,33},{2,18}... | collective-permute-start | bytes 589832 | tf_op jit(solution)/shard_map/ppermute | solution.py:22
  10.6 2.1 %collective-permute-start.1 = (bf16[64,1536]{1,0:T(8,128)(2,1)S(1)}, bf16[64,1536]{1,0:T(8,128)(2,1)S(1)}, u32[]{:S(2)}, u32[]{:S(2)}) collective-permute-start(bf16[64,1536]{1,0:T(8,128)(2,1)S(1)} %get-tuple-element.57), channel_id=1, source_target_pairs={{16,32},{32,16},{48,0},{0,48},{17,33},{33,17},{49,1},{1,49},{18,34... | collective-permute-start | bytes 589832 | tf_op jit(solution)/shard_map/ppermute | solution.py:22
  12.7 0.7 collective-permute-start.2
  13.4 3.0 %collective-permute-done.refs_0_ = bf16[64,1536]{1,0:T(8,128)(2,1)S(1)} collective-permute-done((bf16[64,1536]{1,0:T(8,128)(2,1)S(1)}, bf16[64,1536]{1,0:T(8,128)(2,1)S(1)}, u32[]{:S(2)}, u32[]{:S(2)}) %collective-permute-start) | collective-permute-done | bytes 196640 | tf_op jit(solution)/shard_map/ppermute | solution.py:22
  16.4 5.4 %collective-permute-done.1.refs_1_ = bf16[64,1536]{1,0:T(8,128)(2,1)S(1)} collective-permute-done((bf16[64,1536]{1,0:T(8,128)(2,1)S(1)}, bf16[64,1536]{1,0:T(8,128)(2,1)S(1)}, u32[]{:S(2)}, u32[]{:S(2)}) %collective-permute-start.1) | collective-permute-done | bytes 196640 | tf_op jit(solution)/shard_map/ppermute | solution.py:22
  22.6 3.5 %collective-permute-start.11 = (bf16[256,1024]{1,0:T(8,128)(2,1)S(1)}, bf16[256,1024]{1,0:T(8,128)(2,1)S(1)}, u32[]{:S(2)}, u32[]{:S(2)}) collective-permute-start(bf16[256,1024]{1,0:T(8,128)(2,1)S(1)} %shard_map.89.refs_7_.refs_0_), channel_id=1, source_target_pairs={{0,128},{64,192},{128,0},{192,64},{1,129},{65,193},{129,1},{193,65... | collective-permute-start | bytes 1572872 | tf_op jit(solution)/shard_map/ppermute | solution.py:26
  26.1 7.2 %collective-permute-start.3 = (bf16[64,1536]{1,0:T(8,128)(2,1)S(1)}, bf16[64,1536]{1,0:T(8,128)(2,1)S(1)}, u32[]{:S(2)}, u32[]{:S(2)}) collective-permute-start(bf16[64,1536]{1,0:T(8,128)(2,1)S(1)} %get-tuple-element.60.refs_1_), channel_id=1, source_target_pairs={{0,8},{8,0},{1,9},{9,1},{2,10},{10,2},{3,11},{11,3},{4,12},{12,4},... | collective-permute-start | bytes 589832 | tf_op jit(solution)/shard_map/ppermute | solution.py:22
  33.3 1.8 %shard_map.90 = (bf16[128,1536]{1,0:T(8,128)(2,1)S(1)}, bf16[128,1536]{1,0:T(8,128)(2,1)S(1)}, bf16[128,1536]{1,0:T(8,128)(2,1)S(1)}, f32[128,1536]{1,0:T(8,128)S(1)}) custom-call(bf16[256,1024]{1,0:T(8,128)(2,1)S(1)} %shard_map.87.refs_1_.refs_0_.refs_2_, bf16[256,1024]{1,0:T(8,128)(2,1)S(1)} %collective-permute-done.5.refs_1_.refs_3_, ...), custom_call_target="tpu_custom_call" | custom-call | tf_op jit(solution)/shard_map/pallas_call | solution.py:42
  35.1 1.6 %collective-permute-start.10 = (bf16[128,1536]{1,0:T(8,128)(2,1)S(1)}, bf16[128,1536]{1,0:T(8,128)(2,1)S(1)}, u32[]{:S(2)}, u32[]{:S(2)}) collective-permute-start(bf16[128,1536]{1,0:T(8,128)(2,1)S(1)} %get-tuple-element.64), channel_id=1, source_target_pairs={{0,32},{32,0},{16,48},{48,16},{1,33},{33,1},{17,49},{49,17},{2,34}... | collective-permute-start | bytes 1179656 | tf_op jit(solution)/shard_map/ppermute | solution.py:22
  36.7 1.4 %collective-permute-start.8 = (bf16[128,1536]{1,0:T(8,128)(2,1)S(1)}, bf16[128,1536]{1,0:T(8,128)(2,1)S(1)}, u32[]{:S(2)}, u32[]{:S(2)}) collective-permute-start(bf16[128,1536]{1,0:T(8,128)(2,1)S(1)} %get-tuple-element.62.refs_2_), channel_id=1, source_target_pairs={{0,16},{16,0},{32,48},{48,32},{1,17},{17,1},{33,49},{49,33},{2,18}... | collective-permute-start | bytes 1179656 | tf_op jit(solution)/shard_map/ppermute | solution.py:22
  38.2 1.1 collective-permute-start.9
  40.1 1.0 collective-permute-done.12.refs_5_.refs_7_
  41.5 7.3 %collective-permute-done.10.refs_2_ = bf16[128,1536]{1,0:T(8,128)(2,1)S(1)} collective-permute-done((bf16[128,1536]{1,0:T(8,128)(2,1)S(1)}, bf16[128,1536]{1,0:T(8,128)(2,1)S(1)}, u32[]{:S(2)}, u32[]{:S(2)}) %collective-permute-start.10) | collective-permute-done | bytes 393248 | tf_op jit(solution)/shard_map/ppermute | solution.py:22
  48.8 6.4 %collective-permute-done.8.refs_0_ = bf16[128,1536]{1,0:T(8,128)(2,1)S(1)} collective-permute-done((bf16[128,1536]{1,0:T(8,128)(2,1)S(1)}, bf16[128,1536]{1,0:T(8,128)(2,1)S(1)}, u32[]{:S(2)}, u32[]{:S(2)}) %collective-permute-start.8) | collective-permute-done | bytes 393248 | tf_op jit(solution)/shard_map/ppermute | solution.py:22
  55.7 1.3 shard_map.93
  57.4 2.1 %collective-permute-start.15 = (bf16[128,1536]{1,0:T(8,128)(2,1)S(1)}, bf16[128,1536]{1,0:T(8,128)(2,1)S(1)}, u32[]{:S(2)}, u32[]{:S(2)}) collective-permute-start(bf16[128,1536]{1,0:T(8,128)(2,1)S(1)} %get-tuple-element.70), channel_id=1, source_target_pairs={{16,32},{32,16},{48,0},{0,48},{17,33},{33,17},{49,1},{1,49},{18,34... | collective-permute-start | bytes 1179656 | tf_op jit(solution)/shard_map/ppermute | solution.py:22
  59.5 1.9 %collective-permute-start.16 = (bf16[128,1536]{1,0:T(8,128)(2,1)S(1)}, bf16[128,1536]{1,0:T(8,128)(2,1)S(1)}, u32[]{:S(2)}, u32[]{:S(2)}) collective-permute-start(bf16[128,1536]{1,0:T(8,128)(2,1)S(1)} %get-tuple-element.71), channel_id=1, source_target_pairs={{0,32},{32,0},{16,48},{48,16},{1,33},{33,1},{17,49},{49,17},{2,34}... | collective-permute-start | bytes 1179656 | tf_op jit(solution)/shard_map/ppermute | solution.py:22
  61.5 18.3 %collective-permute-done.17.refs_0_ = bf16[128,1536]{1,0:T(8,128)(2,1)S(1)} collective-permute-done((bf16[128,1536]{1,0:T(8,128)(2,1)S(1)}, bf16[128,1536]{1,0:T(8,128)(2,1)S(1)}, u32[]{:S(2)}, u32[]{:S(2)}) %collective-permute-start.17) | collective-permute-done | bytes 393248 | tf_op jit(solution)/shard_map/ppermute | solution.py:22
  80.1 2.2 %collective-permute-start.20 = (bf16[128,1024]{1,0:T(8,128)(2,1)S(1)}, bf16[128,1024]{1,0:T(8,128)(2,1)S(1)}, u32[]{:S(2)}, u32[]{:S(2)}) collective-permute-start(bf16[128,1024]{1,0:T(8,128)(2,1)S(1)} %get-tuple-element.75.refs_4_.refs_1_), channel_id=1, source_target_pairs={{16,32},{32,16},{48,0},{0,48},{17,33},{33,17},{49,1},{1,49},{18,34... | collective-permute-start | bytes 786440 | tf_op jit(solution)/shard_map/ppermute | solution.py:22
  82.3 1.9 %collective-permute-start.21 = (bf16[128,1024]{1,0:T(8,128)(2,1)S(1)}, bf16[128,1024]{1,0:T(8,128)(2,1)S(1)}, u32[]{:S(2)}, u32[]{:S(2)}) collective-permute-start(bf16[128,1024]{1,0:T(8,128)(2,1)S(1)} %get-tuple-element.75.refs_4_.refs_1_), channel_id=1, source_target_pairs={{0,32},{32,0},{16,48},{48,16},{1,33},{33,1},{17,49},{49,17},{2,34}... | collective-permute-start | bytes 786440 | tf_op jit(solution)/shard_map/ppermute | solution.py:22
  84.3 0.9 collective-permute-start.22
  85.2 1.4 %shard_map.96 = (bf16[256,512]{1,0:T(8,128)(2,1)S(1)}, f32[256,512]{1,0:T(8,128)S(1)}, bf16[256,1536]{1,0:T(8,128)(2,1)S(1)}) custom-call(s32[9]{0:T(128)S(1)} %stack.39.refs_0_, bf16[64,1536]{1,0:T(8,128)(2,1)S(1)} %shard_map.91.refs_1_.refs_7_, bf16[128,1536]{1,0:T(8,128)(2,1)S(1)} %collective-permute-done.14.refs_0_.refs_2_, ...), custom_call_target="tpu_custom_call" | custom-call | tf_op jit(solution)/shard_map/pallas_call | solution.py:42
  86.7 10.4 %collective-permute-done.22.refs_0_ = bf16[64,1536]{1,0:T(8,128)(2,1)S(1)} collective-permute-done((bf16[64,1536]{1,0:T(8,128)(2,1)S(1)}, bf16[64,1536]{1,0:T(8,128)(2,1)S(1)}, u32[]{:S(2)}, u32[]{:S(2)}) %collective-permute-start.22) | collective-permute-done | bytes 196640 | tf_op jit(solution)/shard_map/ppermute | solution.py:22
  97.2 2.1 %shard_map.98 = (bf16[512,512]{1,0:T(8,128)(2,1)S(1)}, f32[512,512]{1,0:T(8,128)S(1)}, bf16[512,1024]{1,0:T(8,128)(2,1)S(1)}) custom-call(s32[9]{0:T(128)S(1)} %stack.39.refs_0_, bf16[128,1024]{1,0:T(8,128)(2,1)S(1)} %get-tuple-element.75.refs_4_.refs_1_, bf16[128,1024]{1,0:T(8,128)(2,1)S(1)} %collective-permute-done.19.refs_2_, ...), custom_call_target="tpu_custom_call" | custom-call | tf_op jit(solution)/shard_map/pallas_call | solution.py:42
  99.4 0.6 collective-permute-start.26
  100.2 1.5 %collective-permute-start.27 = (bf16[64,1024]{1,0:T(8,128)(2,1)S(1)}, bf16[64,1024]{1,0:T(8,128)(2,1)S(1)}, u32[]{:S(2)}, u32[]{:S(2)}) collective-permute-start(bf16[64,1024]{1,0:T(8,128)(2,1)S(1)} %get-tuple-element.80.refs_7_.refs_1_), channel_id=1, source_target_pairs={{16,32},{32,16},{48,0},{0,48},{17,33},{33,17},{49,1},{1,49},{18,34... | collective-permute-start | bytes 393224 | tf_op jit(solution)/shard_map/ppermute | solution.py:22
  101.7 2.1 %collective-permute-start.28 = (bf16[64,1024]{1,0:T(8,128)(2,1)S(1)}, bf16[64,1024]{1,0:T(8,128)(2,1)S(1)}, u32[]{:S(2)}, u32[]{:S(2)}) collective-permute-start(bf16[64,1024]{1,0:T(8,128)(2,1)S(1)} %get-tuple-element.80.refs_7_.refs_1_), channel_id=1, source_target_pairs={{0,32},{32,0},{16,48},{48,16},{1,33},{33,1},{17,49},{49,17},{2,34}... | collective-permute-start | bytes 393224 | tf_op jit(solution)/shard_map/ppermute | solution.py:22
  103.9 1.7 %collective-permute-done.26.refs_2_ = bf16[64,1024]{1,0:T(8,128)(2,1)S(1)} collective-permute-done((bf16[64,1024]{1,0:T(8,128)(2,1)S(1)}, bf16[64,1024]{1,0:T(8,128)(2,1)S(1)}, u32[]{:S(2)}, u32[]{:S(2)}) %collective-permute-start.26) | collective-permute-done | bytes 131104 | tf_op jit(solution)/shard_map/ppermute | solution.py:22
  105.9 4.0 %collective-permute-done.27.refs_3_ = bf16[64,1024]{1,0:T(8,128)(2,1)S(1)} collective-permute-done((bf16[64,1024]{1,0:T(8,128)(2,1)S(1)}, bf16[64,1024]{1,0:T(8,128)(2,1)S(1)}, u32[]{:S(2)}, u32[]{:S(2)}) %collective-permute-start.27) | collective-permute-done | bytes 131104 | tf_op jit(solution)/shard_map/ppermute | solution.py:22
  110.0 1.4 %shard_map.100 = (bf16[128,512]{1,0:T(8,128)(2,1)S(1)}, bf16[128,512]{1,0:T(8,128)(2,1)S(1)}, f32[256,512]{1,0:T(8,128)S(1)}, bf16[256,1024]{1,0:T(8,128)(2,1)S(1)}) custom-call(s32[9]{0:T(128)S(1)} %stack.39.refs_0_, bf16[64,1024]{1,0:T(8,128)(2,1)S(1)} %get-tuple-element.80.refs_7_.refs_1_, bf16[64,1024]{1,0:T(8,128)(2,1)S(1)} %collective-permute-done.26.refs_2_, ...), custom_call_target="tpu_custom_call" | custom-call | tf_op jit(solution)/shard_map/pallas_call | solution.py:42
  112.0 0.8 collective-permute-done.29.refs_5_
  113.3 0.9 collective-permute-start.31
  114.3 0.6 collective-permute-start.33
  114.9 1.3 collective-permute-start.34
  116.2 2.2 %collective-permute-start.35 = (bf16[192,512]{1,0:T(8,128)(2,1)S(1)}, bf16[192,512]{1,0:T(8,128)(2,1)S(1)}, u32[]{:S(2)}, u32[]{:S(2)}) collective-permute-start(bf16[192,512]{1,0:T(8,128)(2,1)S(1)} %shard_map.102.refs_11_.refs_9_), channel_id=1, source_target_pairs={{0,32},{32,0},{16,48},{48,16},{1,33},{33,1},{17,49},{49,17},{2,34}... | collective-permute-start | bytes 589832 | tf_op jit(solution)/shard_map/ppermute | solution.py:22
  118.4 3.4 %shard_map.103 = (f32[8,128]{1,0:T(8,128)S(1)}, bf16[1024,512]{1,0:T(8,128)(2,1)}, bf16[1024,512]{1,0:T(8,128)(2,1)}) custom-call(bf16[256,1024]{1,0:T(8,128)(2,1)S(1)} %shard_map.89.refs_7_.refs_0_, bf16[256,1024]{1,0:T(8,128)(2,1)S(1)} %get-tuple-element.55.refs_1_, bf16[256,1024]{1,0:T(8,128)(2,1)S(1)} %shard_map.87.refs_1_.refs_0_.refs_2_, ...), custom_call_target="tpu_custom_call" | custom-call | tf_op jit(solution)/shard_map/pallas_call | solution.py:42
  121.9 1.4 %collective-permute-done.31.refs_2_ = bf16[256,512]{1,0:T(8,128)(2,1)S(1)} collective-permute-done((bf16[256,512]{1,0:T(8,128)(2,1)S(1)}, bf16[256,512]{1,0:T(8,128)(2,1)S(1)}, u32[]{:S(2)}, u32[]{:S(2)}) %collective-permute-start.31) | collective-permute-done | bytes 262176 | tf_op jit(solution)/shard_map/ppermute | solution.py:26
  123.3 0.7 shard_map.104
  124.5 1.6 %collective-permute-done.34.refs_11_ = bf16[192,512]{1,0:T(8,128)(2,1)S(1)} collective-permute-done((bf16[192,512]{1,0:T(8,128)(2,1)S(1)}, bf16[192,512]{1,0:T(8,128)(2,1)S(1)}, u32[]{:S(2)}, u32[]{:S(2)}) %collective-permute-start.34) | collective-permute-done | bytes 196640 | tf_op jit(solution)/shard_map/ppermute | solution.py:22
  126.1 2.3 %shard_map.105 = (f32[8,128]{1,0:T(8,128)S(1)}, bf16[512,1024]{1,0:T(8,128)(2,1)}) custom-call(bf16[256,1024]{1,0:T(8,128)(2,1)S(1)} %shard_map.89.refs_7_.refs_0_, bf16[256,1024]{1,0:T(8,128)(2,1)S(1)} %get-tuple-element.55.refs_1_, bf16[256,1024]{1,0:T(8,128)(2,1)S(1)} %shard_map.87.refs_1_.refs_0_.refs_2_, ...), custom_call_target="tpu_custom_call" | custom-call | tf_op jit(solution)/shard_map/pallas_call | solution.py:42
  128.4 3.8 %collective-permute-done.32.refs_1_ = bf16[256,256]{1,0:T(8,128)(2,1)S(1)} collective-permute-done((bf16[256,256]{1,0:T(8,128)(2,1)S(1)}, bf16[256,256]{1,0:T(8,128)(2,1)S(1)}, u32[]{:S(2)}, u32[]{:S(2)}) %collective-permute-start.32) | collective-permute-done | bytes 131104 | tf_op jit(solution)/shard_map/ppermute | solution.py:349
  132.3 4.3 %collective-permute-done.36.refs_1_ = bf16[256,128]{1,0:T(8,128)(2,1)S(1)} collective-permute-done((bf16[256,128]{1,0:T(8,128)(2,1)S(1)}, bf16[256,128]{1,0:T(8,128)(2,1)S(1)}, u32[]{:S(2)}, u32[]{:S(2)}) %collective-permute-start.36) | collective-permute-done | bytes 65568 | tf_op jit(solution)/shard_map/ppermute | solution.py:352
  (63 shorter events, 7.1 us)
Async XLA Ops:
  0.6 5.2 %copy-start = (bf16[1024,512]{1,0:T(8,128)(2,1)S(1)}, bf16[1024,512]{1,0:T(8,128)(2,1)}, u32[]{:S(2)}) copy-start(bf16[1024,512]{1,0:T(8,128)(2,1)} %refs_5_.7) | copy-start | bytes 3145732
  0.7 1.1 copy-start.4
  1.9 1.0 copy-start.5
  3.5 18.4 %collective-permute-start.4 = (bf16[256,1024]{1,0:T(8,128)(2,1)S(1)}, bf16[256,1024]{1,0:T(8,128)(2,1)S(1)}, u32[]{:S(2)}, u32[]{:S(2)}) collective-permute-start(bf16[256,1024]{1,0:T(8,128)(2,1)S(1)} %get-tuple-element.54.refs_0_.refs_5_), channel_id=1, source_target_pairs={{0,192},{64,0},{128,64},{192,128},{1,193},{65,1},{129,65},{193,129... | collective-permute-start | bytes 1572872 | tf_op jit(solution)/shard_map/ppermute | solution.py:26
  5.8 16.2 %collective-permute-start.6 = (bf16[256,1024]{1,0:T(8,128)(2,1)S(1)}, bf16[256,1024]{1,0:T(8,128)(2,1)S(1)}, u32[]{:S(2)}, u32[]{:S(2)}) collective-permute-start(bf16[256,1024]{1,0:T(8,128)(2,1)S(1)} %get-tuple-element.54.refs_0_.refs_5_), channel_id=1, source_target_pairs={{0,64},{64,128},{128,192},{192,0},{1,65},{65,129},{129,193},{193,1... | collective-permute-start | bytes 1572872 | tf_op jit(solution)/shard_map/ppermute | solution.py:26
  5.8 1.2 copy-start.1
  7.0 1.2 copy-start.3
  9.2 7.2 %collective-permute-start = (bf16[64,1536]{1,0:T(8,128)(2,1)S(1)}, bf16[64,1536]{1,0:T(8,128)(2,1)S(1)}, u32[]{:S(2)}, u32[]{:S(2)}) collective-permute-start(bf16[64,1536]{1,0:T(8,128)(2,1)S(1)} %get-tuple-element.56.refs_4_), channel_id=1, source_target_pairs={{0,16},{16,0},{32,48},{48,32},{1,17},{17,1},{33,49},{49,33},{2,18}... | collective-permute-start | bytes 589832 | tf_op jit(solution)/shard_map/ppermute | solution.py:22
  10.6 11.2 %collective-permute-start.1 = (bf16[64,1536]{1,0:T(8,128)(2,1)S(1)}, bf16[64,1536]{1,0:T(8,128)(2,1)S(1)}, u32[]{:S(2)}, u32[]{:S(2)}) collective-permute-start(bf16[64,1536]{1,0:T(8,128)(2,1)S(1)} %get-tuple-element.57), channel_id=1, source_target_pairs={{16,32},{32,16},{48,0},{0,48},{17,33},{33,17},{49,1},{1,49},{18,34... | collective-permute-start | bytes 589832 | tf_op jit(solution)/shard_map/ppermute | solution.py:22
  12.7 9.1 %collective-permute-start.2 = (bf16[64,1536]{1,0:T(8,128)(2,1)S(1)}, bf16[64,1536]{1,0:T(8,128)(2,1)S(1)}, u32[]{:S(2)}, u32[]{:S(2)}) collective-permute-start(bf16[64,1536]{1,0:T(8,128)(2,1)S(1)} %get-tuple-element.58), channel_id=1, source_target_pairs={{0,32},{32,0},{16,48},{48,16},{1,33},{33,1},{17,49},{49,17},{2,34}... | collective-permute-start | bytes 589832 | tf_op jit(solution)/shard_map/ppermute | solution.py:22
  22.0 11.3 %copy-start.2 = (bf16[1024,512]{1,0:T(8,128)(2,1)S(1)}, bf16[1024,512]{1,0:T(8,128)(2,1)}, u32[]{:S(2)}) copy-start(bf16[1024,512]{1,0:T(8,128)(2,1)} %refs_6_.7) | copy-start | bytes 3145732
  22.0 11.3 %collective-permute-start.7 = (bf16[256,1024]{1,0:T(8,128)(2,1)S(1)}, bf16[256,1024]{1,0:T(8,128)(2,1)S(1)}, u32[]{:S(2)}, u32[]{:S(2)}) collective-permute-start(bf16[256,1024]{1,0:T(8,128)(2,1)S(1)} %shard_map.88.refs_1_.refs_2_.refs_4_), channel_id=1, source_target_pairs={{0,1},{1,0},{2,3},{3,2},{4,5},{5,4},{6,7},{7,6},{8,9},{9,8},{10,11... | collective-permute-start | bytes 1572872 | tf_op jit(solution)/shard_map/ppermute | solution.py:22
  22.1 11.2 %collective-permute-start.5 = (bf16[256,1024]{1,0:T(8,128)(2,1)S(1)}, bf16[256,1024]{1,0:T(8,128)(2,1)S(1)}, u32[]{:S(2)}, u32[]{:S(2)}) collective-permute-start(bf16[256,1024]{1,0:T(8,128)(2,1)S(1)} %shard_map.87.refs_1_.refs_0_.refs_2_), channel_id=1, source_target_pairs={{0,1},{1,0},{2,3},{3,2},{4,5},{5,4},{6,7},{7,6},{8,9},{9,8},{10,11... | collective-permute-start | bytes 1572872 | tf_op jit(solution)/shard_map/ppermute | solution.py:22
  22.6 16.8 %collective-permute-start.11 = (bf16[256,1024]{1,0:T(8,128)(2,1)S(1)}, bf16[256,1024]{1,0:T(8,128)(2,1)S(1)}, u32[]{:S(2)}, u32[]{:S(2)}) collective-permute-start(bf16[256,1024]{1,0:T(8,128)(2,1)S(1)} %shard_map.89.refs_7_.refs_0_), channel_id=1, source_target_pairs={{0,128},{64,192},{128,0},{192,64},{1,129},{65,193},{129,1},{193,65... | collective-permute-start | bytes 1572872 | tf_op jit(solution)/shard_map/ppermute | solution.py:26
  26.1 13.2 %collective-permute-start.3 = (bf16[64,1536]{1,0:T(8,128)(2,1)S(1)}, bf16[64,1536]{1,0:T(8,128)(2,1)S(1)}, u32[]{:S(2)}, u32[]{:S(2)}) collective-permute-start(bf16[64,1536]{1,0:T(8,128)(2,1)S(1)} %get-tuple-element.60.refs_1_), channel_id=1, source_target_pairs={{0,8},{8,0},{1,9},{9,1},{2,10},{10,2},{3,11},{11,3},{4,12},{12,4},... | collective-permute-start | bytes 589832 | tf_op jit(solution)/shard_map/ppermute | solution.py:22
  35.1 13.7 %collective-permute-start.10 = (bf16[128,1536]{1,0:T(8,128)(2,1)S(1)}, bf16[128,1536]{1,0:T(8,128)(2,1)S(1)}, u32[]{:S(2)}, u32[]{:S(2)}) collective-permute-start(bf16[128,1536]{1,0:T(8,128)(2,1)S(1)} %get-tuple-element.64), channel_id=1, source_target_pairs={{0,32},{32,0},{16,48},{48,16},{1,33},{33,1},{17,49},{49,17},{2,34}... | collective-permute-start | bytes 1179656 | tf_op jit(solution)/shard_map/ppermute | solution.py:22
  36.7 18.4 %collective-permute-start.8 = (bf16[128,1536]{1,0:T(8,128)(2,1)S(1)}, bf16[128,1536]{1,0:T(8,128)(2,1)S(1)}, u32[]{:S(2)}, u32[]{:S(2)}) collective-permute-start(bf16[128,1536]{1,0:T(8,128)(2,1)S(1)} %get-tuple-element.62.refs_2_), channel_id=1, source_target_pairs={{0,16},{16,0},{32,48},{48,32},{1,17},{17,1},{33,49},{49,33},{2,18}... | collective-permute-start | bytes 1179656 | tf_op jit(solution)/shard_map/ppermute | solution.py:22
  38.2 17.5 %collective-permute-start.9 = (bf16[128,1536]{1,0:T(8,128)(2,1)S(1)}, bf16[128,1536]{1,0:T(8,128)(2,1)S(1)}, u32[]{:S(2)}, u32[]{:S(2)}) collective-permute-start(bf16[128,1536]{1,0:T(8,128)(2,1)S(1)} %get-tuple-element.63), channel_id=1, source_target_pairs={{16,32},{32,16},{48,0},{0,48},{17,33},{33,17},{49,1},{1,49},{18,34... | collective-permute-start | bytes 1179656 | tf_op jit(solution)/shard_map/ppermute | solution.py:22
  39.5 1.6 %collective-permute-start.12 = (bf16[128,1024]{1,0:T(8,128)(2,1)S(1)}, bf16[128,1024]{1,0:T(8,128)(2,1)S(1)}, u32[]{:S(2)}, u32[]{:S(2)}) collective-permute-start(bf16[128,1024]{1,0:T(8,128)(2,1)S(1)} %get-tuple-element.67.refs_11_), channel_id=1, source_target_pairs={{0,1},{1,0},{2,3},{3,2},{4,5},{5,4},{6,7},{7,6},{8,9},{9,8},{10,11... | collective-permute-start | bytes 786440 | tf_op jit(solution)/shard_map/ppermute | solution.py:22
  39.6 1.9 %collective-permute-start.13 = (bf16[128,1024]{1,0:T(8,128)(2,1)S(1)}, bf16[128,1024]{1,0:T(8,128)(2,1)S(1)}, u32[]{:S(2)}, u32[]{:S(2)}) collective-permute-start(bf16[128,1024]{1,0:T(8,128)(2,1)S(1)} %get-tuple-element.68), channel_id=1, source_target_pairs={{0,1},{1,0},{2,3},{3,2},{4,5},{5,4},{6,7},{7,6},{8,9},{9,8},{10,11... | collective-permute-start | bytes 786440 | tf_op jit(solution)/shard_map/ppermute | solution.py:22
  57.0 22.8 %collective-permute-start.17 = (bf16[128,1536]{1,0:T(8,128)(2,1)S(1)}, bf16[128,1536]{1,0:T(8,128)(2,1)S(1)}, u32[]{:S(2)}, u32[]{:S(2)}) collective-permute-start(bf16[128,1536]{1,0:T(8,128)(2,1)S(1)} %get-tuple-element.73.refs_2_), channel_id=1, source_target_pairs={{0,8},{8,0},{1,9},{9,1},{2,10},{10,2},{3,11},{11,3},{4,12},{12,4},... | collective-permute-start | bytes 1179656 | tf_op jit(solution)/shard_map/ppermute | solution.py:22
  57.4 24.9 %collective-permute-start.14 = (bf16[128,1536]{1,0:T(8,128)(2,1)S(1)}, bf16[128,1536]{1,0:T(8,128)(2,1)S(1)}, u32[]{:S(2)}, u32[]{:S(2)}) collective-permute-start(bf16[128,1536]{1,0:T(8,128)(2,1)S(1)} %get-tuple-element.69), channel_id=1, source_target_pairs={{0,16},{16,0},{32,48},{48,32},{1,17},{17,1},{33,49},{49,33},{2,18}... | collective-permute-start | bytes 1179656 | tf_op jit(solution)/shard_map/ppermute | solution.py:22
  57.4 26.7 %collective-permute-start.15 = (bf16[128,1536]{1,0:T(8,128)(2,1)S(1)}, bf16[128,1536]{1,0:T(8,128)(2,1)S(1)}, u32[]{:S(2)}, u32[]{:S(2)}) collective-permute-start(bf16[128,1536]{1,0:T(8,128)(2,1)S(1)} %get-tuple-element.70), channel_id=1, source_target_pairs={{16,32},{32,16},{48,0},{0,48},{17,33},{33,17},{49,1},{1,49},{18,34... | collective-permute-start | bytes 1179656 | tf_op jit(solution)/shard_map/ppermute | solution.py:22
  59.5 24.6 %collective-permute-start.16 = (bf16[128,1536]{1,0:T(8,128)(2,1)S(1)}, bf16[128,1536]{1,0:T(8,128)(2,1)S(1)}, u32[]{:S(2)}, u32[]{:S(2)}) collective-permute-start(bf16[128,1536]{1,0:T(8,128)(2,1)S(1)} %get-tuple-element.71), channel_id=1, source_target_pairs={{0,32},{32,0},{16,48},{48,16},{1,33},{33,1},{17,49},{49,17},{2,34}... | collective-permute-start | bytes 1179656 | tf_op jit(solution)/shard_map/ppermute | solution.py:22
  80.0 17.1 %collective-permute-start.19 = (bf16[128,1024]{1,0:T(8,128)(2,1)S(1)}, bf16[128,1024]{1,0:T(8,128)(2,1)S(1)}, u32[]{:S(2)}, u32[]{:S(2)}) collective-permute-start(bf16[128,1024]{1,0:T(8,128)(2,1)S(1)} %get-tuple-element.75.refs_4_.refs_1_), channel_id=1, source_target_pairs={{0,16},{16,0},{32,48},{48,32},{1,17},{17,1},{33,49},{49,33},{2,18}... | collective-permute-start | bytes 786440 | tf_op jit(solution)/shard_map/ppermute | solution.py:22
  80.1 17.1 %collective-permute-start.20 = (bf16[128,1024]{1,0:T(8,128)(2,1)S(1)}, bf16[128,1024]{1,0:T(8,128)(2,1)S(1)}, u32[]{:S(2)}, u32[]{:S(2)}) collective-permute-start(bf16[128,1024]{1,0:T(8,128)(2,1)S(1)} %get-tuple-element.75.refs_4_.refs_1_), channel_id=1, source_target_pairs={{16,32},{32,16},{48,0},{0,48},{17,33},{33,17},{49,1},{1,49},{18,34... | collective-permute-start | bytes 786440 | tf_op jit(solution)/shard_map/ppermute | solution.py:22
  82.3 14.9 %collective-permute-start.21 = (bf16[128,1024]{1,0:T(8,128)(2,1)S(1)}, bf16[128,1024]{1,0:T(8,128)(2,1)S(1)}, u32[]{:S(2)}, u32[]{:S(2)}) collective-permute-start(bf16[128,1024]{1,0:T(8,128)(2,1)S(1)} %get-tuple-element.75.refs_4_.refs_1_), channel_id=1, source_target_pairs={{0,32},{32,0},{16,48},{48,16},{1,33},{33,1},{17,49},{49,17},{2,34}... | collective-permute-start | bytes 786440 | tf_op jit(solution)/shard_map/ppermute | solution.py:22
  84.3 12.7 %collective-permute-start.22 = (bf16[64,1536]{1,0:T(8,128)(2,1)S(1)}, bf16[64,1536]{1,0:T(8,128)(2,1)S(1)}, u32[]{:S(2)}, u32[]{:S(2)}) collective-permute-start(bf16[64,1536]{1,0:T(8,128)(2,1)S(1)} %get-tuple-element.76.refs_7_), channel_id=1, source_target_pairs={{0,8},{8,0},{1,9},{9,1},{2,10},{10,2},{3,11},{11,3},{4,12},{12,4},... | collective-permute-start | bytes 589832 | tf_op jit(solution)/shard_map/ppermute | solution.py:22
  99.3 4.4 %collective-permute-start.23 = (bf16[512,512]{1,0:T(8,128)(2,1)S(1)}, bf16[512,512]{1,0:T(8,128)(2,1)S(1)}, u32[]{:S(2)}, u32[]{:S(2)}) collective-permute-start(bf16[512,512]{1,0:T(8,128)(2,1)S(1)} %get-tuple-element.82.refs_2_), channel_id=1, source_target_pairs={{0,1},{1,0},{2,3},{3,2},{4,5},{5,4},{6,7},{7,6},{8,9},{9,8},{10,11... | collective-permute-start | bytes 1572872 | tf_op jit(solution)/shard_map/ppermute | solution.py:22
  99.4 6.2 %collective-permute-start.26 = (bf16[64,1024]{1,0:T(8,128)(2,1)S(1)}, bf16[64,1024]{1,0:T(8,128)(2,1)S(1)}, u32[]{:S(2)}, u32[]{:S(2)}) collective-permute-start(bf16[64,1024]{1,0:T(8,128)(2,1)S(1)} %get-tuple-element.80.refs_7_.refs_1_), channel_id=1, source_target_pairs={{0,16},{16,0},{32,48},{48,32},{1,17},{17,1},{33,49},{49,33},{2,18}... | collective-permute-start | bytes 393224 | tf_op jit(solution)/shard_map/ppermute | solution.py:22
  100.0 12.0 %collective-permute-start.18 = (bf16[256,512]{1,0:T(8,128)(2,1)S(1)}, bf16[256,512]{1,0:T(8,128)(2,1)S(1)}, u32[]{:S(2)}, u32[]{:S(2)}) collective-permute-start(bf16[256,512]{1,0:T(8,128)(2,1)S(1)} %get-tuple-element.78.refs_2_), channel_id=1, source_target_pairs={{0,1},{1,0},{2,3},{3,2},{4,5},{5,4},{6,7},{7,6},{8,9},{9,8},{10,11... | collective-permute-start | bytes 786440 | tf_op jit(solution)/shard_map/ppermute | solution.py:22
  100.2 9.8 %collective-permute-start.27 = (bf16[64,1024]{1,0:T(8,128)(2,1)S(1)}, bf16[64,1024]{1,0:T(8,128)(2,1)S(1)}, u32[]{:S(2)}, u32[]{:S(2)}) collective-permute-start(bf16[64,1024]{1,0:T(8,128)(2,1)S(1)} %get-tuple-element.80.refs_7_.refs_1_), channel_id=1, source_target_pairs={{16,32},{32,16},{48,0},{0,48},{17,33},{33,17},{49,1},{1,49},{18,34... | collective-permute-start | bytes 393224 | tf_op jit(solution)/shard_map/ppermute | solution.py:22
  101.7 8.3 %collective-permute-start.28 = (bf16[64,1024]{1,0:T(8,128)(2,1)S(1)}, bf16[64,1024]{1,0:T(8,128)(2,1)S(1)}, u32[]{:S(2)}, u32[]{:S(2)}) collective-permute-start(bf16[64,1024]{1,0:T(8,128)(2,1)S(1)} %get-tuple-element.80.refs_7_.refs_1_), channel_id=1, source_target_pairs={{0,32},{32,0},{16,48},{48,16},{1,33},{33,1},{17,49},{49,17},{2,34}... | collective-permute-start | bytes 393224 | tf_op jit(solution)/shard_map/ppermute | solution.py:22
  103.8 9.3 %collective-permute-start.24 = (bf16[256,512]{1,0:T(8,128)(2,1)S(1)}, bf16[256,512]{1,0:T(8,128)(2,1)S(1)}, u32[]{:S(2)}, u32[]{:S(2)}) collective-permute-start(bf16[256,512]{1,0:T(8,128)(2,1)S(1)} %get-tuple-element.83.refs_7_), channel_id=1, source_target_pairs={{0,64},{64,128},{128,192},{192,0},{1,65},{65,129},{129,193},{193,1... | collective-permute-start | bytes 786440 | tf_op jit(solution)/shard_map/ppermute | solution.py:26
  105.6 7.5 %collective-permute-start.25 = (bf16[256,512]{1,0:T(8,128)(2,1)S(1)}, bf16[256,512]{1,0:T(8,128)(2,1)S(1)}, u32[]{:S(2)}, u32[]{:S(2)}) collective-permute-start(bf16[256,512]{1,0:T(8,128)(2,1)S(1)} %get-tuple-element.84), channel_id=1, source_target_pairs={{0,192},{64,0},{128,64},{192,128},{1,193},{65,1},{129,65},{193,129... | collective-permute-start | bytes 786440 | tf_op jit(solution)/shard_map/ppermute | solution.py:26
  111.4 1.4 %collective-permute-start.29 = (bf16[128,512]{1,0:T(8,128)(2,1)S(1)}, bf16[128,512]{1,0:T(8,128)(2,1)S(1)}, u32[]{:S(2)}, u32[]{:S(2)}) collective-permute-start(bf16[128,512]{1,0:T(8,128)(2,1)S(1)} %get-tuple-element.86.refs_7_), channel_id=1, source_target_pairs={{0,1},{1,0},{2,3},{3,2},{4,5},{5,4},{6,7},{7,6},{8,9},{9,8},{10,11... | collective-permute-start | bytes 393224 | tf_op jit(solution)/shard_map/ppermute | solution.py:22
  111.5 1.7 %collective-permute-start.30 = (bf16[128,512]{1,0:T(8,128)(2,1)S(1)}, bf16[128,512]{1,0:T(8,128)(2,1)S(1)}, u32[]{:S(2)}, u32[]{:S(2)}) collective-permute-start(bf16[128,512]{1,0:T(8,128)(2,1)S(1)} %get-tuple-element.87), channel_id=1, source_target_pairs={{0,1},{1,0},{2,3},{3,2},{4,5},{5,4},{6,7},{7,6},{8,9},{9,8},{10,11... | collective-permute-start | bytes 393224 | tf_op jit(solution)/shard_map/ppermute | solution.py:22
  113.3 10.0 %collective-permute-start.31 = (bf16[256,512]{1,0:T(8,128)(2,1)S(1)}, bf16[256,512]{1,0:T(8,128)(2,1)S(1)}, u32[]{:S(2)}, u32[]{:S(2)}) collective-permute-start(bf16[256,512]{1,0:T(8,128)(2,1)S(1)} %get-tuple-element.89.refs_2_), channel_id=1, source_target_pairs={{0,128},{64,192},{128,0},{192,64},{1,129},{65,193},{129,1},{193,65... | collective-permute-start | bytes 786440 | tf_op jit(solution)/shard_map/ppermute | solution.py:26
  114.3 10.2 %collective-permute-start.33 = (bf16[192,512]{1,0:T(8,128)(2,1)S(1)}, bf16[192,512]{1,0:T(8,128)(2,1)S(1)}, u32[]{:S(2)}, u32[]{:S(2)}) collective-permute-start(bf16[192,512]{1,0:T(8,128)(2,1)S(1)} %shard_map.102.refs_11_.refs_9_), channel_id=1, source_target_pairs={{0,16},{16,0},{32,48},{48,32},{1,17},{17,1},{33,49},{49,33},{2,18}... | collective-permute-start | bytes 589832 | tf_op jit(solution)/shard_map/ppermute | solution.py:22
  114.9 11.2 %collective-permute-start.34 = (bf16[192,512]{1,0:T(8,128)(2,1)S(1)}, bf16[192,512]{1,0:T(8,128)(2,1)S(1)}, u32[]{:S(2)}, u32[]{:S(2)}) collective-permute-start(bf16[192,512]{1,0:T(8,128)(2,1)S(1)} %shard_map.102.refs_11_.refs_9_), channel_id=1, source_target_pairs={{16,32},{32,16},{48,0},{0,48},{17,33},{33,17},{49,1},{1,49},{18,34... | collective-permute-start | bytes 589832 | tf_op jit(solution)/shard_map/ppermute | solution.py:22
  116.2 9.8 %collective-permute-start.35 = (bf16[192,512]{1,0:T(8,128)(2,1)S(1)}, bf16[192,512]{1,0:T(8,128)(2,1)S(1)}, u32[]{:S(2)}, u32[]{:S(2)}) collective-permute-start(bf16[192,512]{1,0:T(8,128)(2,1)S(1)} %shard_map.102.refs_11_.refs_9_), channel_id=1, source_target_pairs={{0,32},{32,0},{16,48},{48,16},{1,33},{33,1},{17,49},{49,17},{2,34}... | collective-permute-start | bytes 589832 | tf_op jit(solution)/shard_map/ppermute | solution.py:22
  124.0 8.1 %collective-permute-start.32 = (bf16[256,256]{1,0:T(8,128)(2,1)S(1)}, bf16[256,256]{1,0:T(8,128)(2,1)S(1)}, u32[]{:S(2)}, u32[]{:S(2)}) collective-permute-start(bf16[256,256]{1,0:T(8,128)(2,1)S(1)} %get-tuple-element.97.refs_13_), channel_id=1, source_target_pairs={{0,4},{2,6},{4,0},{6,2},{1,5},{3,7},{5,1},{7,3},{8,12},{10,14},{12... | collective-permute-start | bytes 393224 | tf_op jit(solution)/shard_map/ppermute | solution.py:349
  132.2 4.4 %collective-permute-start.36 = (bf16[256,128]{1,0:T(8,128)(2,1)S(1)}, bf16[256,128]{1,0:T(8,128)(2,1)S(1)}, u32[]{:S(2)}, u32[]{:S(2)}) collective-permute-start(bf16[256,128]{1,0:T(8,128)(2,1)S(1)} %get-tuple-element.100.refs_2_), channel_id=1, source_target_pairs={{0,2},{2,0},{4,6},{6,4},{1,3},{3,1},{5,7},{7,5},{8,10},{10,8},{12,... | collective-permute-start | bytes 196616 | tf_op jit(solution)/shard_map/ppermute | solution.py:352

commit v4 on v3

--- a/solution.py
+++ b/solution.py
@@ -197,8 +197,8 @@
     held[...] = mine[...] + r3[...].astype(F32)
     for k in range(2):
         cols = slice(k * 128, (k + 1) * 128)
-        keep[:, cols] = held[:, pl.ds(pl.multiple_of(place[5 + k] * 128, 128), 128)]
-        send[:, cols] = held[:, pl.ds(pl.multiple_of(place[7 + k] * 128, 128), 128)].astype(BF)
+        keep[:, cols] = held[:, pl.ds(pl.multiple_of(place[5 + 2 * k] * 128, 128), 128)]
+        send[:, cols] = held[:, pl.ds(pl.multiple_of(place[6 + 2 * k] * 128, 128), 128)].astype(BF)
 
 
 def sum_half(kept, got, send, keep):
@@ -346,10 +346,10 @@
         scratch=[pltpu.VMEM((rows, width // 2), F32)],
         scalars=1,
     )
-    got = lax.ppermute(send, "zl", [(i, i ^ 2) for i in range(4)])
+    got = lax.ppermute(send, "zl", [(i, i ^ 1) for i in range(4)])
     _, down_grad = line(down_grads, [mark, ((n, width), BF)], (*tokens, low, full0, hidden, *hiddens))
     send, keep = line(sum_half, [((rows, 128), BF), ((rows, 128), F32)], (keep, got))
-    got = lax.ppermute(send, "zl", [(i, i ^ 1) for i in range(4)])
+    got = lax.ppermute(send, "zl", [(i, i ^ 2) for i in range(4)])
     (input_grad,) = line(sum_last, [((rows, 128), BF)], (keep, got))
     return input_grad, gate_grad, up_grad, down_grad
 

time: 137 us -> 136 us (level)
  waiting for transfers between devices: 70.8 us -> 68.7 us
    ppermute x1, waiting for transfers between devices: 4.25 us -> 0.71 us  [local(): got = lax.ppermute(send, 'zl', [(i, i ^ 1) for i in range(4)])]
    ppermute x1, waiting for transfers between devices: 3.79 us -> 5.38 us  [local(): got = lax.ppermute(send, 'zl', [(i, i ^ 2) for i in range(4)])]
where the time goes in v4:
time: 136 us
  waiting for transfers between devices  68.7 us (51%)
  starting transfers between devices  43.6 us (32%)
  Pallas kernels  17.6 us (13%)
  local copies, waits for them, and re-layouts  4.7 us (3%)
    ppermute x29, waiting for transfers between devices, swap(): return lax.ppermute(a, axis, both(pairs))  61.2 us
    ppermute x29, starting transfers between devices, swap(): return lax.ppermute(a, axis, both(pairs))  35.5 us
    pallas_call x24, Pallas kernels, call(): pl.pallas_call(run, out_shape=[jax.ShapeDtypeStruct(s, d) for s, d in out...  17.6 us
    ppermute x6, starting transfers between devices, turn(): return lax.ppermute(a, 'y', [(i, (i + shift) % 4) for i in range(4)])  7.08 us
    ppermute x1, waiting for transfers between devices, local(): got = lax.ppermute(send, 'zl', [(i, i ^ 2) for i in range(4)])  5.38 us
    unnamed x12, local copies, waits for them, and re-layouts  4.61 us
  transfers between devices with their start and end apart: 37, of which 17 were waited for; matrix products, arithmetic and copies ran while one was open for 0% of the time, Pallas kernels for 9%

profile of v4, /device:TPU:8, one launch (start us, length us, event | category | flops | bytes accessed | tf_op | source)
XLA Modules:
  0.0 135.6 jit_solution(3943473631919811823)
XLA Ops:
  0.8 1.1 copy-done.4
  1.9 1.0 copy-done.5
  3.5 2.3 %collective-permute-start.4 = (bf16[256,1024]{1,0:T(8,128)(2,1)S(1)}, bf16[256,1024]{1,0:T(8,128)(2,1)S(1)}, u32[]{:S(2)}, u32[]{:S(2)}) collective-permute-start(bf16[256,1024]{1,0:T(8,128)(2,1)S(1)} %get-tuple-element.54.refs_0_.refs_5_), channel_id=1, source_target_pairs={{0,192},{64,0},{128,64},{192,128},{1,193},{65,1},{129,65},{193,129... | collective-permute-start | bytes 1572872 | tf_op jit(solution)/shard_map/ppermute | solution.py:26
  5.8 1.2 copy-done.1
  7.0 1.2 copy-done.3
  8.2 1.0 shard_map.85
  9.2 1.4 %collective-permute-start = (bf16[64,1536]{1,0:T(8,128)(2,1)S(1)}, bf16[64,1536]{1,0:T(8,128)(2,1)S(1)}, u32[]{:S(2)}, u32[]{:S(2)}) collective-permute-start(bf16[64,1536]{1,0:T(8,128)(2,1)S(1)} %get-tuple-element.56.refs_4_), channel_id=1, source_target_pairs={{0,16},{16,0},{32,48},{48,32},{1,17},{17,1},{33,49},{49,33},{2,18}... | collective-permute-start | bytes 589832 | tf_op jit(solution)/shard_map/ppermute | solution.py:22
  10.6 2.1 %collective-permute-start.1 = (bf16[64,1536]{1,0:T(8,128)(2,1)S(1)}, bf16[64,1536]{1,0:T(8,128)(2,1)S(1)}, u32[]{:S(2)}, u32[]{:S(2)}) collective-permute-start(bf16[64,1536]{1,0:T(8,128)(2,1)S(1)} %get-tuple-element.57), channel_id=1, source_target_pairs={{16,32},{32,16},{48,0},{0,48},{17,33},{33,17},{49,1},{1,49},{18,34... | collective-permute-start | bytes 589832 | tf_op jit(solution)/shard_map/ppermute | solution.py:22
  12.7 0.7 collective-permute-start.2
  13.4 3.0 %collective-permute-done.refs_0_ = bf16[64,1536]{1,0:T(8,128)(2,1)S(1)} collective-permute-done((bf16[64,1536]{1,0:T(8,128)(2,1)S(1)}, bf16[64,1536]{1,0:T(8,128)(2,1)S(1)}, u32[]{:S(2)}, u32[]{:S(2)}) %collective-permute-start) | collective-permute-done | bytes 196640 | tf_op jit(solution)/shard_map/ppermute | solution.py:22
  16.4 5.4 %collective-permute-done.1.refs_1_ = bf16[64,1536]{1,0:T(8,128)(2,1)S(1)} collective-permute-done((bf16[64,1536]{1,0:T(8,128)(2,1)S(1)}, bf16[64,1536]{1,0:T(8,128)(2,1)S(1)}, u32[]{:S(2)}, u32[]{:S(2)}) %collective-permute-start.1) | collective-permute-done | bytes 196640 | tf_op jit(solution)/shard_map/ppermute | solution.py:22
  22.6 3.5 %collective-permute-start.11 = (bf16[256,1024]{1,0:T(8,128)(2,1)S(1)}, bf16[256,1024]{1,0:T(8,128)(2,1)S(1)}, u32[]{:S(2)}, u32[]{:S(2)}) collective-permute-start(bf16[256,1024]{1,0:T(8,128)(2,1)S(1)} %shard_map.89.refs_7_.refs_0_), channel_id=1, source_target_pairs={{0,128},{64,192},{128,0},{192,64},{1,129},{65,193},{129,1},{193,65... | collective-permute-start | bytes 1572872 | tf_op jit(solution)/shard_map/ppermute | solution.py:26
  26.1 7.2 %collective-permute-start.3 = (bf16[64,1536]{1,0:T(8,128)(2,1)S(1)}, bf16[64,1536]{1,0:T(8,128)(2,1)S(1)}, u32[]{:S(2)}, u32[]{:S(2)}) collective-permute-start(bf16[64,1536]{1,0:T(8,128)(2,1)S(1)} %get-tuple-element.60.refs_1_), channel_id=1, source_target_pairs={{0,8},{8,0},{1,9},{9,1},{2,10},{10,2},{3,11},{11,3},{4,12},{12,4},... | collective-permute-start | bytes 589832 | tf_op jit(solution)/shard_map/ppermute | solution.py:22
  33.3 1.8 %shard_map.90 = (bf16[128,1536]{1,0:T(8,128)(2,1)S(1)}, bf16[128,1536]{1,0:T(8,128)(2,1)S(1)}, bf16[128,1536]{1,0:T(8,128)(2,1)S(1)}, f32[128,1536]{1,0:T(8,128)S(1)}) custom-call(bf16[256,1024]{1,0:T(8,128)(2,1)S(1)} %shard_map.87.refs_1_.refs_0_.refs_2_, bf16[256,1024]{1,0:T(8,128)(2,1)S(1)} %collective-permute-done.5.refs_1_.refs_3_, ...), custom_call_target="tpu_custom_call" | custom-call | tf_op jit(solution)/shard_map/pallas_call | solution.py:42
  35.1 1.6 %collective-permute-start.10 = (bf16[128,1536]{1,0:T(8,128)(2,1)S(1)}, bf16[128,1536]{1,0:T(8,128)(2,1)S(1)}, u32[]{:S(2)}, u32[]{:S(2)}) collective-permute-start(bf16[128,1536]{1,0:T(8,128)(2,1)S(1)} %get-tuple-element.64), channel_id=1, source_target_pairs={{0,32},{32,0},{16,48},{48,16},{1,33},{33,1},{17,49},{49,17},{2,34}... | collective-permute-start | bytes 1179656 | tf_op jit(solution)/shard_map/ppermute | solution.py:22
  36.7 1.4 %collective-permute-start.8 = (bf16[128,1536]{1,0:T(8,128)(2,1)S(1)}, bf16[128,1536]{1,0:T(8,128)(2,1)S(1)}, u32[]{:S(2)}, u32[]{:S(2)}) collective-permute-start(bf16[128,1536]{1,0:T(8,128)(2,1)S(1)} %get-tuple-element.62.refs_2_), channel_id=1, source_target_pairs={{0,16},{16,0},{32,48},{48,32},{1,17},{17,1},{33,49},{49,33},{2,18}... | collective-permute-start | bytes 1179656 | tf_op jit(solution)/shard_map/ppermute | solution.py:22
  38.2 1.1 collective-permute-start.9
  40.1 1.0 collective-permute-done.12.refs_5_.refs_7_
  41.5 7.3 %collective-permute-done.10.refs_2_ = bf16[128,1536]{1,0:T(8,128)(2,1)S(1)} collective-permute-done((bf16[128,1536]{1,0:T(8,128)(2,1)S(1)}, bf16[128,1536]{1,0:T(8,128)(2,1)S(1)}, u32[]{:S(2)}, u32[]{:S(2)}) %collective-permute-start.10) | collective-permute-done | bytes 393248 | tf_op jit(solution)/shard_map/ppermute | solution.py:22
  48.8 6.4 %collective-permute-done.8.refs_0_ = bf16[128,1536]{1,0:T(8,128)(2,1)S(1)} collective-permute-done((bf16[128,1536]{1,0:T(8,128)(2,1)S(1)}, bf16[128,1536]{1,0:T(8,128)(2,1)S(1)}, u32[]{:S(2)}, u32[]{:S(2)}) %collective-permute-start.8) | collective-permute-done | bytes 393248 | tf_op jit(solution)/shard_map/ppermute | solution.py:22
  55.7 1.3 shard_map.93
  57.4 2.1 %collective-permute-start.15 = (bf16[128,1536]{1,0:T(8,128)(2,1)S(1)}, bf16[128,1536]{1,0:T(8,128)(2,1)S(1)}, u32[]{:S(2)}, u32[]{:S(2)}) collective-permute-start(bf16[128,1536]{1,0:T(8,128)(2,1)S(1)} %get-tuple-element.70), channel_id=1, source_target_pairs={{16,32},{32,16},{48,0},{0,48},{17,33},{33,17},{49,1},{1,49},{18,34... | collective-permute-start | bytes 1179656 | tf_op jit(solution)/shard_map/ppermute | solution.py:22
  59.5 1.9 %collective-permute-start.16 = (bf16[128,1536]{1,0:T(8,128)(2,1)S(1)}, bf16[128,1536]{1,0:T(8,128)(2,1)S(1)}, u32[]{:S(2)}, u32[]{:S(2)}) collective-permute-start(bf16[128,1536]{1,0:T(8,128)(2,1)S(1)} %get-tuple-element.71), channel_id=1, source_target_pairs={{0,32},{32,0},{16,48},{48,16},{1,33},{33,1},{17,49},{49,17},{2,34}... | collective-permute-start | bytes 1179656 | tf_op jit(solution)/shard_map/ppermute | solution.py:22
  61.5 18.3 %collective-permute-done.17.refs_0_ = bf16[128,1536]{1,0:T(8,128)(2,1)S(1)} collective-permute-done((bf16[128,1536]{1,0:T(8,128)(2,1)S(1)}, bf16[128,1536]{1,0:T(8,128)(2,1)S(1)}, u32[]{:S(2)}, u32[]{:S(2)}) %collective-permute-start.17) | collective-permute-done | bytes 393248 | tf_op jit(solution)/shard_map/ppermute | solution.py:22
  80.1 2.2 %collective-permute-start.20 = (bf16[128,1024]{1,0:T(8,128)(2,1)S(1)}, bf16[128,1024]{1,0:T(8,128)(2,1)S(1)}, u32[]{:S(2)}, u32[]{:S(2)}) collective-permute-start(bf16[128,1024]{1,0:T(8,128)(2,1)S(1)} %get-tuple-element.75.refs_4_.refs_1_), channel_id=1, source_target_pairs={{16,32},{32,16},{48,0},{0,48},{17,33},{33,17},{49,1},{1,49},{18,34... | collective-permute-start | bytes 786440 | tf_op jit(solution)/shard_map/ppermute | solution.py:22
  82.3 1.9 %collective-permute-start.21 = (bf16[128,1024]{1,0:T(8,128)(2,1)S(1)}, bf16[128,1024]{1,0:T(8,128)(2,1)S(1)}, u32[]{:S(2)}, u32[]{:S(2)}) collective-permute-start(bf16[128,1024]{1,0:T(8,128)(2,1)S(1)} %get-tuple-element.75.refs_4_.refs_1_), channel_id=1, source_target_pairs={{0,32},{32,0},{16,48},{48,16},{1,33},{33,1},{17,49},{49,17},{2,34}... | collective-permute-start | bytes 786440 | tf_op jit(solution)/shard_map/ppermute | solution.py:22
  84.3 0.9 collective-permute-start.22
  85.2 1.4 %shard_map.96 = (bf16[256,512]{1,0:T(8,128)(2,1)S(1)}, f32[256,512]{1,0:T(8,128)S(1)}, bf16[256,1536]{1,0:T(8,128)(2,1)S(1)}) custom-call(s32[9]{0:T(128)S(1)} %stack.39.refs_0_, bf16[64,1536]{1,0:T(8,128)(2,1)S(1)} %shard_map.91.refs_1_.refs_7_, bf16[128,1536]{1,0:T(8,128)(2,1)S(1)} %collective-permute-done.14.refs_0_.refs_2_, ...), custom_call_target="tpu_custom_call" | custom-call | tf_op jit(solution)/shard_map/pallas_call | solution.py:42
  86.7 10.4 %collective-permute-done.22.refs_0_ = bf16[64,1536]{1,0:T(8,128)(2,1)S(1)} collective-permute-done((bf16[64,1536]{1,0:T(8,128)(2,1)S(1)}, bf16[64,1536]{1,0:T(8,128)(2,1)S(1)}, u32[]{:S(2)}, u32[]{:S(2)}) %collective-permute-start.22) | collective-permute-done | bytes 196640 | tf_op jit(solution)/shard_map/ppermute | solution.py:22
  97.2 2.1 %shard_map.98 = (bf16[512,512]{1,0:T(8,128)(2,1)S(1)}, f32[512,512]{1,0:T(8,128)S(1)}, bf16[512,1024]{1,0:T(8,128)(2,1)S(1)}) custom-call(s32[9]{0:T(128)S(1)} %stack.39.refs_0_, bf16[128,1024]{1,0:T(8,128)(2,1)S(1)} %get-tuple-element.75.refs_4_.refs_1_, bf16[128,1024]{1,0:T(8,128)(2,1)S(1)} %collective-permute-done.19.refs_2_, ...), custom_call_target="tpu_custom_call" | custom-call | tf_op jit(solution)/shard_map/pallas_call | solution.py:42
  99.4 0.6 collective-permute-start.26
  100.2 1.5 %collective-permute-start.27 = (bf16[64,1024]{1,0:T(8,128)(2,1)S(1)}, bf16[64,1024]{1,0:T(8,128)(2,1)S(1)}, u32[]{:S(2)}, u32[]{:S(2)}) collective-permute-start(bf16[64,1024]{1,0:T(8,128)(2,1)S(1)} %get-tuple-element.80.refs_7_.refs_1_), channel_id=1, source_target_pairs={{16,32},{32,16},{48,0},{0,48},{17,33},{33,17},{49,1},{1,49},{18,34... | collective-permute-start | bytes 393224 | tf_op jit(solution)/shard_map/ppermute | solution.py:22
  101.7 2.1 %collective-permute-start.28 = (bf16[64,1024]{1,0:T(8,128)(2,1)S(1)}, bf16[64,1024]{1,0:T(8,128)(2,1)S(1)}, u32[]{:S(2)}, u32[]{:S(2)}) collective-permute-start(bf16[64,1024]{1,0:T(8,128)(2,1)S(1)} %get-tuple-element.80.refs_7_.refs_1_), channel_id=1, source_target_pairs={{0,32},{32,0},{16,48},{48,16},{1,33},{33,1},{17,49},{49,17},{2,34}... | collective-permute-start | bytes 393224 | tf_op jit(solution)/shard_map/ppermute | solution.py:22
  103.9 1.7 %collective-permute-done.26.refs_2_ = bf16[64,1024]{1,0:T(8,128)(2,1)S(1)} collective-permute-done((bf16[64,1024]{1,0:T(8,128)(2,1)S(1)}, bf16[64,1024]{1,0:T(8,128)(2,1)S(1)}, u32[]{:S(2)}, u32[]{:S(2)}) %collective-permute-start.26) | collective-permute-done | bytes 131104 | tf_op jit(solution)/shard_map/ppermute | solution.py:22
  105.9 4.0 %collective-permute-done.27.refs_3_ = bf16[64,1024]{1,0:T(8,128)(2,1)S(1)} collective-permute-done((bf16[64,1024]{1,0:T(8,128)(2,1)S(1)}, bf16[64,1024]{1,0:T(8,128)(2,1)S(1)}, u32[]{:S(2)}, u32[]{:S(2)}) %collective-permute-start.27) | collective-permute-done | bytes 131104 | tf_op jit(solution)/shard_map/ppermute | solution.py:22
  110.0 1.4 %shard_map.100 = (bf16[128,512]{1,0:T(8,128)(2,1)S(1)}, bf16[128,512]{1,0:T(8,128)(2,1)S(1)}, f32[256,512]{1,0:T(8,128)S(1)}, bf16[256,1024]{1,0:T(8,128)(2,1)S(1)}) custom-call(s32[9]{0:T(128)S(1)} %stack.39.refs_0_, bf16[64,1024]{1,0:T(8,128)(2,1)S(1)} %get-tuple-element.80.refs_7_.refs_1_, bf16[64,1024]{1,0:T(8,128)(2,1)S(1)} %collective-permute-done.26.refs_2_, ...), custom_call_target="tpu_custom_call" | custom-call | tf_op jit(solution)/shard_map/pallas_call | solution.py:42
  112.0 0.8 collective-permute-done.29.refs_5_
  113.3 0.9 collective-permute-start.31
  114.3 0.6 collective-permute-start.33
  114.9 1.3 collective-permute-start.34
  116.2 2.2 %collective-permute-start.35 = (bf16[192,512]{1,0:T(8,128)(2,1)S(1)}, bf16[192,512]{1,0:T(8,128)(2,1)S(1)}, u32[]{:S(2)}, u32[]{:S(2)}) collective-permute-start(bf16[192,512]{1,0:T(8,128)(2,1)S(1)} %shard_map.102.refs_11_.refs_9_), channel_id=1, source_target_pairs={{0,32},{32,0},{16,48},{48,16},{1,33},{33,1},{17,49},{49,17},{2,34}... | collective-permute-start | bytes 589832 | tf_op jit(solution)/shard_map/ppermute | solution.py:22
  118.4 3.4 %shard_map.103 = (f32[8,128]{1,0:T(8,128)S(1)}, bf16[1024,512]{1,0:T(8,128)(2,1)}, bf16[1024,512]{1,0:T(8,128)(2,1)}) custom-call(bf16[256,1024]{1,0:T(8,128)(2,1)S(1)} %shard_map.89.refs_7_.refs_0_, bf16[256,1024]{1,0:T(8,128)(2,1)S(1)} %get-tuple-element.55.refs_1_, bf16[256,1024]{1,0:T(8,128)(2,1)S(1)} %shard_map.87.refs_1_.refs_0_.refs_2_, ...), custom_call_target="tpu_custom_call" | custom-call | tf_op jit(solution)/shard_map/pallas_call | solution.py:42
  121.9 1.4 %collective-permute-done.31.refs_2_ = bf16[256,512]{1,0:T(8,128)(2,1)S(1)} collective-permute-done((bf16[256,512]{1,0:T(8,128)(2,1)S(1)}, bf16[256,512]{1,0:T(8,128)(2,1)S(1)}, u32[]{:S(2)}, u32[]{:S(2)}) %collective-permute-start.31) | collective-permute-done | bytes 262176 | tf_op jit(solution)/shard_map/ppermute | solution.py:26
  123.3 0.7 shard_map.104
  124.6 1.5 %collective-permute-done.34.refs_11_ = bf16[192,512]{1,0:T(8,128)(2,1)S(1)} collective-permute-done((bf16[192,512]{1,0:T(8,128)(2,1)S(1)}, bf16[192,512]{1,0:T(8,128)(2,1)S(1)}, u32[]{:S(2)}, u32[]{:S(2)}) %collective-permute-start.34) | collective-permute-done | bytes 196640 | tf_op jit(solution)/shard_map/ppermute | solution.py:22
  126.1 2.3 %shard_map.105 = (f32[8,128]{1,0:T(8,128)S(1)}, bf16[512,1024]{1,0:T(8,128)(2,1)}) custom-call(bf16[256,1024]{1,0:T(8,128)(2,1)S(1)} %shard_map.89.refs_7_.refs_0_, bf16[256,1024]{1,0:T(8,128)(2,1)S(1)} %get-tuple-element.55.refs_1_, bf16[256,1024]{1,0:T(8,128)(2,1)S(1)} %shard_map.87.refs_1_.refs_0_.refs_2_, ...), custom_call_target="tpu_custom_call" | custom-call | tf_op jit(solution)/shard_map/pallas_call | solution.py:42
  128.4 0.7 collective-permute-done.32.refs_1_
  129.6 5.4 %collective-permute-done.36.refs_1_ = bf16[256,128]{1,0:T(8,128)(2,1)S(1)} collective-permute-done((bf16[256,128]{1,0:T(8,128)(2,1)S(1)}, bf16[256,128]{1,0:T(8,128)(2,1)S(1)}, u32[]{:S(2)}, u32[]{:S(2)}) %collective-permute-start.36) | collective-permute-done | bytes 65568 | tf_op jit(solution)/shard_map/ppermute | solution.py:352
  (63 shorter events, 7.6 us)
Async XLA Ops:
  0.6 5.2 %copy-start = (bf16[1024,512]{1,0:T(8,128)(2,1)S(1)}, bf16[1024,512]{1,0:T(8,128)(2,1)}, u32[]{:S(2)}) copy-start(bf16[1024,512]{1,0:T(8,128)(2,1)} %refs_5_.7) | copy-start | bytes 3145732
  0.7 1.1 copy-start.4
  1.9 1.0 copy-start.5
  3.5 18.4 %collective-permute-start.4 = (bf16[256,1024]{1,0:T(8,128)(2,1)S(1)}, bf16[256,1024]{1,0:T(8,128)(2,1)S(1)}, u32[]{:S(2)}, u32[]{:S(2)}) collective-permute-start(bf16[256,1024]{1,0:T(8,128)(2,1)S(1)} %get-tuple-element.54.refs_0_.refs_5_), channel_id=1, source_target_pairs={{0,192},{64,0},{128,64},{192,128},{1,193},{65,1},{129,65},{193,129... | collective-permute-start | bytes 1572872 | tf_op jit(solution)/shard_map/ppermute | solution.py:26
  5.8 16.2 %collective-permute-start.6 = (bf16[256,1024]{1,0:T(8,128)(2,1)S(1)}, bf16[256,1024]{1,0:T(8,128)(2,1)S(1)}, u32[]{:S(2)}, u32[]{:S(2)}) collective-permute-start(bf16[256,1024]{1,0:T(8,128)(2,1)S(1)} %get-tuple-element.54.refs_0_.refs_5_), channel_id=1, source_target_pairs={{0,64},{64,128},{128,192},{192,0},{1,65},{65,129},{129,193},{193,1... | collective-permute-start | bytes 1572872 | tf_op jit(solution)/shard_map/ppermute | solution.py:26
  5.8 1.2 copy-start.1
  7.0 1.2 copy-start.3
  9.2 7.2 %collective-permute-start = (bf16[64,1536]{1,0:T(8,128)(2,1)S(1)}, bf16[64,1536]{1,0:T(8,128)(2,1)S(1)}, u32[]{:S(2)}, u32[]{:S(2)}) collective-permute-start(bf16[64,1536]{1,0:T(8,128)(2,1)S(1)} %get-tuple-element.56.refs_4_), channel_id=1, source_target_pairs={{0,16},{16,0},{32,48},{48,32},{1,17},{17,1},{33,49},{49,33},{2,18}... | collective-permute-start | bytes 589832 | tf_op jit(solution)/shard_map/ppermute | solution.py:22
  10.6 11.2 %collective-permute-start.1 = (bf16[64,1536]{1,0:T(8,128)(2,1)S(1)}, bf16[64,1536]{1,0:T(8,128)(2,1)S(1)}, u32[]{:S(2)}, u32[]{:S(2)}) collective-permute-start(bf16[64,1536]{1,0:T(8,128)(2,1)S(1)} %get-tuple-element.57), channel_id=1, source_target_pairs={{16,32},{32,16},{48,0},{0,48},{17,33},{33,17},{49,1},{1,49},{18,34... | collective-permute-start | bytes 589832 | tf_op jit(solution)/shard_map/ppermute | solution.py:22
  12.7 9.1 %collective-permute-start.2 = (bf16[64,1536]{1,0:T(8,128)(2,1)S(1)}, bf16[64,1536]{1,0:T(8,128)(2,1)S(1)}, u32[]{:S(2)}, u32[]{:S(2)}) collective-permute-start(bf16[64,1536]{1,0:T(8,128)(2,1)S(1)} %get-tuple-element.58), channel_id=1, source_target_pairs={{0,32},{32,0},{16,48},{48,16},{1,33},{33,1},{17,49},{49,17},{2,34}... | collective-permute-start | bytes 589832 | tf_op jit(solution)/shard_map/ppermute | solution.py:22
  22.0 11.3 %copy-start.2 = (bf16[1024,512]{1,0:T(8,128)(2,1)S(1)}, bf16[1024,512]{1,0:T(8,128)(2,1)}, u32[]{:S(2)}) copy-start(bf16[1024,512]{1,0:T(8,128)(2,1)} %refs_6_.7) | copy-start | bytes 3145732
  22.0 11.3 %collective-permute-start.7 = (bf16[256,1024]{1,0:T(8,128)(2,1)S(1)}, bf16[256,1024]{1,0:T(8,128)(2,1)S(1)}, u32[]{:S(2)}, u32[]{:S(2)}) collective-permute-start(bf16[256,1024]{1,0:T(8,128)(2,1)S(1)} %shard_map.88.refs_1_.refs_2_.refs_4_), channel_id=1, source_target_pairs={{0,1},{1,0},{2,3},{3,2},{4,5},{5,4},{6,7},{7,6},{8,9},{9,8},{10,11... | collective-permute-start | bytes 1572872 | tf_op jit(solution)/shard_map/ppermute | solution.py:22
  22.1 11.2 %collective-permute-start.5 = (bf16[256,1024]{1,0:T(8,128)(2,1)S(1)}, bf16[256,1024]{1,0:T(8,128)(2,1)S(1)}, u32[]{:S(2)}, u32[]{:S(2)}) collective-permute-start(bf16[256,1024]{1,0:T(8,128)(2,1)S(1)} %shard_map.87.refs_1_.refs_0_.refs_2_), channel_id=1, source_target_pairs={{0,1},{1,0},{2,3},{3,2},{4,5},{5,4},{6,7},{7,6},{8,9},{9,8},{10,11... | collective-permute-start | bytes 1572872 | tf_op jit(solution)/shard_map/ppermute | solution.py:22
  22.6 16.8 %collective-permute-start.11 = (bf16[256,1024]{1,0:T(8,128)(2,1)S(1)}, bf16[256,1024]{1,0:T(8,128)(2,1)S(1)}, u32[]{:S(2)}, u32[]{:S(2)}) collective-permute-start(bf16[256,1024]{1,0:T(8,128)(2,1)S(1)} %shard_map.89.refs_7_.refs_0_), channel_id=1, source_target_pairs={{0,128},{64,192},{128,0},{192,64},{1,129},{65,193},{129,1},{193,65... | collective-permute-start | bytes 1572872 | tf_op jit(solution)/shard_map/ppermute | solution.py:26
  26.1 13.2 %collective-permute-start.3 = (bf16[64,1536]{1,0:T(8,128)(2,1)S(1)}, bf16[64,1536]{1,0:T(8,128)(2,1)S(1)}, u32[]{:S(2)}, u32[]{:S(2)}) collective-permute-start(bf16[64,1536]{1,0:T(8,128)(2,1)S(1)} %get-tuple-element.60.refs_1_), channel_id=1, source_target_pairs={{0,8},{8,0},{1,9},{9,1},{2,10},{10,2},{3,11},{11,3},{4,12},{12,4},... | collective-permute-start | bytes 589832 | tf_op jit(solution)/shard_map/ppermute | solution.py:22
  35.1 13.7 %collective-permute-start.10 = (bf16[128,1536]{1,0:T(8,128)(2,1)S(1)}, bf16[128,1536]{1,0:T(8,128)(2,1)S(1)}, u32[]{:S(2)}, u32[]{:S(2)}) collective-permute-start(bf16[128,1536]{1,0:T(8,128)(2,1)S(1)} %get-tuple-element.64), channel_id=1, source_target_pairs={{0,32},{32,0},{16,48},{48,16},{1,33},{33,1},{17,49},{49,17},{2,34}... | collective-permute-start | bytes 1179656 | tf_op jit(solution)/shard_map/ppermute | solution.py:22
  36.7 18.4 %collective-permute-start.8 = (bf16[128,1536]{1,0:T(8,128)(2,1)S(1)}, bf16[128,1536]{1,0:T(8,128)(2,1)S(1)}, u32[]{:S(2)}, u32[]{:S(2)}) collective-permute-start(bf16[128,1536]{1,0:T(8,128)(2,1)S(1)} %get-tuple-element.62.refs_2_), channel_id=1, source_target_pairs={{0,16},{16,0},{32,48},{48,32},{1,17},{17,1},{33,49},{49,33},{2,18}... | collective-permute-start | bytes 1179656 | tf_op jit(solution)/shard_map/ppermute | solution.py:22
  38.2 17.5 %collective-permute-start.9 = (bf16[128,1536]{1,0:T(8,128)(2,1)S(1)}, bf16[128,1536]{1,0:T(8,128)(2,1)S(1)}, u32[]{:S(2)}, u32[]{:S(2)}) collective-permute-start(bf16[128,1536]{1,0:T(8,128)(2,1)S(1)} %get-tuple-element.63), channel_id=1, source_target_pairs={{16,32},{32,16},{48,0},{0,48},{17,33},{33,17},{49,1},{1,49},{18,34... | collective-permute-start | bytes 1179656 | tf_op jit(solution)/shard_map/ppermute | solution.py:22
  39.5 1.6 %collective-permute-start.12 = (bf16[128,1024]{1,0:T(8,128)(2,1)S(1)}, bf16[128,1024]{1,0:T(8,128)(2,1)S(1)}, u32[]{:S(2)}, u32[]{:S(2)}) collective-permute-start(bf16[128,1024]{1,0:T(8,128)(2,1)S(1)} %get-tuple-element.67.refs_11_), channel_id=1, source_target_pairs={{0,1},{1,0},{2,3},{3,2},{4,5},{5,4},{6,7},{7,6},{8,9},{9,8},{10,11... | collective-permute-start | bytes 786440 | tf_op jit(solution)/shard_map/ppermute | solution.py:22
  39.6 1.9 %collective-permute-start.13 = (bf16[128,1024]{1,0:T(8,128)(2,1)S(1)}, bf16[128,1024]{1,0:T(8,128)(2,1)S(1)}, u32[]{:S(2)}, u32[]{:S(2)}) collective-permute-start(bf16[128,1024]{1,0:T(8,128)(2,1)S(1)} %get-tuple-element.68), channel_id=1, source_target_pairs={{0,1},{1,0},{2,3},{3,2},{4,5},{5,4},{6,7},{7,6},{8,9},{9,8},{10,11... | collective-permute-start | bytes 786440 | tf_op jit(solution)/shard_map/ppermute | solution.py:22
  57.0 22.8 %collective-permute-start.17 = (bf16[128,1536]{1,0:T(8,128)(2,1)S(1)}, bf16[128,1536]{1,0:T(8,128)(2,1)S(1)}, u32[]{:S(2)}, u32[]{:S(2)}) collective-permute-start(bf16[128,1536]{1,0:T(8,128)(2,1)S(1)} %get-tuple-element.73.refs_2_), channel_id=1, source_target_pairs={{0,8},{8,0},{1,9},{9,1},{2,10},{10,2},{3,11},{11,3},{4,12},{12,4},... | collective-permute-start | bytes 1179656 | tf_op jit(solution)/shard_map/ppermute | solution.py:22
  57.4 24.9 %collective-permute-start.14 = (bf16[128,1536]{1,0:T(8,128)(2,1)S(1)}, bf16[128,1536]{1,0:T(8,128)(2,1)S(1)}, u32[]{:S(2)}, u32[]{:S(2)}) collective-permute-start(bf16[128,1536]{1,0:T(8,128)(2,1)S(1)} %get-tuple-element.69), channel_id=1, source_target_pairs={{0,16},{16,0},{32,48},{48,32},{1,17},{17,1},{33,49},{49,33},{2,18}... | collective-permute-start | bytes 1179656 | tf_op jit(solution)/shard_map/ppermute | solution.py:22
  57.4 26.7 %collective-permute-start.15 = (bf16[128,1536]{1,0:T(8,128)(2,1)S(1)}, bf16[128,1536]{1,0:T(8,128)(2,1)S(1)}, u32[]{:S(2)}, u32[]{:S(2)}) collective-permute-start(bf16[128,1536]{1,0:T(8,128)(2,1)S(1)} %get-tuple-element.70), channel_id=1, source_target_pairs={{16,32},{32,16},{48,0},{0,48},{17,33},{33,17},{49,1},{1,49},{18,34... | collective-permute-start | bytes 1179656 | tf_op jit(solution)/shard_map/ppermute | solution.py:22
  59.5 24.6 %collective-permute-start.16 = (bf16[128,1536]{1,0:T(8,128)(2,1)S(1)}, bf16[128,1536]{1,0:T(8,128)(2,1)S(1)}, u32[]{:S(2)}, u32[]{:S(2)}) collective-permute-start(bf16[128,1536]{1,0:T(8,128)(2,1)S(1)} %get-tuple-element.71), channel_id=1, source_target_pairs={{0,32},{32,0},{16,48},{48,16},{1,33},{33,1},{17,49},{49,17},{2,34}... | collective-permute-start | bytes 1179656 | tf_op jit(solution)/shard_map/ppermute | solution.py:22
  80.0 17.1 %collective-permute-start.19 = (bf16[128,1024]{1,0:T(8,128)(2,1)S(1)}, bf16[128,1024]{1,0:T(8,128)(2,1)S(1)}, u32[]{:S(2)}, u32[]{:S(2)}) collective-permute-start(bf16[128,1024]{1,0:T(8,128)(2,1)S(1)} %get-tuple-element.75.refs_4_.refs_1_), channel_id=1, source_target_pairs={{0,16},{16,0},{32,48},{48,32},{1,17},{17,1},{33,49},{49,33},{2,18}... | collective-permute-start | bytes 786440 | tf_op jit(solution)/shard_map/ppermute | solution.py:22
  80.1 17.1 %collective-permute-start.20 = (bf16[128,1024]{1,0:T(8,128)(2,1)S(1)}, bf16[128,1024]{1,0:T(8,128)(2,1)S(1)}, u32[]{:S(2)}, u32[]{:S(2)}) collective-permute-start(bf16[128,1024]{1,0:T(8,128)(2,1)S(1)} %get-tuple-element.75.refs_4_.refs_1_), channel_id=1, source_target_pairs={{16,32},{32,16},{48,0},{0,48},{17,33},{33,17},{49,1},{1,49},{18,34... | collective-permute-start | bytes 786440 | tf_op jit(solution)/shard_map/ppermute | solution.py:22
  82.3 14.9 %collective-permute-start.21 = (bf16[128,1024]{1,0:T(8,128)(2,1)S(1)}, bf16[128,1024]{1,0:T(8,128)(2,1)S(1)}, u32[]{:S(2)}, u32[]{:S(2)}) collective-permute-start(bf16[128,1024]{1,0:T(8,128)(2,1)S(1)} %get-tuple-element.75.refs_4_.refs_1_), channel_id=1, source_target_pairs={{0,32},{32,0},{16,48},{48,16},{1,33},{33,1},{17,49},{49,17},{2,34}... | collective-permute-start | bytes 786440 | tf_op jit(solution)/shard_map/ppermute | solution.py:22
  84.3 12.7 %collective-permute-start.22 = (bf16[64,1536]{1,0:T(8,128)(2,1)S(1)}, bf16[64,1536]{1,0:T(8,128)(2,1)S(1)}, u32[]{:S(2)}, u32[]{:S(2)}) collective-permute-start(bf16[64,1536]{1,0:T(8,128)(2,1)S(1)} %get-tuple-element.76.refs_7_), channel_id=1, source_target_pairs={{0,8},{8,0},{1,9},{9,1},{2,10},{10,2},{3,11},{11,3},{4,12},{12,4},... | collective-permute-start | bytes 589832 | tf_op jit(solution)/shard_map/ppermute | solution.py:22
  99.3 4.4 %collective-permute-start.23 = (bf16[512,512]{1,0:T(8,128)(2,1)S(1)}, bf16[512,512]{1,0:T(8,128)(2,1)S(1)}, u32[]{:S(2)}, u32[]{:S(2)}) collective-permute-start(bf16[512,512]{1,0:T(8,128)(2,1)S(1)} %get-tuple-element.82.refs_2_), channel_id=1, source_target_pairs={{0,1},{1,0},{2,3},{3,2},{4,5},{5,4},{6,7},{7,6},{8,9},{9,8},{10,11... | collective-permute-start | bytes 1572872 | tf_op jit(solution)/shard_map/ppermute | solution.py:22
  99.4 6.2 %collective-permute-start.26 = (bf16[64,1024]{1,0:T(8,128)(2,1)S(1)}, bf16[64,1024]{1,0:T(8,128)(2,1)S(1)}, u32[]{:S(2)}, u32[]{:S(2)}) collective-permute-start(bf16[64,1024]{1,0:T(8,128)(2,1)S(1)} %get-tuple-element.80.refs_7_.refs_1_), channel_id=1, source_target_pairs={{0,16},{16,0},{32,48},{48,32},{1,17},{17,1},{33,49},{49,33},{2,18}... | collective-permute-start | bytes 393224 | tf_op jit(solution)/shard_map/ppermute | solution.py:22
  100.0 12.0 %collective-permute-start.18 = (bf16[256,512]{1,0:T(8,128)(2,1)S(1)}, bf16[256,512]{1,0:T(8,128)(2,1)S(1)}, u32[]{:S(2)}, u32[]{:S(2)}) collective-permute-start(bf16[256,512]{1,0:T(8,128)(2,1)S(1)} %get-tuple-element.78.refs_2_), channel_id=1, source_target_pairs={{0,1},{1,0},{2,3},{3,2},{4,5},{5,4},{6,7},{7,6},{8,9},{9,8},{10,11... | collective-permute-start | bytes 786440 | tf_op jit(solution)/shard_map/ppermute | solution.py:22
  100.2 9.8 %collective-permute-start.27 = (bf16[64,1024]{1,0:T(8,128)(2,1)S(1)}, bf16[64,1024]{1,0:T(8,128)(2,1)S(1)}, u32[]{:S(2)}, u32[]{:S(2)}) collective-permute-start(bf16[64,1024]{1,0:T(8,128)(2,1)S(1)} %get-tuple-element.80.refs_7_.refs_1_), channel_id=1, source_target_pairs={{16,32},{32,16},{48,0},{0,48},{17,33},{33,17},{49,1},{1,49},{18,34... | collective-permute-start | bytes 393224 | tf_op jit(solution)/shard_map/ppermute | solution.py:22
  101.7 8.3 %collective-permute-start.28 = (bf16[64,1024]{1,0:T(8,128)(2,1)S(1)}, bf16[64,1024]{1,0:T(8,128)(2,1)S(1)}, u32[]{:S(2)}, u32[]{:S(2)}) collective-permute-start(bf16[64,1024]{1,0:T(8,128)(2,1)S(1)} %get-tuple-element.80.refs_7_.refs_1_), channel_id=1, source_target_pairs={{0,32},{32,0},{16,48},{48,16},{1,33},{33,1},{17,49},{49,17},{2,34}... | collective-permute-start | bytes 393224 | tf_op jit(solution)/shard_map/ppermute | solution.py:22
  103.8 9.3 %collective-permute-start.24 = (bf16[256,512]{1,0:T(8,128)(2,1)S(1)}, bf16[256,512]{1,0:T(8,128)(2,1)S(1)}, u32[]{:S(2)}, u32[]{:S(2)}) collective-permute-start(bf16[256,512]{1,0:T(8,128)(2,1)S(1)} %get-tuple-element.83.refs_7_), channel_id=1, source_target_pairs={{0,64},{64,128},{128,192},{192,0},{1,65},{65,129},{129,193},{193,1... | collective-permute-start | bytes 786440 | tf_op jit(solution)/shard_map/ppermute | solution.py:26
  105.6 7.5 %collective-permute-start.25 = (bf16[256,512]{1,0:T(8,128)(2,1)S(1)}, bf16[256,512]{1,0:T(8,128)(2,1)S(1)}, u32[]{:S(2)}, u32[]{:S(2)}) collective-permute-start(bf16[256,512]{1,0:T(8,128)(2,1)S(1)} %get-tuple-element.84), channel_id=1, source_target_pairs={{0,192},{64,0},{128,64},{192,128},{1,193},{65,1},{129,65},{193,129... | collective-permute-start | bytes 786440 | tf_op jit(solution)/shard_map/ppermute | solution.py:26
  111.4 1.4 %collective-permute-start.29 = (bf16[128,512]{1,0:T(8,128)(2,1)S(1)}, bf16[128,512]{1,0:T(8,128)(2,1)S(1)}, u32[]{:S(2)}, u32[]{:S(2)}) collective-permute-start(bf16[128,512]{1,0:T(8,128)(2,1)S(1)} %get-tuple-element.86.refs_7_), channel_id=1, source_target_pairs={{0,1},{1,0},{2,3},{3,2},{4,5},{5,4},{6,7},{7,6},{8,9},{9,8},{10,11... | collective-permute-start | bytes 393224 | tf_op jit(solution)/shard_map/ppermute | solution.py:22
  111.5 1.7 %collective-permute-start.30 = (bf16[128,512]{1,0:T(8,128)(2,1)S(1)}, bf16[128,512]{1,0:T(8,128)(2,1)S(1)}, u32[]{:S(2)}, u32[]{:S(2)}) collective-permute-start(bf16[128,512]{1,0:T(8,128)(2,1)S(1)} %get-tuple-element.87), channel_id=1, source_target_pairs={{0,1},{1,0},{2,3},{3,2},{4,5},{5,4},{6,7},{7,6},{8,9},{9,8},{10,11... | collective-permute-start | bytes 393224 | tf_op jit(solution)/shard_map/ppermute | solution.py:22
  113.3 10.0 %collective-permute-start.31 = (bf16[256,512]{1,0:T(8,128)(2,1)S(1)}, bf16[256,512]{1,0:T(8,128)(2,1)S(1)}, u32[]{:S(2)}, u32[]{:S(2)}) collective-permute-start(bf16[256,512]{1,0:T(8,128)(2,1)S(1)} %get-tuple-element.89.refs_2_), channel_id=1, source_target_pairs={{0,128},{64,192},{128,0},{192,64},{1,129},{65,193},{129,1},{193,65... | collective-permute-start | bytes 786440 | tf_op jit(solution)/shard_map/ppermute | solution.py:26
  114.3 10.3 %collective-permute-start.33 = (bf16[192,512]{1,0:T(8,128)(2,1)S(1)}, bf16[192,512]{1,0:T(8,128)(2,1)S(1)}, u32[]{:S(2)}, u32[]{:S(2)}) collective-permute-start(bf16[192,512]{1,0:T(8,128)(2,1)S(1)} %shard_map.102.refs_11_.refs_9_), channel_id=1, source_target_pairs={{0,16},{16,0},{32,48},{48,32},{1,17},{17,1},{33,49},{49,33},{2,18}... | collective-permute-start | bytes 589832 | tf_op jit(solution)/shard_map/ppermute | solution.py:22
  114.9 11.2 %collective-permute-start.34 = (bf16[192,512]{1,0:T(8,128)(2,1)S(1)}, bf16[192,512]{1,0:T(8,128)(2,1)S(1)}, u32[]{:S(2)}, u32[]{:S(2)}) collective-permute-start(bf16[192,512]{1,0:T(8,128)(2,1)S(1)} %shard_map.102.refs_11_.refs_9_), channel_id=1, source_target_pairs={{16,32},{32,16},{48,0},{0,48},{17,33},{33,17},{49,1},{1,49},{18,34... | collective-permute-start | bytes 589832 | tf_op jit(solution)/shard_map/ppermute | solution.py:22
  116.2 9.8 %collective-permute-start.35 = (bf16[192,512]{1,0:T(8,128)(2,1)S(1)}, bf16[192,512]{1,0:T(8,128)(2,1)S(1)}, u32[]{:S(2)}, u32[]{:S(2)}) collective-permute-start(bf16[192,512]{1,0:T(8,128)(2,1)S(1)} %shard_map.102.refs_11_.refs_9_), channel_id=1, source_target_pairs={{0,32},{32,0},{16,48},{48,16},{1,33},{33,1},{17,49},{49,17},{2,34}... | collective-permute-start | bytes 589832 | tf_op jit(solution)/shard_map/ppermute | solution.py:22
  124.0 5.1 %collective-permute-start.32 = (bf16[256,256]{1,0:T(8,128)(2,1)S(1)}, bf16[256,256]{1,0:T(8,128)(2,1)S(1)}, u32[]{:S(2)}, u32[]{:S(2)}) collective-permute-start(bf16[256,256]{1,0:T(8,128)(2,1)S(1)} %get-tuple-element.97.refs_13_), channel_id=1, source_target_pairs={{0,2},{2,0},{4,6},{6,4},{1,3},{3,1},{5,7},{7,5},{8,10},{10,8},{12,... | collective-permute-start | bytes 393224 | tf_op jit(solution)/shard_map/ppermute | solution.py:349
  129.1 5.8 %collective-permute-start.36 = (bf16[256,128]{1,0:T(8,128)(2,1)S(1)}, bf16[256,128]{1,0:T(8,128)(2,1)S(1)}, u32[]{:S(2)}, u32[]{:S(2)}) collective-permute-start(bf16[256,128]{1,0:T(8,128)(2,1)S(1)} %get-tuple-element.100.refs_2_), channel_id=1, source_target_pairs={{0,4},{2,6},{4,0},{6,2},{1,5},{3,7},{5,1},{7,3},{8,12},{10,14},{12... | collective-permute-start | bytes 196616 | tf_op jit(solution)/shard_map/ppermute | solution.py:352
